TPU v7x, 512 devices: a whole 4x8x8 slice. The times are simulated.
512 devices in a mesh: grp: 16 (over z, core), dom: 32 (over y, x).
Axes of the slice: x: 4, y: 8, z: 8, core: 2. Of those that a mesh axis runs over, the one named last changes fastest.
Arguments:
- feats_t: bfloat16 [512, 131072], P('dom', 'grp'), may hold values from -6 to 6
- w_first: bfloat16 [512, 1024], replicated, may hold values from -0.25 to 0.25
- w_second: bfloat16 [1024, 128], replicated, may hold values from -2.5 to 2.5
- stale_rows: bfloat16 [65536, 1152], P(('grp', 'dom')), may hold values from -6 to 6
- tile_vals: bfloat16 [1024, 4, 128, 128], P(('grp', 'dom')), may hold values from 0 to 0.076171875
- tile_src: int32 [1024, 4], P(('grp', 'dom')), may hold values from 0 to 5, as said below
- tile_count: int32 [1024], P(('grp', 'dom')), may hold values from 1 to 4, as said below
- labels: int32 [131072], P(('grp', 'dom')), may hold values from 0 to 127
Outputs:
- logits: bfloat16 [131072, 128], P(('grp', 'dom'))
- grad_feats: bfloat16 [512, 131072], P('dom', 'grp')
- grad_first: float32 [512, 1024], P('dom')
- grad_second: float32 [1024, 128], P('dom')
Inputs may be any that keep to these rules, and one draw needn't show every extreme that they name: `tile_src`: the 4 entries of one block row are distinct. Slots from tile_count on are not used; in every partition some block row holds that partition's largest count, and some partition reaches 4.
All inputs are finite; a program needn't handle non-finite values.
Results may differ from a plain program's by a relative error of at most 0.025.
Values may be sent and summed in bfloat16 or wider, within the bound.
No kernel may reach another device: no remote copies, remote signals or barrier semaphores. Data moves between devices by JAX's collectives and lax.ppermute only.
A program may use at most 64 MiB of HBM per device.

v0:
```python
import math

import jax
import jax.numpy as jnp
from jax import lax
from jax.sharding import PartitionSpec as P


def extended(cells, sides, width):
    for axis, dim in sides:
        count = lax.axis_size(axis)
        ends = count - 1
        head = lax.slice_in_dim(cells, 0, width, axis=dim)
        tail = lax.slice_in_dim(cells, cells.shape[dim] - width, cells.shape[dim], axis=dim)
        cells = jnp.concatenate(
            [
                lax.ppermute(tail, axis, [(i, (i + 1) % count) for i in range(ends)]),
                cells,
                lax.ppermute(head, axis, [((i + 1) % count, i) for i in range(ends)]),
            ],
            axis=dim,
        )
    return cells


def block_window(padded, stale_before, stale_after, block_rows):
    whole = jnp.concatenate([padded, stale_before, stale_after], axis=0)
    return whole.reshape(whole.shape[0] // block_rows, block_rows, whole.shape[1])


def pick_slot(slot_index, tile_vals, tile_src, tile_count):
    source = lax.dynamic_index_in_dim(tile_src, slot_index, 1, keepdims=False)
    tile_slot = lax.dynamic_index_in_dim(tile_vals, slot_index, 1, keepdims=False)
    live_mask = (slot_index < tile_count).astype(tile_slot.dtype)
    return (tile_slot * live_mask[:, None, None], source)


def run_slots(add_slot, running, tile_src):
    for slot_index in range(tile_src.shape[1]):
        running = add_slot(slot_index, running)
    return running


def aggregate(window, tile_vals, tile_src, tile_count):
    block_count = tile_vals.shape[0]
    block_rows = tile_vals.shape[-1]
    columns = window.shape[-1]

    def add_slot(slot_index, running):
        tile_live, source = pick_slot(slot_index, tile_vals, tile_src, tile_count)
        picked = jnp.take(window, source, axis=0)
        return running + jnp.einsum(
            "rab,rbw->raw", tile_live, picked, preferred_element_type=jnp.float32
        )

    running = jnp.zeros((block_count, block_rows, columns), jnp.float32)
    running = run_slots(add_slot, running, tile_src)
    return running.reshape(block_count * block_rows, columns)


def spread(grads, tile_vals, tile_src, tile_count):
    block_count = tile_vals.shape[0]
    block_rows = tile_vals.shape[-1]
    columns = grads.shape[-1]
    grad_blocks = grads.reshape(block_count, block_rows, columns)
    reach_count = block_count + 2
    targets = jnp.arange(reach_count, dtype=jnp.int32)

    def add_slot(slot_index, running):
        tile_live, source = pick_slot(slot_index, tile_vals, tile_src, tile_count)
        contrib = jnp.einsum(
            "rab,raw->rbw", tile_live, grad_blocks, preferred_element_type=jnp.float32
        )
        placing = (targets[:, None] == source[None, :]).astype(jnp.float32)
        return running + jnp.einsum(
            "tr,rbw->tbw", placing, contrib, precision=lax.Precision.HIGHEST
        )

    running = jnp.zeros((reach_count, block_rows, columns), jnp.float32)
    return run_slots(add_slot, running, tile_src)


def rim_pair(running):
    return jnp.concatenate([running[0], running[-1]], axis=0)


def settle(running, arrived, block_rows):
    own_rows = running[1:-1].reshape(-1, running.shape[-1])
    remainder = own_rows.shape[0] - block_rows
    upper = jnp.pad(arrived[:block_rows], ((0, remainder), (0, 0)))
    lower = jnp.pad(arrived[arrived.shape[0] - block_rows :], ((remainder, 0), (0, 0)))
    return own_rows + upper + lower


def local(feats_t, w_first, w_second, stale_rows, tile_vals, tile_src, tile_count, labels):
    block_rows = tile_vals.shape[-1]
    hidden_width = w_first.shape[1]
    classes = w_second.shape[1]
    vertices = labels.shape[0] * lax.axis_size("grp") * lax.axis_size("dom")
    grad_scale = 1.0 / math.sqrt(vertices)
    stale_count = stale_rows.shape[0]
    stale_padded = extended(stale_rows, (("grp", 0),), stale_count)
    before = stale_padded[:stale_count]
    stale_after = stale_padded[2 * stale_count :]
    feats = lax.all_to_all(feats_t, "dom", split_axis=1, concat_axis=0, tiled=True)
    proj_first = lax.dot_general(
        feats, w_first, (((0,), (0,)), ((), ())), preferred_element_type=jnp.float32
    ).astype(jnp.bfloat16)
    padded_first = extended(proj_first, (("dom", 0),), block_rows)
    window_first = block_window(
        padded_first, before[:, :hidden_width], stale_after[:, :hidden_width], block_rows
    )
    agg_first = aggregate(window_first, tile_vals, tile_src, tile_count)
    squash = jax.nn.sigmoid(agg_first)
    hidden = (agg_first * squash).astype(jnp.bfloat16)
    proj_second = jnp.dot(hidden, w_second, preferred_element_type=jnp.float32).astype(jnp.bfloat16)
    padded_second = extended(proj_second, (("dom", 0),), block_rows)
    window_second = block_window(
        padded_second, before[:, hidden_width:], stale_after[:, hidden_width:], block_rows
    )
    agg_second = aggregate(window_second, tile_vals, tile_src, tile_count)
    logits = agg_second.astype(jnp.bfloat16)
    top_value = jnp.max(agg_second, axis=1, keepdims=True)
    exp_logits = jnp.exp(agg_second - top_value)
    predicted = exp_logits / jnp.sum(exp_logits, axis=1, keepdims=True)
    label_mask = (labels[:, None] == jnp.arange(classes, dtype=jnp.int32)[None, :]).astype(
        jnp.float32
    )
    grad_logits = (predicted - label_mask).astype(jnp.bfloat16)
    spread_second = spread(grad_logits, tile_vals, tile_src, tile_count)
    arrived_second = extended(
        rim_pair(spread_second).astype(jnp.bfloat16), (("dom", 0),), block_rows
    ).astype(jnp.float32)
    grad_p2 = settle(spread_second, arrived_second, block_rows).astype(jnp.bfloat16)
    second_term = (
        lax.dot_general(
            hidden, grad_p2, (((0,), (0,)), ((), ())), preferred_element_type=jnp.float32
        )
        * grad_scale
    )
    second_part = lax.psum_scatter(
        second_term.astype(jnp.bfloat16), "dom", scatter_dimension=0, tiled=True
    ).astype(jnp.float32)
    grad_second = lax.psum(second_part, "grp")
    grad_hidden = lax.dot_general(
        grad_p2, w_second, (((1,), (1,)), ((), ())), preferred_element_type=jnp.float32
    )
    grad_agg = (grad_hidden * squash * (1.0 + agg_first * (1.0 - squash))).astype(jnp.bfloat16)
    spread_first = spread(grad_agg, tile_vals, tile_src, tile_count)
    arrived_first = extended(
        rim_pair(spread_first).astype(jnp.bfloat16), (("dom", 0),), block_rows
    ).astype(jnp.float32)
    grad_p1 = settle(spread_first, arrived_first, block_rows).astype(jnp.bfloat16)
    first_term = jnp.dot(feats, grad_p1, preferred_element_type=jnp.float32) * grad_scale
    grad_vertex = lax.dot_general(
        w_first, grad_p1, (((1,), (1,)), ((), ())), preferred_element_type=jnp.float32
    ).astype(jnp.bfloat16)
    grad_feats = lax.all_to_all(grad_vertex, "dom", split_axis=0, concat_axis=1, tiled=True)
    first_part = lax.psum_scatter(
        first_term.astype(jnp.bfloat16), "dom", scatter_dimension=0, tiled=True
    )
    grad_first = lax.psum(first_part, "grp").astype(jnp.float32)
    return (logits, grad_feats, grad_first, grad_second)


def solution(mesh):
    return jax.shard_map(
        local,
        mesh=mesh,
        in_specs=(
            P("dom", "grp"),
            P(),
            P(),
            P(("grp", "dom"), None),
            P(("grp", "dom"), None, None, None),
            P(("grp", "dom"), None),
            P(("grp", "dom")),
            P(("grp", "dom")),
        ),
        out_specs=(P(("grp", "dom"), None), P("dom", "grp"), P("dom", None), P("dom", None)),
        check_vma=False,
    )
```

profile of v0, /device:TPU:1, one launch (start us, length us, event | category | flops | bytes accessed | tf_op | source)
XLA Modules:
  0.0 633.7 jit_solution(16039935903969852206)
XLA Ops:
  7.2 8.9 %collective-permute-start.3 = (bf16[128,1152]{1,0:T(8,128)(2,1)}, bf16[128,1152]{1,0:T(8,128)(2,1)S(1)}, u32[]{:S(2)}, u32[]{:S(2)}) collective-permute-start(bf16[128,1152]{1,0:T(8,128)(2,1)} %param.15), channel_id=1, source_target_pairs={{32,0},{64,32},{96,64},{128,96},{160,128},{192,160},{224,192},{256... | collective-permute-start | bytes 884744 | tf_op jit(solution)/shard_map/ppermute | solution.py:19
  16.1 1.9 collective-permute-start.2
  18.0 1.7 copy.127
  19.7 6.3 all-to-all-start
  26.0 1.0 slice_reduce_fusion
  27.7 0.7 compare_convert_fusion
  28.4 10.6 %all-to-all-done = bf16[16,32,256]{2,0,1:T(8,128)(2,1)S(1)} async-done(((bf16[16,32,256]{2,0,1:T(8,128)(2,1)}), bf16[16,32,256]{2,0,1:T(8,128)(2,1)S(1)}, u32[]{:S(2)}, u32[]{:S(2)}) %all-to-all-start) | async-done | bytes 262176 | tf_op jit(solution)/shard_map/all_to_all | solution.py:105
  39.4 2.1 collective-permute-start
  41.5 1.3 collective-permute-start.1
  42.8 3.9 collective-permute-done
  46.8 3.8 collective-permute-done.1
  50.6 1.0 slice_dynamic-update-slice_fusion.1
  51.7 1.4 gather_fusion.3
  53.1 1.4 gather_fusion.2
  54.5 1.4 gather_fusion.1
  55.8 1.4 gather_fusion
  57.2 1.5 fusion.26
  58.7 1.5 convolution_add_fusion.2
  60.9 1.4 fusion.13
  62.7 3.1 collective-permute-start.4
  65.8 1.3 collective-permute-start.5
  67.1 0.6 constant_dynamic-update-slice_fusion.5
  67.7 0.6 constant_dynamic-update-slice_fusion.4
  68.3 2.1 collective-permute-done.5
  70.4 0.6 constant_dynamic-update-slice_fusion.3
  71.0 1.4 slice_dynamic-update-slice_fusion.3
  72.4 1.4 slice_dynamic-update-slice_fusion.2
  73.8 1.5 gather_fusion.7
  75.3 1.6 gather_fusion.6
  76.9 2.2 gather_fusion.5
  79.1 2.2 gather_fusion.4
  81.4 1.1 fusion.47
  82.4 1.1 convolution_add_fusion.8
  83.5 0.9 convolution_add_fusion.7
  84.4 1.4 fusion.93
  86.2 0.8 subtract_convert_fusion
  88.2 1.1 fusion.42
  89.3 1.2 convolution_add_fusion.5
  90.6 0.5 convolution_add_fusion.4
  91.1 0.5 fusion.95
  91.8 1.3 collective-permute-start.7
  93.1 5.9 collective-permute-start.6
  99.1 0.7 collective-permute-done.6
  102.0 3.0 fusion.17
  105.0 3.0 fusion.21
  108.1 3.0 fusion.19
  111.1 5.1 fusion.96
  116.2 0.7 fusion.89
  117.1 1.3 collective-permute-start.9
  118.4 4.3 collective-permute-start.8
  122.7 1.1 fusion.4
  123.9 2.1 slice.118
  126.9 0.5 fusion.1
  127.4 1.3 copy.94
  128.7 0.5 fusion.5
  129.2 0.8 copy.83
  130.1 18.0 %all-to-all-start.1 = ((bf16[32,16,256]{2,1,0:T(8,128)(2,1)}), bf16[32,16,256]{2,1,0:T(8,128)(2,1)S(1)}, u32[]{:S(2)}, u32[]{:S(2)}) async-start(bf16[32,16,256]{2,1,0:T(8,128)(2,1)} %bitcast.19), calls=%async_computation.1 | async-start | bytes 524288 | tf_op jit(solution)/shard_map/all_to_all | solution.py:158
  148.1 202.4 %reduce-scatter.5.cloned.1.call-done = bf16[32,128]{1,0:T(8,128)(2,1)} async-done(((bf16[1024,128]{1,0:T(8,128)(2,1)}), bf16[32,128]{1,0:T(8,128)(2,1)}) %reduce-scatter.5.cloned.1.call-update) | async-done | bytes 8208 | tf_op jit(solution)/shard_map/reduce_scatter | solution.py:141
  350.5 49.4 %psum.15 = f32[32,128]{1,0:T(8,128)} all-reduce(bf16[32,128]{1,0:T(8,128)(2,1)} %reduce-scatter.5.cloned.1.call-done), channel_id=1, replica_groups=mesh['grp'=16,'dom'=32] {'grp'}, use_global_device_ids=true, to_apply=%region_5.8 | all-reduce | flops 4096 | bytes 24576 | tf_op jit(solution)/shard_map/psum | solution.py:144
  400.0 0.7 copy.101
  400.7 173.2 %reduce-scatter.7.cloned.1.call-done = bf16[16,1024]{1,0:T(8,128)(2,1)} async-done(((bf16[512,1024]{1,0:T(8,128)(2,1)}), bf16[16,1024]{1,0:T(8,128)(2,1)}) %reduce-scatter.7.cloned.1.call-update) | async-done | bytes 32784
  573.9 0.9 copy.95
  574.9 51.2 %psum.14 = bf16[16,1024]{0,1:T(8,128)(2,1)S(1)} all-reduce(bf16[16,1024]{0,1:T(8,128)(2,1)S(1)} %copy.95), channel_id=1, replica_groups=mesh['grp'=16,'dom'=32] {'grp'}, use_global_device_ids=true, to_apply=%region_3.6 | all-reduce | flops 16384 | bytes 65536 | tf_op jit(solution)/shard_map/psum | solution.py:162
  626.1 0.7 copy.85
  (99 shorter events, 7.2 us)
Async XLA Ops:
  7.2 31.8 %copy-start = (bf16[512,1024]{1,0:T(8,128)(2,1)S(1)}, bf16[512,1024]{1,0:T(8,128)(2,1)}, u32[]{:S(2)}) copy-start(bf16[512,1024]{1,0:T(8,128)(2,1)} %param.13) | copy-start | bytes 3145732
  7.2 44.4 %collective-permute-start.3 = (bf16[128,1152]{1,0:T(8,128)(2,1)}, bf16[128,1152]{1,0:T(8,128)(2,1)S(1)}, u32[]{:S(2)}, u32[]{:S(2)}) collective-permute-start(bf16[128,1152]{1,0:T(8,128)(2,1)} %param.15), channel_id=1, source_target_pairs={{32,0},{64,32},{96,64},{128,96},{160,128},{192,160},{224,192},{256... | collective-permute-start | bytes 884744 | tf_op jit(solution)/shard_map/ppermute | solution.py:19
  16.1 34.5 %collective-permute-start.2 = (bf16[128,1152]{1,0:T(8,128)(2,1)}, bf16[128,1152]{1,0:T(8,128)(2,1)}, u32[]{:S(2)}, u32[]{:S(2)}) collective-permute-start(bf16[128,1152]{1,0:T(8,128)(2,1)} %param.15), channel_id=1, source_target_pairs={{0,32},{32,64},{64,96},{96,128},{128,160},{160,192},{192,224},{224... | collective-permute-start | bytes 884744 | tf_op jit(solution)/shard_map/ppermute | solution.py:17
  19.7 19.2 %all-to-all-start = ((bf16[16,32,256]{2,0,1:T(8,128)(2,1)}), bf16[16,32,256]{2,0,1:T(8,128)(2,1)S(1)}, u32[]{:S(2)}, u32[]{:S(2)}) async-start(bf16[16,32,256]{2,0,1:T(8,128)(2,1)} %bitcast.121), calls=%async_computation | async-start | bytes 524288 | tf_op jit(solution)/shard_map/all_to_all | solution.py:105
  26.0 324.5 %reduce-scatter.5.cloned.1.call-start = ((), (), s32[]{:S(2)}) async-start(), calls=%async_computation.4 | async-start | bytes 270336 | tf_op jit(solution)/shard_map/reduce_scatter | solution.py:141
  27.1 0.5 copy-start.7
  27.1 0.6 copy-start.11
  27.1 0.6 copy-start.13
  27.1 19.7 %copy-start.9 = (s32[2]{0:T(128)}, s32[2]{0:T(128)S(1)}, u32[]{:S(2)}) copy-start(s32[2]{0:T(128)S(1)} %get-tuple-element.27) | copy-start | bytes 28
  27.1 33.4 %copy-start.21 = (pred[2]{0:T(512)(128)(4,1)}, pred[2]{0:T(512)(128)(4,1)S(1)}, u32[]{:S(2)}) copy-start(pred[2]{0:T(512)(128)(4,1)S(1)} %compare_and_fusion.1) | copy-start | bytes 10
  27.2 25.9 %copy-start.15 = (s32[1024]{0:T(1024)}, s32[1024]{0:T(1024)S(1)}, u32[]{:S(2)}) copy-start(s32[1024]{0:T(1024)S(1)} %pad_clamp_fusion.1) | copy-start | bytes 12292
  27.7 29.5 %copy-start.20 = (pred[2]{0:T(512)(128)(4,1)}, pred[2]{0:T(512)(128)(4,1)S(1)}, u32[]{:S(2)}) copy-start(pred[2]{0:T(512)(128)(4,1)S(1)} %get-tuple-element.57) | copy-start | bytes 10
  27.7 32.5 %copy-start.19 = (pred[2]{0:T(512)(128)(4,1)}, pred[2]{0:T(512)(128)(4,1)S(1)}, u32[]{:S(2)}) copy-start(pred[2]{0:T(512)(128)(4,1)S(1)} %get-tuple-element.58) | copy-start | bytes 10
  28.4 30.3 %copy-start.18 = (pred[2]{0:T(512)(128)(4,1)}, pred[2]{0:T(512)(128)(4,1)S(1)}, u32[]{:S(2)}) copy-start(pred[2]{0:T(512)(128)(4,1)S(1)} %get-tuple-element.59) | copy-start | bytes 10
  39.4 7.3 %collective-permute-start = (bf16[128,1024]{1,0:T(8,128)(2,1)S(1)}, bf16[128,1024]{1,0:T(8,128)(2,1)S(1)}, u32[]{:S(2)}, u32[]{:S(2)}) collective-permute-start(bf16[128,1024]{1,0:T(8,128)(2,1)S(1)} %get-tuple-element.36), channel_id=1, source_target_pairs={{0,1},{1,2},{2,3},{3,4},{4,5},{5,6},{6,7},{7,8},{8,9},{9,10},{10,1... | collective-permute-start | bytes 786440 | tf_op jit(solution)/shard_map/ppermute | solution.py:17
  41.5 14.3 %copy-start.16 = (s32[1024]{0:T(1024)}, s32[1024]{0:T(1024)S(1)}, u32[]{:S(2)}) copy-start(s32[1024]{0:T(1024)S(1)} %pad_clamp_fusion.3) | copy-start | bytes 12292
  41.5 12.9 %copy-start.17 = (s32[1024]{0:T(1024)}, s32[1024]{0:T(1024)S(1)}, u32[]{:S(2)}) copy-start(s32[1024]{0:T(1024)S(1)} %pad_clamp_fusion.2) | copy-start | bytes 12292
  41.5 9.1 %collective-permute-start.1 = (bf16[128,1024]{1,0:T(8,128)(2,1)S(1)}, bf16[128,1024]{1,0:T(8,128)(2,1)S(1)}, u32[]{:S(2)}, u32[]{:S(2)}) collective-permute-start(bf16[128,1024]{1,0:T(8,128)(2,1)S(1)} %get-tuple-element.35), channel_id=1, source_target_pairs={{1,0},{2,1},{3,2},{4,3},{5,4},{6,5},{7,6},{8,7},{9,8},{10,9},{11,1... | collective-permute-start | bytes 786440 | tf_op jit(solution)/shard_map/ppermute | solution.py:19
  51.6 5.6 copy-start.6
  51.7 5.6 copy-start.2
  57.2 3.0 copy-start.4
  58.7 1.9 copy-start.3
  60.9 1.4 copy-start.5
  62.7 4.4 collective-permute-start.4
  65.8 4.7 collective-permute-start.5
  81.4 9.2 %copy-start.12 = (s32[2]{0:T(128)S(1)}, s32[2]{0:T(128)}, u32[]{:S(2)}) copy-start(s32[2]{0:T(128)} %copy-done.11) | copy-start | bytes 28
  83.5 7.6 %copy-start.14 = (s32[2]{0:T(128)S(1)}, s32[2]{0:T(128)}, u32[]{:S(2)}) copy-start(s32[2]{0:T(128)} %copy-done.13) | copy-start | bytes 28
  88.2 11.7 %copy-start.22 = (pred[256]{0:T(512)(128)(4,1)S(1)}, pred[256]{0:T(512)(128)(4,1)}, u32[]{:S(2)}) copy-start(pred[256]{0:T(512)(128)(4,1)} %constant.115.clone.1) | copy-start | bytes 772
  89.3 10.7 %copy-start.1 = (f32[256,1024]{1,0:T(8,128)S(1)}, f32[256,1024]{1,0:T(8,128)}, u32[]{:S(2)}) copy-start(f32[256,1024]{1,0:T(8,128)} %get-tuple-element.34) | copy-start | bytes 3145732
  91.8 7.3 %collective-permute-start.7 = (bf16[128,128]{1,0:T(8,128)(2,1)S(1)}, bf16[128,128]{1,0:T(8,128)(2,1)S(1)}, u32[]{:S(2)}, u32[]{:S(2)}) collective-permute-start(bf16[128,128]{1,0:T(8,128)(2,1)S(1)} %bitcast.146), channel_id=1, source_target_pairs={{1,0},{2,1},{3,2},{4,3},{5,4},{6,5},{7,6},{8,7},{9,8},{10,9},{11,1... | collective-permute-start | bytes 98312 | tf_op jit(solution)/shard_map/ppermute | solution.py:19
  93.1 6.7 %collective-permute-start.6 = (bf16[128,128]{1,0:T(8,128)(2,1)S(1)}, bf16[128,128]{1,0:T(8,128)(2,1)S(1)}, u32[]{:S(2)}, u32[]{:S(2)}) collective-permute-start(bf16[128,128]{1,0:T(8,128)(2,1)S(1)} %bitcast.143), channel_id=1, source_target_pairs={{0,1},{1,2},{2,3},{3,4},{4,5},{5,6},{6,7},{7,8},{8,9},{9,10},{10,1... | collective-permute-start | bytes 98312 | tf_op jit(solution)/shard_map/ppermute | solution.py:17
  101.6 3.5 copy-start.8
  105.0 3.0 copy-start.10
  117.1 9.2 %collective-permute-start.9 = (bf16[128,1024]{1,0:T(8,128)(2,1)S(1)}, bf16[128,1024]{1,0:T(8,128)(2,1)S(1)}, u32[]{:S(2)}, u32[]{:S(2)}) collective-permute-start(bf16[128,1024]{1,0:T(8,128)(2,1)S(1)} %bitcast.139), channel_id=1, source_target_pairs={{1,0},{2,1},{3,2},{4,3},{5,4},{6,5},{7,6},{8,7},{9,8},{10,9},{11,1... | collective-permute-start | bytes 786440 | tf_op jit(solution)/shard_map/ppermute | solution.py:19
  118.4 7.9 %collective-permute-start.8 = (bf16[128,1024]{1,0:T(8,128)(2,1)S(1)}, bf16[128,1024]{1,0:T(8,128)(2,1)S(1)}, u32[]{:S(2)}, u32[]{:S(2)}) collective-permute-start(bf16[128,1024]{1,0:T(8,128)(2,1)S(1)} %bitcast.136), channel_id=1, source_target_pairs={{0,1},{1,2},{2,3},{3,4},{4,5},{5,6},{6,7},{7,8},{8,9},{9,10},{10,1... | collective-permute-start | bytes 786440 | tf_op jit(solution)/shard_map/ppermute | solution.py:17
  123.8 450.1 %reduce-scatter.7.cloned.1.call-start = ((), (), s32[]{:S(2)}) async-start(), calls=%async_computation.5 | async-start | bytes 1081344
  130.1 269.9 %all-to-all-start.1 = ((bf16[32,16,256]{2,1,0:T(8,128)(2,1)}), bf16[32,16,256]{2,1,0:T(8,128)(2,1)S(1)}, u32[]{:S(2)}, u32[]{:S(2)}) async-start(bf16[32,16,256]{2,1,0:T(8,128)(2,1)} %bitcast.19), calls=%async_computation.1 | async-start | bytes 524288 | tf_op jit(solution)/shard_map/all_to_all | solution.py:158
Sparse Core Ops, SparseCore 0:
  123.9 226.5 reduce-scatter.4
  355.5 218.3 reduce-scatter.6
where the time goes:
time: 637 us; the launch traced here: 634 us
  waiting for transfers between devices  397 us (62%)
  blocking collectives  101 us (16%)
  starting transfers between devices  55.7 us (9%)
  matrix products  31.5 us (5%)
  local copies, waits for them, and re-layouts  30.2 us (5%)
  between operations  14.8 us (2%)
    reduce_scatter x1, waiting for transfers between devices, local(): lax.psum_scatter(second_term.astype(jnp.bfloat16), 'dom', scatter_dimensi...  202 us
    unnamed x3, waiting for transfers between devices  173 us
    psum x1, blocking collectives, local(): grad_first = lax.psum(first_part, 'grp').astype(jnp.float32)  51.2 us
    psum x1, blocking collectives, local(): grad_second = lax.psum(second_part, 'grp')  49.4 us
    all_to_all x1, starting transfers between devices, local(): lax.all_to_all(grad_vertex, 'dom', split_axis=0, concat_axis=1, tiled=True)  18 us
    dot_general x8, matrix products, add_slot(): jnp.einsum('tr,rbw->tbw', placing, contrib, precision=lax.Precision.HIGHEST)  17.6 us
    ppermute x5, starting transfers between devices, extended(): lax.ppermute(tail, axis, [(i, (i + 1) % count) for i in range(ends)])  17.2 us
    ppermute x5, starting transfers between devices, extended(): lax.ppermute(head, axis, [((i + 1) % count, i) for i in range(ends)])  14.1 us
  transfers between devices with their start and end apart: 14, of which 7 were waited for; matrix products, arithmetic and copies ran while one was open for 2% of the time, Pallas kernels for 0%

commit v1 on v0

v1 whole, which is shorter than its diff:
```python
import math

import jax
import jax.numpy as jnp
from jax import lax
from jax.sharding import PartitionSpec as P

BF = jnp.bfloat16
F32 = jnp.float32


def dot(a, b, ca, cb):
    return lax.dot_general(a, b, (((ca,), (cb,)), ((), ())), preferred_element_type=F32)


def swapped(x, axis):
    count = lax.axis_size(axis)
    return lax.ppermute(x, axis, [(i, i ^ 1) for i in range(count)])


def from_previous(x, axis):
    count = lax.axis_size(axis)
    return lax.ppermute(x, axis, [(i, i + 1) for i in range(count - 1)])


def from_next(x, axis):
    count = lax.axis_size(axis)
    return lax.ppermute(x, axis, [(i + 1, i) for i in range(count - 1)])


def adjacency(tile_vals, tile_src, tile_count, window_blocks):
    block_rows, slots, blk, _ = tile_vals.shape
    live = jnp.arange(slots, dtype=jnp.int32)[None, :] < tile_count[:, None]
    columns = []
    for t in range(window_blocks):
        hit = (tile_src == t) & live
        block = jnp.zeros((block_rows, blk, blk), BF)
        for k in range(slots):
            block = jnp.where(hit[:, k, None, None], tile_vals[:, k], block)
        columns.append(block.reshape(block_rows * blk, blk))
    return jnp.concatenate(columns, axis=1)


def local(feats_t, w_first, w_second, stale_rows, tile_vals, tile_src, tile_count, labels):
    blk = tile_vals.shape[-1]
    hid = w_first.shape[1]
    classes = w_second.shape[1]
    own = labels.shape[0]
    reach = own + 2 * blk
    n_grp, n_dom = lax.axis_size("grp"), lax.axis_size("dom")
    scale = 1.0 / math.sqrt(own * n_grp * n_dom)
    feat_rows = feats_t.shape[0]
    feat_all = feat_rows * n_dom
    half = hid // 2
    core = lax.axis_index("grp") % 2

    parts = feats_t.reshape(feat_rows, n_dom, own)
    edge = jnp.zeros((feat_rows, 1, blk), BF)
    left = jnp.concatenate([edge, parts[:, :-1, own - blk :]], axis=1)
    right = jnp.concatenate([parts[:, 1:, :blk], edge], axis=1)
    wide = jnp.concatenate([left, parts, right], axis=2)
    feats = lax.all_to_all(wide, "dom", split_axis=1, concat_axis=0, tiled=True).reshape(feat_all, reach)

    before = from_previous(stale_rows, "grp")
    after = from_next(stale_rows, "grp")
    adj_all = adjacency(tile_vals, tile_src, tile_count, reach // blk + 2)
    adj = adj_all[:, :reach]
    stale_part = dot(adj_all[:, reach:], jnp.concatenate([before, after], axis=0), 1, 0)

    feats_agg = dot(adj, feats, 1, 1).astype(BF)
    agg_first = dot(feats_agg, w_first, 1, 0) + stale_part[:, :hid]
    squash = jax.nn.sigmoid(agg_first)
    hidden = (agg_first * squash).astype(BF)
    proj_second = dot(hidden, w_second, 1, 0).astype(BF)

    window = jnp.concatenate(
        [from_previous(proj_second[own - blk :], "dom"), proj_second, from_next(proj_second[:blk], "dom")], axis=0
    )
    agg_second = dot(adj, window, 1, 0) + stale_part[:, hid:]
    logits = agg_second.astype(BF)
    top_value = jnp.max(agg_second, axis=1, keepdims=True)
    exp_logits = jnp.exp(agg_second - top_value)
    predicted = exp_logits / jnp.sum(exp_logits, axis=1, keepdims=True)
    mark = (labels[:, None] == jnp.arange(classes, dtype=jnp.int32)[None, :]).astype(F32)
    grad_logits = (predicted - mark).astype(BF)

    spread_second = dot(adj, grad_logits, 0, 0)
    to_first = from_previous(spread_second[reach - blk :].astype(BF), "dom").astype(F32)
    to_last = from_next(spread_second[:blk].astype(BF), "dom").astype(F32)
    inner = jnp.zeros((own - blk, classes), F32)
    grad_p2 = (
        spread_second[blk : reach - blk]
        + jnp.concatenate([to_first, inner], axis=0)
        + jnp.concatenate([inner, to_last], axis=0)
    ).astype(BF)

    grad_hidden = dot(grad_p2, w_second, 1, 1)
    grad_agg = (grad_hidden * squash * (1.0 + agg_first * (1.0 - squash))).astype(BF)
    first_term = (dot(feats_agg, grad_agg, 0, 0) * scale).astype(BF)
    second_term = (dot(hidden, grad_p2, 0, 0) * scale).astype(BF)
    first_pair = jnp.stack([first_term[:, :half], first_term[:, half:]])
    second_pair = second_term.reshape(n_dom, 2, feat_rows, classes).transpose(1, 0, 2, 3).reshape(2, feat_all, classes)
    both = jnp.concatenate([first_pair, second_pair], axis=2)
    keep = lax.dynamic_index_in_dim(both, core, 0, keepdims=False)
    send = lax.dynamic_index_in_dim(both, 1 - core, 0, keepdims=False)
    summed = (keep.astype(F32) + swapped(send, "grp").astype(F32)).astype(BF)

    back = dot(grad_agg, w_first, 1, 1).astype(BF)
    grad_wide = dot(back, adj, 0, 0).astype(BF)
    sent = jnp.concatenate([summed, grad_wide], axis=1)
    got = lax.all_to_all(sent, "dom", split_axis=0, concat_axis=0, tiled=True).reshape(n_dom, feat_rows, -1)

    width = half + classes
    band = jnp.sum(got[:, :, :width].astype(F32), axis=0).astype(BF)
    copies = jnp.broadcast_to(band[None], (n_grp, feat_rows, width))
    bands = lax.all_to_all(copies, "grp", split_axis=0, concat_axis=0, tiled=True)
    total = jnp.sum(bands.reshape(n_grp // 2, 2, feat_rows, width).astype(F32), axis=0)
    grad_first = jnp.concatenate([total[0, :, :half], total[1, :, :half]], axis=1)
    grad_second = total[:, :, half:].reshape(2 * feat_rows, classes)

    wide_back = got[:, :, width:].astype(F32)
    none = jnp.zeros((1, feat_rows, blk), F32)
    first_block = jnp.concatenate([none, wide_back[:-1, :, reach - blk :]], axis=0)
    last_block = jnp.concatenate([wide_back[1:, :, :blk], none], axis=0)
    middle = jnp.zeros((n_dom, feat_rows, own - blk), F32)
    grad_feats = (
        wide_back[:, :, blk : reach - blk]
        + jnp.concatenate([first_block, middle], axis=2)
        + jnp.concatenate([middle, last_block], axis=2)
    )
    grad_feats = grad_feats.astype(BF).transpose(1, 0, 2).reshape(feat_rows, n_dom * own)
    return (logits, grad_feats, grad_first, grad_second)


def solution(mesh):
    return jax.shard_map(
        local,
        mesh=mesh,
        in_specs=(
            P("dom", "grp"),
            P(),
            P(),
            P(("grp", "dom"), None),
            P(("grp", "dom"), None, None, None),
            P(("grp", "dom"), None),
            P(("grp", "dom")),
            P(("grp", "dom")),
        ),
        out_specs=(P(("grp", "dom"), None), P("dom", "grp"), P("dom", None), P("dom", None)),
        check_vma=False,
    )
```

time: 637 us -> 140 us (0.22)
  waiting for transfers between devices: 397 us -> 26.3 us
  blocking collectives: 101 us -> 45.9 us
  matrix products: 31.5 us -> 8.8 us
  local copies, waits for them, and re-layouts: 30.2 us -> 9.05 us
  between operations: 14.8 us -> 1.06 us
  starting transfers between devices: 55.7 us -> 43.7 us
    reduce_scatter x1 -> x0, waiting for transfers between devices: 202 us -> none  [local(): lax.psum_scatter(second_term.astype(jnp.bfloat16), 'dom', scatter_dimensi...]
    unnamed x3 -> x0, waiting for transfers between devices: 173 us -> none
    psum x2 -> x0, blocking collectives: 101 us -> none  [the longest x1 51.2 us: local(): grad_first = lax.psum(first_part, 'grp').astype(jnp.float32)]
    all_to_all x0 -> x1, blocking collectives: none -> 45.9 us  [local(): lax.all_to_all(sent, 'dom', split_axis=0, concat_axis=0, tiled=True)]
    dot_general x30 -> x10, matrix products: 31.5 us -> 8.8 us  [dot(): lax.dot_general(a, b, (((ca,), (cb,)), ((), ())), preferred_element_type=...]
    all_to_all x2, waiting for transfers between devices: 10.6 us -> 24.3 us  [the longest x1 12.2 us: local(): lax.all_to_all(wide, 'dom', split_axis=1, concat_axis=0, tiled=True)]
    gather x8 -> x0, local copies, waits for them, and re-layouts: 13.1 us -> none  [add_slot(): picked = jnp.take(window, source, axis=0)]
    ppermute x10 -> x7, waiting for transfers between devices: 10.5 us -> 1.96 us  [the longest x3 1.95 us: from_previous(): return lax.ppermute(x, axis, [(i, i + 1) for i in range(count - 1)])]
  transfers between devices with their start and end apart: 14 -> 9, of which waited for: 7 -> 4; matrix products, arithmetic and copies ran while one was open for 2% -> 8% of each run, Pallas kernels for 0% -> 0%
where the time goes in v1:
time: 140 us; the launch traced here: 139 us
  blocking collectives  45.9 us (33%)
  starting transfers between devices  43.7 us (31%)
  waiting for transfers between devices  26.3 us (19%)
  local copies, waits for them, and re-layouts  9.05 us (6%)
  matrix products  8.8 us (6%)
  other arithmetic  4.16 us (3%)
    all_to_all x1, blocking collectives, local(): lax.all_to_all(sent, 'dom', split_axis=0, concat_axis=0, tiled=True)  45.9 us
    all_to_all x1, waiting for transfers between devices, local(): lax.all_to_all(wide, 'dom', split_axis=1, concat_axis=0, tiled=True)  12.2 us
    all_to_all x1, waiting for transfers between devices, local(): lax.all_to_all(copies, 'grp', split_axis=0, concat_axis=0, tiled=True)  12.1 us
    all_to_all x1, starting transfers between devices, local(): lax.all_to_all(copies, 'grp', split_axis=0, concat_axis=0, tiled=True)  11.9 us
    ppermute x3, starting transfers between devices, from_next(): return lax.ppermute(x, axis, [(i + 1, i) for i in range(count - 1)])  11.5 us
    ppermute x3, starting transfers between devices, from_previous(): return lax.ppermute(x, axis, [(i, i + 1) for i in range(count - 1)])  10.6 us
    dot_general x10, matrix products, dot(): lax.dot_general(a, b, (((ca,), (cb,)), ((), ())), preferred_element_type=...  8.8 us
    all_to_all x1, starting transfers between devices, local(): lax.all_to_all(wide, 'dom', split_axis=1, concat_axis=0, tiled=True)  6.27 us
  transfers between devices with their start and end apart: 9, of which 4 were waited for; matrix products, arithmetic and copies ran while one was open for 8% of the time, Pallas kernels for 0%

profile of v1, /device:TPU:1, one launch (start us, length us, event | category | flops | bytes accessed | tf_op | source)
XLA Modules:
  0.0 138.9 jit_solution(12004744844037815455)
XLA Ops:
  0.6 8.9 %collective-permute-start.1 = (bf16[128,1152]{1,0:T(8,128)(2,1)}, bf16[128,1152]{1,0:T(8,128)(2,1)S(1)}, u32[]{:S(2)}, u32[]{:S(2)}) collective-permute-start(bf16[128,1152]{1,0:T(8,128)(2,1)} %param.11), channel_id=1, source_target_pairs={{32,0},{64,32},{96,64},{128,96},{160,128},{192,160},{224,192},{256... | collective-permute-start | bytes 884744 | tf_op jit(solution)/shard_map/ppermute | solution.py:28
  9.6 1.9 %collective-permute-start = (bf16[128,1152]{1,0:T(8,128)(2,1)}, bf16[128,1152]{1,0:T(8,128)(2,1)S(1)}, u32[]{:S(2)}, u32[]{:S(2)}) collective-permute-start(bf16[128,1152]{1,0:T(8,128)(2,1)} %param.11), channel_id=1, source_target_pairs={{0,32},{32,64},{64,96},{96,128},{128,160},{160,192},{192,224},{224... | collective-permute-start | bytes 884744 | tf_op jit(solution)/shard_map/ppermute | solution.py:23
  11.5 1.0 copy.38
  12.6 0.1 fusion.10
  12.7 1.1 copy.30
  13.8 6.3 %all-to-all-start = ((bf16[16,32,512]{2,0,1:T(8,128)(2,1)}), bf16[16,32,512]{2,0,1:T(8,128)(2,1)S(1)}, u32[]{:S(2)}, u32[]{:S(2)}) async-start(bf16[16,32,512]{2,0,1:T(8,128)(2,1)} %copy.30), calls=%async_computation | async-start | bytes 1048576 | tf_op jit(solution)/shard_map/all_to_all | solution.py:62
  20.1 0.1 compare_and_fusion.5
  20.2 0.3 slice_reduce_fusion.12
  20.5 0.1 broadcast_bitcast_fusion.8
  20.6 0.1 broadcast_bitcast_fusion.9
  20.6 0.1 broadcast_bitcast_fusion.10
  20.7 0.1 broadcast_bitcast_fusion.11
  20.8 0.3 slice_reduce_fusion.4
  21.1 0.1 broadcast_bitcast_fusion.4
  21.2 0.1 broadcast_bitcast_fusion.5
  21.2 0.1 broadcast_bitcast_fusion.6
  21.5 0.1 broadcast_bitcast_fusion.2
  21.6 0.1 broadcast_bitcast_fusion.3
  21.7 0.3 slice_reduce_fusion.20
  22.0 0.1 broadcast_bitcast_fusion.20
  22.0 0.1 broadcast_bitcast_fusion.21
  22.1 0.1 broadcast_bitcast_fusion.22
  22.5 0.1 broadcast_bitcast_fusion.19
  22.6 0.1 broadcast_bitcast_fusion.12
  22.6 0.1 broadcast_bitcast_fusion.13
  22.7 0.1 broadcast_bitcast_fusion.14
  22.8 0.6 fusion.37
  23.4 0.1 broadcast_bitcast_fusion.15
  23.5 1.2 fusion.28
  24.8 0.3 fusion.6
  25.1 12.2 %all-to-all-done = bf16[16,32,512]{2,0,1:T(8,128)(2,1)S(1)} async-done(((bf16[16,32,512]{2,0,1:T(8,128)(2,1)}), bf16[16,32,512]{2,0,1:T(8,128)(2,1)S(1)}, u32[]{:S(2)}, u32[]{:S(2)}) %all-to-all-start) | async-done | bytes 524320 | tf_op jit(solution)/shard_map/all_to_all | solution.py:62
  37.3 1.2 convolution_convert_fusion.2
  38.6 1.4 %multiply_convert_fusion.1 = (bf16[256,1024]{1,0:T(8,128)(2,1)S(1)}, f32[256,1024]{1,0:T(8,128)}) fusion(f32[256,1152]{1,0:T(8,128)S(1)} %fusion.6, bf16[256,512]{1,0:T(8,128)(2,1)S(1)} %convolution_convert_fusion.2, bf16[512,1024]{1,0:T(8,128)(2,1)S(1)} %copy-done), kind=kOutput, calls=%fused_computation.18 | convolution fusion | flops 270008320 | bytes 3932160 | tf_op jit(solution)/shard_map/dot_general | solution.py:13
  40.0 0.3 convolution_convert_fusion.3
  40.3 1.3 collective-permute-start.3
  41.6 4.0 %collective-permute-start.2 = (bf16[128,128]{1,0:T(8,128)(2,1)S(1)}, bf16[128,128]{1,0:T(8,128)(2,1)S(1)}, u32[]{:S(2)}, u32[]{:S(2)}) collective-permute-start(bf16[128,128]{1,0:T(8,128)(2,1)S(1)} %get-tuple-element.50), channel_id=1, source_target_pairs={{0,1},{1,2},{2,3},{3,4},{4,5},{5,6},{6,7},{7,8},{8,9},{9,10},{10,1... | collective-permute-start | bytes 98312 | tf_op jit(solution)/shard_map/ppermute | solution.py:23
  45.6 1.0 collective-permute-done.2
  46.6 0.3 fusion.56
  46.9 0.7 fusion.24
  47.7 0.4 fusion.57
  48.1 1.3 collective-permute-start.5
  49.4 4.7 %collective-permute-start.4 = (bf16[128,128]{1,0:T(8,128)(2,1)S(1)}, bf16[128,128]{1,0:T(8,128)(2,1)S(1)}, u32[]{:S(2)}, u32[]{:S(2)}) collective-permute-start(bf16[128,128]{1,0:T(8,128)(2,1)S(1)} %get-tuple-element.44), channel_id=1, source_target_pairs={{0,1},{1,2},{2,3},{3,4},{4,5},{5,6},{6,7},{7,8},{8,9},{9,10},{10,1... | collective-permute-start | bytes 98312 | tf_op jit(solution)/shard_map/ppermute | solution.py:23
  54.1 1.0 collective-permute-done.4
  55.1 0.4 fusion.3
  55.5 0.2 copy-done.10
  55.7 1.5 %fusion.2 = bf16[256,1024]{1,0:T(8,128)(2,1)S(1)} fusion(bf16[1024,128]{1,0:T(8,128)(2,1)} %param.10, f32[256,1024]{1,0:T(8,128)S(1)} %copy-done.14, f32[256,1152]{1,0:T(8,128)S(1)} %fusion.6, f32[512,128]{1,0:T(8,128)} %copy-done.4, bf16[128,128]{1,0:T(8,128)(2,1)} %copy-done.9, bf16[128,128]{1,0:T(8,128)(2,1)} %copy-done.10), kind=kOutput, calls=%fused_computation.6 | convolution fusion | flops 69894144 | bytes 3080192 | tf_op jit(solution)/shard_map/dot_general | solution.py:13
  57.3 0.5 multiply_convert_fusion
  57.8 0.1 pad_maximum_fusion
  57.9 0.9 dynamic-slice_bitcast_fusion
  58.8 3.4 %collective-permute-start.6 = (bf16[512,640]{1,0:T(8,128)(2,1)}, bf16[512,640]{1,0:T(8,128)(2,1)S(1)}, u32[]{:S(2)}, u32[]{:S(2)}) collective-permute-start(bf16[512,640]{1,0:T(8,128)(2,1)} %dynamic-slice_bitcast_fusion), channel_id=1, source_target_pairs={{0,32},{32,0},{64,96},{96,64},{128,160},{160,128},{192,224},{224,1... | collective-permute-start | bytes 1966088 | tf_op jit(solution)/shard_map/ppermute | solution.py:18
  62.2 2.5 %convolution_convert_fusion = bf16[512,512]{1,0:T(8,128)(2,1)} fusion(bf16[256,1024]{1,0:T(8,128)(2,1)S(1)} %fusion.2, bf16[512,1024]{1,0:T(8,128)(2,1)S(1)} %copy-done, bf16[256,128]{1,0:T(8,128)(2,1)} %copy-done.5, bf16[256,128]{1,0:T(8,128)(2,1)} %get-tuple-element.34, bf16[256,128]{1,0:T(8,128)(2,1)} %copy-done.7, bf16[256,128]{1,0:T(8,128)(2,1)} %copy-done.6), kind=kOutput, calls=%fused_computation.7 | convolution fusion | flops 404094976 | bytes 2359296 | tf_op jit(solution)/shard_map/dot_general | solution.py:13
  64.7 0.2 fusion.1
  64.9 0.9 copy-done.1
  65.8 0.1 pad_maximum_fusion.1
  65.9 45.9 %all_to_all.29 = bf16[32,16,1152]{2,1,0:T(8,128)(2,1)S(1)} all-to-all(bf16[32,16,1152]{2,1,0:T(8,128)(2,1)S(1)} %bitcast.155), channel_id=1, replica_groups=mesh['grp'=16,'dom'=32] {'dom'}, dimensions={0} | all-to-all | bytes 2359296 | tf_op jit(solution)/shard_map/all_to_all | solution.py:111
  111.7 0.1 slice_reduce_fusion
  111.8 0.7 broadcast_in_dim.379
  112.6 11.9 %all-to-all-start.2 = ((bf16[16,16,640]{2,1,0:T(8,128)(2,1)}), bf16[16,16,640]{2,1,0:T(8,128)(2,1)S(1)}, u32[]{:S(2)}, u32[]{:S(2)}) async-start(bf16[16,16,640]{2,1,0:T(8,128)(2,1)} %broadcast_in_dim.379), calls=%async_computation.2 | async-start | bytes 655360 | tf_op jit(solution)/shard_map/all_to_all | solution.py:116
  124.5 0.1 slice_convert_fusion
  124.7 0.1 fusion.13
  124.8 0.7 copy.37
  125.5 12.1 %all-to-all-done.2 = bf16[16,16,640]{2,1,0:T(8,128)(2,1)S(1)} async-done(((bf16[16,16,640]{2,1,0:T(8,128)(2,1)}), bf16[16,16,640]{2,1,0:T(8,128)(2,1)S(1)}, u32[]{:S(2)}, u32[]{:S(2)}) %all-to-all-start.2) | async-done | bytes 327712 | tf_op jit(solution)/shard_map/all_to_all | solution.py:116
  137.7 0.6 slice.232
  138.3 0.6 pad_maximum_fusion.3
  (49 shorter events, 0.9 us)
Async XLA Ops:
  0.6 37.9 %copy-start = (bf16[512,1024]{1,0:T(8,128)(2,1)S(1)}, bf16[512,1024]{1,0:T(8,128)(2,1)}, u32[]{:S(2)}) copy-start(bf16[512,1024]{1,0:T(8,128)(2,1)} %param.9) | copy-start | bytes 3145732
  0.6 24.1 %collective-permute-start.1 = (bf16[128,1152]{1,0:T(8,128)(2,1)}, bf16[128,1152]{1,0:T(8,128)(2,1)S(1)}, u32[]{:S(2)}, u32[]{:S(2)}) collective-permute-start(bf16[128,1152]{1,0:T(8,128)(2,1)} %param.11), channel_id=1, source_target_pairs={{32,0},{64,32},{96,64},{128,96},{160,128},{192,160},{224,192},{256... | collective-permute-start | bytes 884744 | tf_op jit(solution)/shard_map/ppermute | solution.py:28
  9.6 15.2 %collective-permute-start = (bf16[128,1152]{1,0:T(8,128)(2,1)}, bf16[128,1152]{1,0:T(8,128)(2,1)S(1)}, u32[]{:S(2)}, u32[]{:S(2)}) collective-permute-start(bf16[128,1152]{1,0:T(8,128)(2,1)} %param.11), channel_id=1, source_target_pairs={{0,32},{32,64},{64,96},{96,128},{128,160},{160,192},{192,224},{224... | collective-permute-start | bytes 884744 | tf_op jit(solution)/shard_map/ppermute | solution.py:23
  12.6 7.5 %copy-start.2 = (bf16[2,4,128,128]{3,2,1,0:T(8,128)(2,1)S(1)}, bf16[2,4,128,128]{3,2,1,0:T(8,128)(2,1)}, u32[]{:S(2)}) copy-start(bf16[2,4,128,128]{3,2,1,0:T(8,128)(2,1)} %param.12) | copy-start | bytes 786436
  12.7 7.4 %copy-start.11 = (s32[2,4]{1,0:T(2,128)S(1)}, s32[2,4]{1,0:T(2,128)}, u32[]{:S(2)}) copy-start(s32[2,4]{1,0:T(2,128)} %param.13) | copy-start | bytes 100
  12.7 7.4 %copy-start.12 = (s32[2]{0:T(128)S(1)}, s32[2]{0:T(128)}, u32[]{:S(2)}) copy-start(s32[2]{0:T(128)} %param.14) | copy-start | bytes 28
  13.8 23.6 %all-to-all-start = ((bf16[16,32,512]{2,0,1:T(8,128)(2,1)}), bf16[16,32,512]{2,0,1:T(8,128)(2,1)S(1)}, u32[]{:S(2)}, u32[]{:S(2)}) async-start(bf16[16,32,512]{2,0,1:T(8,128)(2,1)} %copy.30), calls=%async_computation | async-start | bytes 1048576 | tf_op jit(solution)/shard_map/all_to_all | solution.py:62
  23.4 24.2 %copy-start.5 = (bf16[256,128]{1,0:T(8,128)(2,1)}, bf16[256,128]{1,0:T(8,128)(2,1)S(1)}, u32[]{:S(2)}) copy-start(bf16[256,128]{1,0:T(8,128)(2,1)S(1)} %get-tuple-element.35) | copy-start | bytes 196612
  24.7 22.9 %copy-start.6 = (bf16[256,128]{1,0:T(8,128)(2,1)}, bf16[256,128]{1,0:T(8,128)(2,1)S(1)}, u32[]{:S(2)}) copy-start(bf16[256,128]{1,0:T(8,128)(2,1)S(1)} %get-tuple-element.32) | copy-start | bytes 196612
  24.7 22.9 %copy-start.7 = (bf16[256,128]{1,0:T(8,128)(2,1)}, bf16[256,128]{1,0:T(8,128)(2,1)S(1)}, u32[]{:S(2)}) copy-start(bf16[256,128]{1,0:T(8,128)(2,1)S(1)} %get-tuple-element.33) | copy-start | bytes 196612
  38.5 1.5 %copy-start.3 = (bf16[1024,128]{1,0:T(8,128)(2,1)S(1)}, bf16[1024,128]{1,0:T(8,128)(2,1)}, u32[]{:S(2)}) copy-start(bf16[1024,128]{1,0:T(8,128)(2,1)} %param.10) | copy-start | bytes 786436
  38.5 8.1 %copy-start.8 = (bf16[256,128]{1,0:T(8,128)(2,1)S(1)}, bf16[256,128]{1,0:T(8,128)(2,1)}, u32[]{:S(2)}) copy-start(bf16[256,128]{1,0:T(8,128)(2,1)} %get-tuple-element.34) | copy-start | bytes 196612
  40.0 7.7 %copy-start.13 = (s32[256]{0:T(256)S(1)}, s32[256]{0:T(256)}, u32[]{:S(2)}) copy-start(s32[256]{0:T(256)} %param.15) | copy-start | bytes 3076
  40.3 5.3 %collective-permute-start.3 = (bf16[128,128]{1,0:T(8,128)(2,1)S(1)}, bf16[128,128]{1,0:T(8,128)(2,1)S(1)}, u32[]{:S(2)}, u32[]{:S(2)}) collective-permute-start(bf16[128,128]{1,0:T(8,128)(2,1)S(1)} %get-tuple-element.51), channel_id=1, source_target_pairs={{1,0},{2,1},{3,2},{4,3},{5,4},{6,5},{7,6},{8,7},{9,8},{10,9},{11,1... | collective-permute-start | bytes 98312 | tf_op jit(solution)/shard_map/ppermute | solution.py:28
  41.6 5.0 %collective-permute-start.2 = (bf16[128,128]{1,0:T(8,128)(2,1)S(1)}, bf16[128,128]{1,0:T(8,128)(2,1)S(1)}, u32[]{:S(2)}, u32[]{:S(2)}) collective-permute-start(bf16[128,128]{1,0:T(8,128)(2,1)S(1)} %get-tuple-element.50), channel_id=1, source_target_pairs={{0,1},{1,2},{2,3},{3,4},{4,5},{5,6},{6,7},{7,8},{8,9},{9,10},{10,1... | collective-permute-start | bytes 98312 | tf_op jit(solution)/shard_map/ppermute | solution.py:23
  48.1 7.4 %copy-start.4 = (f32[512,128]{1,0:T(8,128)}, f32[512,128]{1,0:T(8,128)S(1)}, u32[]{:S(2)}) copy-start(f32[512,128]{1,0:T(8,128)S(1)} %get-tuple-element.63) | copy-start | bytes 786436
  48.1 6.0 %collective-permute-start.5 = (bf16[128,128]{1,0:T(8,128)(2,1)S(1)}, bf16[128,128]{1,0:T(8,128)(2,1)S(1)}, u32[]{:S(2)}, u32[]{:S(2)}) collective-permute-start(bf16[128,128]{1,0:T(8,128)(2,1)S(1)} %get-tuple-element.45), channel_id=1, source_target_pairs={{1,0},{2,1},{3,2},{4,3},{5,4},{6,5},{7,6},{8,7},{9,8},{10,9},{11,1... | collective-permute-start | bytes 98312 | tf_op jit(solution)/shard_map/ppermute | solution.py:28
  49.4 5.7 %collective-permute-start.4 = (bf16[128,128]{1,0:T(8,128)(2,1)S(1)}, bf16[128,128]{1,0:T(8,128)(2,1)S(1)}, u32[]{:S(2)}, u32[]{:S(2)}) collective-permute-start(bf16[128,128]{1,0:T(8,128)(2,1)S(1)} %get-tuple-element.44), channel_id=1, source_target_pairs={{0,1},{1,2},{2,3},{3,4},{4,5},{5,6},{6,7},{7,8},{8,9},{9,10},{10,1... | collective-permute-start | bytes 98312 | tf_op jit(solution)/shard_map/ppermute | solution.py:23
  54.1 1.6 %copy-start.14 = (f32[256,1024]{1,0:T(8,128)S(1)}, f32[256,1024]{1,0:T(8,128)}, u32[]{:S(2)}) copy-start(f32[256,1024]{1,0:T(8,128)} %get-tuple-element.59) | copy-start | bytes 3145732
  54.1 1.4 copy-start.9
  55.1 0.6 copy-start.10
  58.8 5.9 %collective-permute-start.6 = (bf16[512,640]{1,0:T(8,128)(2,1)}, bf16[512,640]{1,0:T(8,128)(2,1)S(1)}, u32[]{:S(2)}, u32[]{:S(2)}) collective-permute-start(bf16[512,640]{1,0:T(8,128)(2,1)} %dynamic-slice_bitcast_fusion), channel_id=1, source_target_pairs={{0,32},{32,0},{64,96},{96,64},{128,160},{160,128},{192,224},{224,1... | collective-permute-start | bytes 1966088 | tf_op jit(solution)/shard_map/ppermute | solution.py:18
  64.7 1.0 copy-start.1
  112.6 25.0 %all-to-all-start.2 = ((bf16[16,16,640]{2,1,0:T(8,128)(2,1)}), bf16[16,16,640]{2,1,0:T(8,128)(2,1)S(1)}, u32[]{:S(2)}, u32[]{:S(2)}) async-start(bf16[16,16,640]{2,1,0:T(8,128)(2,1)} %broadcast_in_dim.379), calls=%async_computation.2 | async-start | bytes 655360 | tf_op jit(solution)/shard_map/all_to_all | solution.py:116

commit v2 on v1

--- a/solution.py
+++ b/solution.py
@@ -1,8 +1,11 @@
+import functools
 import math
 
 import jax
 import jax.numpy as jnp
 from jax import lax
+from jax.experimental import pallas as pl
+from jax.experimental.pallas import tpu as pltpu
 from jax.sharding import PartitionSpec as P
 
 BF = jnp.bfloat16
@@ -39,6 +42,95 @@
             block = jnp.where(hit[:, k, None, None], tile_vals[:, k], block)
         columns.append(block.reshape(block_rows * blk, blk))
     return jnp.concatenate(columns, axis=1)
+
+
+def whole(kernel, outs, scratch=(), flops=0):
+    return pl.pallas_call(
+        kernel,
+        out_shape=[jax.ShapeDtypeStruct(shape, dtype) for shape, dtype in outs],
+        scratch_shapes=list(scratch),
+        compiler_params=pltpu.CompilerParams(vmem_limit_bytes=40 * 1024 * 1024),
+        cost_estimate=pl.CostEstimate(flops=flops, bytes_accessed=4_000_000, transcendentals=0),
+    )
+
+
+def forward_kernel(adj, feats, w_first, stale, w_second, agg_t, hidden, slope, proj):
+    width = feats.shape[1]
+    hid = w_first.shape[1]
+    step = min(256, hid)
+    m = adj[:, :width]
+    agg = dot(m, feats[...], 1, 1).astype(BF)
+    agg_t[...] = dot(feats[...], m, 1, 1).astype(BF)
+    total = jnp.zeros(proj.shape, F32)
+    for at in range(0, hid, step):
+        cols = slice(at, at + step)
+        a = dot(agg, w_first[:, cols], 1, 0) + stale[:, cols]
+        s = jax.nn.sigmoid(a)
+        h = (a * s).astype(BF)
+        hidden[:, cols] = h
+        slope[:, cols] = s * (1.0 + a * (1.0 - s))
+        total += dot(h, w_second[cols, :], 1, 0)
+    proj[...] = total.astype(BF)
+
+
+def middle_kernel(hid, adj, up, own, down, stale, mark, logits, inner, rim_up, rim_down):
+    blk = up.shape[0]
+    size = own.shape[0]
+    reach = size + 2 * blk
+    agg = dot(adj[:, :blk], up[...], 1, 0)
+    agg += dot(adj[:, blk : blk + size], own[...], 1, 0)
+    agg += dot(adj[:, blk + size : reach], down[...], 1, 0)
+    agg += stale[:, hid:]
+    logits[...] = agg.astype(BF)
+    e = jnp.exp(agg - jnp.max(agg, axis=1, keepdims=True))
+    grad = (e / jnp.sum(e, axis=1, keepdims=True) - mark[...]).astype(BF)
+    spread = dot(adj[:, :reach], grad, 0, 0)
+    inner[...] = spread[blk : blk + size]
+    rim_up[...] = spread[:blk].astype(BF)
+    rim_down[...] = spread[blk + size :].astype(BF)
+
+
+def backward_kernel(scale, core, inner, up, down, hidden, w_second, slope, agg_t, send, keep, grad_agg, second):
+    blk = up.shape[0]
+    size = inner.shape[0]
+    hid = slope.shape[1]
+    step = min(256, hid)
+    half = hid // 2
+    other = 1 - core[0]
+    upper = inner[:blk] + up[...].astype(F32)
+    lower = inner[size - blk :] + down[...].astype(F32)
+    if size > 2 * blk:
+        parts = [upper, inner[blk : size - blk], lower]
+    else:
+        parts = [upper, lower]
+    grad_p2 = jnp.concatenate(parts, axis=0).astype(BF)
+    for at in range(0, hid, step):
+        cols = slice(at, at + step)
+        grad_agg[:, cols] = (dot(grad_p2, w_second[cols, :], 1, 1) * slope[:, cols]).astype(BF)
+    second[...] = (dot(hidden[...], grad_p2, 0, 0) * scale).reshape(second.shape)
+    rows = second.shape[0] * second.shape[2]
+    send[:, half:] = second[:, other].reshape(rows, second.shape[3]).astype(BF)
+    keep[:, half:] = second[:, core[0]].reshape(rows, second.shape[3])
+    for mine, out in ((other, send), (core[0], keep)):
+        g = grad_agg[:, pl.ds(pl.multiple_of(mine * half, half), half)]
+        out[:, :half] = (dot(agg_t[...], g, 1, 0) * scale).astype(out.dtype)
+
+
+def feature_kernel(grad_agg, w_first, adj, out):
+    width = out.shape[1]
+    back = dot(w_first[...], grad_agg[...], 1, 1).astype(BF)
+    out[...] = dot(back, adj[:, :width], 1, 0).astype(BF)
+
+
+def whole_core(kernel, outs, blocks, scratch, flops):
+    return pl.pallas_call(
+        kernel,
+        out_shape=[jax.ShapeDtypeStruct(shape, dtype) for shape, dtype in outs],
+        in_specs=[pl.BlockSpec(memory_space=pltpu.SMEM)] + [pl.BlockSpec(memory_space=pltpu.VMEM)] * (blocks + 1),
+        scratch_shapes=scratch,
+        compiler_params=pltpu.CompilerParams(vmem_limit_bytes=40 * 1024 * 1024),
+        cost_estimate=pl.CostEstimate(flops=flops, bytes_accessed=4_000_000, transcendentals=0),
+    )
 
 
 def local(feats_t, w_first, w_second, stale_rows, tile_vals, tile_src, tile_count, labels):
@@ -59,58 +151,48 @@
     left = jnp.concatenate([edge, parts[:, :-1, own - blk :]], axis=1)
     right = jnp.concatenate([parts[:, 1:, :blk], edge], axis=1)
     wide = jnp.concatenate([left, parts, right], axis=2)
+    wide, tile_vals, stale_rows = lax.optimization_barrier((wide, tile_vals, stale_rows))
     feats = lax.all_to_all(wide, "dom", split_axis=1, concat_axis=0, tiled=True).reshape(feat_all, reach)
 
+    adj = adjacency(tile_vals, tile_src, tile_count, reach // blk + 2)
+    stale_rows, adj = lax.optimization_barrier((stale_rows, adj))
     before = from_previous(stale_rows, "grp")
     after = from_next(stale_rows, "grp")
-    adj_all = adjacency(tile_vals, tile_src, tile_count, reach // blk + 2)
-    adj = adj_all[:, :reach]
-    stale_part = dot(adj_all[:, reach:], jnp.concatenate([before, after], axis=0), 1, 0)
-
-    feats_agg = dot(adj, feats, 1, 1).astype(BF)
-    agg_first = dot(feats_agg, w_first, 1, 0) + stale_part[:, :hid]
-    squash = jax.nn.sigmoid(agg_first)
-    hidden = (agg_first * squash).astype(BF)
-    proj_second = dot(hidden, w_second, 1, 0).astype(BF)
-
-    window = jnp.concatenate(
-        [from_previous(proj_second[own - blk :], "dom"), proj_second, from_next(proj_second[:blk], "dom")], axis=0
-    )
-    agg_second = dot(adj, window, 1, 0) + stale_part[:, hid:]
-    logits = agg_second.astype(BF)
-    top_value = jnp.max(agg_second, axis=1, keepdims=True)
-    exp_logits = jnp.exp(agg_second - top_value)
-    predicted = exp_logits / jnp.sum(exp_logits, axis=1, keepdims=True)
+    stale_part = dot(adj[:, reach:], jnp.concatenate([before, after], axis=0), 1, 0)
     mark = (labels[:, None] == jnp.arange(classes, dtype=jnp.int32)[None, :]).astype(F32)
-    grad_logits = (predicted - mark).astype(BF)
-
-    spread_second = dot(adj, grad_logits, 0, 0)
-    to_first = from_previous(spread_second[reach - blk :].astype(BF), "dom").astype(F32)
-    to_last = from_next(spread_second[:blk].astype(BF), "dom").astype(F32)
-    inner = jnp.zeros((own - blk, classes), F32)
-    grad_p2 = (
-        spread_second[blk : reach - blk]
-        + jnp.concatenate([to_first, inner], axis=0)
-        + jnp.concatenate([inner, to_last], axis=0)
-    ).astype(BF)
-
-    grad_hidden = dot(grad_p2, w_second, 1, 1)
-    grad_agg = (grad_hidden * squash * (1.0 + agg_first * (1.0 - squash))).astype(BF)
-    first_term = (dot(feats_agg, grad_agg, 0, 0) * scale).astype(BF)
-    second_term = (dot(hidden, grad_p2, 0, 0) * scale).astype(BF)
-    first_pair = jnp.stack([first_term[:, :half], first_term[:, half:]])
-    second_pair = second_term.reshape(n_dom, 2, feat_rows, classes).transpose(1, 0, 2, 3).reshape(2, feat_all, classes)
-    both = jnp.concatenate([first_pair, second_pair], axis=2)
-    keep = lax.dynamic_index_in_dim(both, core, 0, keepdims=False)
-    send = lax.dynamic_index_in_dim(both, 1 - core, 0, keepdims=False)
-    summed = (keep.astype(F32) + swapped(send, "grp").astype(F32)).astype(BF)
-
-    back = dot(grad_agg, w_first, 1, 1).astype(BF)
-    grad_wide = dot(back, adj, 0, 0).astype(BF)
+
+    agg_t, hidden, slope, proj_second = whole(
+        forward_kernel,
+        [((feat_all, own), BF), ((own, hid), BF), ((own, hid), F32), ((own, classes), BF)],
+        flops=2 * own * (2 * feat_all * reach + feat_all * hid + hid * classes),
+    )(adj, feats, w_first, stale_part, w_second)
+
+    up = from_previous(proj_second[own - blk :], "dom")
+    down = from_next(proj_second[:blk], "dom")
+    logits, inner, rim_up, rim_down = whole(
+        functools.partial(middle_kernel, hid),
+        [((own, classes), BF), ((own, classes), F32), ((blk, classes), BF), ((blk, classes), BF)],
+        flops=4 * own * reach * classes,
+    )(adj, up, proj_second, down, stale_part, mark)
+
+    to_first = from_previous(rim_down, "dom")
+    to_last = from_next(rim_up, "dom")
+    width = half + classes
+    send, keep, grad_agg = whole_core(
+        functools.partial(backward_kernel, scale),
+        [((feat_all, width), BF), ((feat_all, width), F32), ((own, hid), BF)],
+        6,
+        scratch=[pltpu.VMEM((n_dom, 2, feat_rows, classes), F32)],
+        flops=2 * own * (hid * classes * 2 + feat_all * hid),
+    )(core[None], inner, to_first, to_last, hidden, w_second, slope, agg_t)
+    summed = (keep + swapped(send, "grp").astype(F32)).astype(BF)
+
+    (grad_wide,) = whole(
+        feature_kernel, [((feat_all, reach), BF)], flops=2 * own * (hid * feat_all + reach * feat_all)
+    )(grad_agg, w_first, adj)
     sent = jnp.concatenate([summed, grad_wide], axis=1)
     got = lax.all_to_all(sent, "dom", split_axis=0, concat_axis=0, tiled=True).reshape(n_dom, feat_rows, -1)
 
-    width = half + classes
     band = jnp.sum(got[:, :, :width].astype(F32), axis=0).astype(BF)
     copies = jnp.broadcast_to(band[None], (n_grp, feat_rows, width))
     bands = lax.all_to_all(copies, "grp", split_axis=0, concat_axis=0, tiled=True)

time: 140 us -> 135 us (0.964)
  matrix products: 8.8 us -> 0.35 us
  starting transfers between devices: 43.7 us -> 48.4 us
  waiting for transfers between devices: 26.3 us -> 21.9 us
  Pallas kernels: 0 us -> 4.15 us
    all_to_all x1, waiting for transfers between devices: 12.2 us -> 1.06 us  [local(): lax.all_to_all(wide, 'dom', split_axis=1, concat_axis=0, tiled=True)]
    dot_general x10 -> x1, matrix products: 8.8 us -> 0.35 us  [dot(): lax.dot_general(a, b, (((ca,), (cb,)), ((), ())), preferred_element_type=...]
    ppermute x3, waiting for transfers between devices: 0.01 us -> 6.1 us  [from_next(): return lax.ppermute(x, axis, [(i + 1, i) for i in range(count - 1)])]
    ppermute x3, starting transfers between devices: 11.5 us -> 5.58 us  [from_next(): return lax.ppermute(x, axis, [(i + 1, i) for i in range(count - 1)])]
    all_to_all x1, starting transfers between devices: 6.27 us -> 10.5 us  [local(): lax.all_to_all(wide, 'dom', split_axis=1, concat_axis=0, tiled=True)]
    pallas_call x0 -> x4, Pallas kernels: none -> 4.15 us  [the longest x1 1.38 us: local(): whole(forward_kernel, [((feat_all, own), BF), ((own, hid), BF), ((own, hi...]
    ppermute x1, starting transfers between devices: 3.38 us -> 6.87 us  [swapped(): return lax.ppermute(x, axis, [(i, i ^ 1) for i in range(count)])]
    all_to_all x1, starting transfers between devices: 11.9 us -> 13.6 us  [local(): lax.all_to_all(copies, 'grp', split_axis=0, concat_axis=0, tiled=True)]
  transfers between devices with their start and end apart: 9 -> 9, of which waited for: 4 -> 7; matrix products, arithmetic and copies ran while one was open for 8% -> 4% of each run, Pallas kernels for 0% -> 1%
where the time goes in v2:
time: 135 us; the launch traced here: 134 us
  starting transfers between devices  48.4 us (36%)
  blocking collectives  45.8 us (34%)
  waiting for transfers between devices  21.9 us (16%)
  local copies, waits for them, and re-layouts  9.17 us (7%)
  Pallas kernels  4.15 us (3%)
  other arithmetic  3.62 us (3%)
    all_to_all x1, blocking collectives, local(): lax.all_to_all(sent, 'dom', split_axis=0, concat_axis=0, tiled=True)  45.8 us
    all_to_all x1, starting transfers between devices, local(): lax.all_to_all(copies, 'grp', split_axis=0, concat_axis=0, tiled=True)  13.6 us
    all_to_all x1, waiting for transfers between devices, local(): lax.all_to_all(copies, 'grp', split_axis=0, concat_axis=0, tiled=True)  12.1 us
    ppermute x3, starting transfers between devices, from_previous(): return lax.ppermute(x, axis, [(i, i + 1) for i in range(count - 1)])  11.8 us
    all_to_all x1, starting transfers between devices, local(): lax.all_to_all(wide, 'dom', split_axis=1, concat_axis=0, tiled=True)  10.5 us
    ppermute x1, starting transfers between devices, swapped(): return lax.ppermute(x, axis, [(i, i ^ 1) for i in range(count)])  6.87 us
    ppermute x3, waiting for transfers between devices, from_next(): return lax.ppermute(x, axis, [(i + 1, i) for i in range(count - 1)])  6.1 us
    ppermute x3, starting transfers between devices, from_next(): return lax.ppermute(x, axis, [(i + 1, i) for i in range(count - 1)])  5.58 us
  transfers between devices with their start and end apart: 9, of which 7 were waited for; matrix products, arithmetic and copies ran while one was open for 4% of the time, Pallas kernels for 1%

profile of v2, /device:TPU:1, one launch (start us, length us, event | category | flops | bytes accessed | tf_op | source)
XLA Modules:
  0.0 134.3 jit_solution(5645257500046535072)
XLA Ops:
  0.6 1.0 copy.23
  1.7 0.9 fusion.6
  2.6 10.5 %all-to-all-start = ((bf16[16,32,512]{2,0,1:T(8,128)(2,1)}), bf16[16,32,512]{2,0,1:T(8,128)(2,1)S(1)}, u32[]{:S(2)}, u32[]{:S(2)}) async-start(bf16[16,32,512]{2,0,1:T(8,128)(2,1)} %fusion.6), calls=%async_computation | async-start | bytes 1048576 | tf_op jit(solution)/shard_map/all_to_all | solution.py:155
  13.1 0.1 compare_and_fusion
  13.2 0.3 slice_reduce_fusion.4
  13.5 0.1 broadcast_bitcast_fusion.3
  13.5 0.1 broadcast_bitcast_fusion
  13.6 0.1 broadcast_bitcast_fusion.1
  13.7 0.1 broadcast_bitcast_fusion.2
  13.8 0.1 broadcast_bitcast_fusion.6
  13.8 0.1 broadcast_bitcast_fusion.5
  13.9 0.1 broadcast_bitcast_fusion.4
  14.0 0.1 broadcast_bitcast_fusion.7
  14.0 0.3 slice_reduce_fusion.12
  14.3 0.1 broadcast_bitcast_fusion.11
  14.4 0.1 broadcast_bitcast_fusion.8
  14.5 0.1 broadcast_bitcast_fusion.9
  14.6 0.1 broadcast_bitcast_fusion.10
  14.6 0.1 broadcast_bitcast_fusion.14
  14.7 0.1 broadcast_bitcast_fusion.13
  14.8 0.1 broadcast_bitcast_fusion.12
  14.9 0.1 broadcast_bitcast_fusion.15
  14.9 0.3 slice_reduce_fusion.20
  15.2 0.1 broadcast_bitcast_fusion.19
  15.3 0.1 broadcast_bitcast_fusion.16
  15.4 0.1 broadcast_bitcast_fusion.17
  15.4 0.1 broadcast_bitcast_fusion.18
  15.5 0.1 broadcast_bitcast_fusion.22
  15.8 0.7 fusion.26
  16.5 0.7 fusion.29
  17.4 3.0 %collective-permute-start.1 = (bf16[128,1152]{1,0:T(8,128)(2,1)S(1)}, bf16[128,1152]{1,0:T(8,128)(2,1)S(1)}, u32[]{:S(2)}, u32[]{:S(2)}) collective-permute-start(bf16[128,1152]{1,0:T(8,128)(2,1)S(1)} %copy-done.12), channel_id=1, source_target_pairs={{32,0},{64,32},{96,64},{128,96},{160,128},{192,160},{224,192},{256... | collective-permute-start | bytes 884744 | tf_op jit(solution)/shard_map/ppermute | solution.py:31
  20.4 3.9 %collective-permute-start = (bf16[128,1152]{1,0:T(8,128)(2,1)S(1)}, bf16[128,1152]{1,0:T(8,128)(2,1)S(1)}, u32[]{:S(2)}, u32[]{:S(2)}) collective-permute-start(bf16[128,1152]{1,0:T(8,128)(2,1)S(1)} %copy-done.12), channel_id=1, source_target_pairs={{0,32},{32,64},{64,96},{96,128},{128,160},{160,192},{192,224},{224... | collective-permute-start | bytes 884744 | tf_op jit(solution)/shard_map/ppermute | solution.py:26
  24.3 2.8 %collective-permute-done.1 = bf16[128,1152]{1,0:T(8,128)(2,1)S(1)} collective-permute-done((bf16[128,1152]{1,0:T(8,128)(2,1)S(1)}, bf16[128,1152]{1,0:T(8,128)(2,1)S(1)}, u32[]{:S(2)}, u32[]{:S(2)}) %collective-permute-start.1) | collective-permute-done | bytes 294944 | tf_op jit(solution)/shard_map/ppermute | solution.py:31
  27.0 0.9 collective-permute-done
  27.9 0.3 fusion.2.stale
  28.3 1.1 all-to-all-done
  29.3 1.4 %shard_map.111 = (bf16[512,256]{1,0:T(8,128)(2,1)S(1)}, bf16[256,1024]{1,0:T(8,128)(2,1)S(1)}, f32[256,1024]{1,0:T(8,128)S(1)}, bf16[256,128]{1,0:T(8,128)(2,1)S(1)}) custom-call(bf16[256,768]{1,0:T(8,128)(2,1)S(1)} %constant_dynamic-update-slice_fusion.adj, bf16[512,512]{1,0:T(8,128)(2,1)S(1)} %bitcast.134, bf16[512,1024]{1,0:T(8,128)(2,1)S(1)} %copy-done, ...), custom_call_target="tpu_custom_call" | custom-call | flops 603979776 | bytes 4000000 | tf_op jit(solution)/shard_map/pallas_call | solution.py:164
  30.8 1.3 collective-permute-start.3
  32.1 4.0 %collective-permute-start.2 = (bf16[128,128]{1,0:T(8,128)(2,1)S(1)}, bf16[128,128]{1,0:T(8,128)(2,1)S(1)}, u32[]{:S(2)}, u32[]{:S(2)}) collective-permute-start(bf16[128,128]{1,0:T(8,128)(2,1)S(1)} %get-tuple-element.77), channel_id=1, source_target_pairs={{0,1},{1,2},{2,3},{3,4},{4,5},{5,6},{6,7},{7,8},{8,9},{9,10},{10,1... | collective-permute-start | bytes 98312 | tf_op jit(solution)/shard_map/ppermute | solution.py:26
  36.1 0.1 fusion.11.mark
  36.2 0.9 collective-permute-done.2.up
  37.1 1.0 shard_map.112
  38.1 3.9 %collective-permute-start.4 = (bf16[128,128]{1,0:T(8,128)(2,1)S(1)}, bf16[128,128]{1,0:T(8,128)(2,1)S(1)}, u32[]{:S(2)}, u32[]{:S(2)}) collective-permute-start(bf16[128,128]{1,0:T(8,128)(2,1)S(1)} %get-tuple-element.28), channel_id=1, source_target_pairs={{0,1},{1,2},{2,3},{3,4},{4,5},{5,6},{6,7},{7,8},{8,9},{9,10},{10,1... | collective-permute-start | bytes 98312 | tf_op jit(solution)/shard_map/ppermute | solution.py:26
  42.1 1.3 collective-permute-start.5
  43.4 3.3 %collective-permute-done.5.down = bf16[128,128]{1,0:T(8,128)(2,1)S(1)} collective-permute-done((bf16[128,128]{1,0:T(8,128)(2,1)S(1)}, bf16[128,128]{1,0:T(8,128)(2,1)S(1)}, u32[]{:S(2)}, u32[]{:S(2)}) %collective-permute-start.5) | collective-permute-done | bytes 32800 | tf_op jit(solution)/shard_map/ppermute | solution.py:31
  46.7 1.2 copy-done.2
  47.9 1.0 copy-done.5
  49.0 0.9 copy-done.7
  49.9 0.9 shard_map.113
  50.8 6.9 %collective-permute-start.6 = (bf16[512,640]{1,0:T(8,128)(2,1)S(1)}, bf16[512,640]{1,0:T(8,128)(2,1)S(1)}, u32[]{:S(2)}, u32[]{:S(2)}) collective-permute-start(bf16[512,640]{1,0:T(8,128)(2,1)S(1)} %get-tuple-element.34), channel_id=1, source_target_pairs={{0,32},{32,0},{64,96},{96,64},{128,160},{160,128},{192,224},{224,1... | collective-permute-start | bytes 1966088 | tf_op jit(solution)/shard_map/ppermute | solution.py:21
  57.7 0.8 shard_map.114
  58.6 0.8 collective-permute-done.6
  59.4 0.2 add_convert_fusion
  59.6 0.1 pad_maximum_fusion
  59.7 45.8 %all_to_all.29 = bf16[32,16,1152]{2,1,0:T(8,128)(2,1)S(1)} all-to-all(bf16[32,16,1152]{2,1,0:T(8,128)(2,1)S(1)} %bitcast.135), channel_id=1, replica_groups=mesh['grp'=16,'dom'=32] {'dom'}, dimensions={0} | all-to-all | bytes 2359296 | tf_op jit(solution)/shard_map/all_to_all | solution.py:194
  105.5 0.1 slice_reduce_fusion
  105.6 0.7 broadcast_in_dim.380
  106.3 13.6 %all-to-all-start.2 = ((bf16[16,16,640]{2,1,0:T(8,128)(2,1)}), bf16[16,16,640]{2,1,0:T(8,128)(2,1)S(1)}, u32[]{:S(2)}, u32[]{:S(2)}) async-start(bf16[16,16,640]{2,1,0:T(8,128)(2,1)} %broadcast_in_dim.380), calls=%async_computation.2 | async-start | bytes 655360 | tf_op jit(solution)/shard_map/all_to_all | solution.py:198
  119.9 0.1 slice_convert_fusion
  120.1 0.1 fusion.9
  120.2 0.7 copy.21
  120.9 12.1 %all-to-all-done.2 = bf16[16,16,640]{2,1,0:T(8,128)(2,1)S(1)} async-done(((bf16[16,16,640]{2,1,0:T(8,128)(2,1)}), bf16[16,16,640]{2,1,0:T(8,128)(2,1)S(1)}, u32[]{:S(2)}, u32[]{:S(2)}) %all-to-all-start.2) | async-done | bytes 327712 | tf_op jit(solution)/shard_map/all_to_all | solution.py:198
  133.0 0.6 slice.193
  133.6 0.6 pad_maximum_fusion.1
  (40 shorter events, 0.6 us)
Async XLA Ops:
  1.6 11.5 %copy-start.10 = (s32[2,4]{1,0:T(2,128)S(1)}, s32[2,4]{1,0:T(2,128)}, u32[]{:S(2)}) copy-start(s32[2,4]{1,0:T(2,128)} %param.13) | copy-start | bytes 100
  1.6 11.5 %copy-start.11 = (s32[2]{0:T(128)S(1)}, s32[2]{0:T(128)}, u32[]{:S(2)}) copy-start(s32[2]{0:T(128)} %param.14) | copy-start | bytes 28
  1.7 14.1 %copy-start.8 = (bf16[2,4,128,128]{3,2,1,0:T(8,128)(2,1)S(1)}, bf16[2,4,128,128]{3,2,1,0:T(8,128)(2,1)}, u32[]{:S(2)}) copy-start(bf16[2,4,128,128]{3,2,1,0:T(8,128)(2,1)} %param.12) | copy-start | bytes 786436
  2.6 26.8 %all-to-all-start = ((bf16[16,32,512]{2,0,1:T(8,128)(2,1)}), bf16[16,32,512]{2,0,1:T(8,128)(2,1)S(1)}, u32[]{:S(2)}, u32[]{:S(2)}) async-start(bf16[16,32,512]{2,0,1:T(8,128)(2,1)} %fusion.6), calls=%async_computation | async-start | bytes 1048576 | tf_op jit(solution)/shard_map/all_to_all | solution.py:155
  13.8 3.6 %copy-start.12 = (bf16[128,1152]{1,0:T(8,128)(2,1)S(1)}, bf16[128,1152]{1,0:T(8,128)(2,1)}, u32[]{:S(2)}) copy-start(bf16[128,1152]{1,0:T(8,128)(2,1)} %param.11) | copy-start | bytes 884740
  17.3 12.1 %copy-start = (bf16[512,1024]{1,0:T(8,128)(2,1)S(1)}, bf16[512,1024]{1,0:T(8,128)(2,1)}, u32[]{:S(2)}) copy-start(bf16[512,1024]{1,0:T(8,128)(2,1)} %w_first.3) | copy-start | bytes 3145732
  17.3 12.1 %copy-start.3 = (bf16[1024,128]{1,0:T(8,128)(2,1)S(1)}, bf16[1024,128]{1,0:T(8,128)(2,1)}, u32[]{:S(2)}) copy-start(bf16[1024,128]{1,0:T(8,128)(2,1)} %w_second.3) | copy-start | bytes 786436
  17.4 9.7 %collective-permute-start.1 = (bf16[128,1152]{1,0:T(8,128)(2,1)S(1)}, bf16[128,1152]{1,0:T(8,128)(2,1)S(1)}, u32[]{:S(2)}, u32[]{:S(2)}) collective-permute-start(bf16[128,1152]{1,0:T(8,128)(2,1)S(1)} %copy-done.12), channel_id=1, source_target_pairs={{32,0},{64,32},{96,64},{128,96},{160,128},{192,160},{224,192},{256... | collective-permute-start | bytes 884744 | tf_op jit(solution)/shard_map/ppermute | solution.py:31
  20.4 7.6 %collective-permute-start = (bf16[128,1152]{1,0:T(8,128)(2,1)S(1)}, bf16[128,1152]{1,0:T(8,128)(2,1)S(1)}, u32[]{:S(2)}, u32[]{:S(2)}) collective-permute-start(bf16[128,1152]{1,0:T(8,128)(2,1)S(1)} %copy-done.12), channel_id=1, source_target_pairs={{0,32},{32,64},{64,96},{96,128},{128,160},{160,192},{192,224},{224... | collective-permute-start | bytes 884744 | tf_op jit(solution)/shard_map/ppermute | solution.py:26
  29.3 6.7 %copy-start.9 = (s32[256]{0:T(256)S(1)}, s32[256]{0:T(256)}, u32[]{:S(2)}) copy-start(s32[256]{0:T(256)} %param.15) | copy-start | bytes 3076
  30.7 7.4 %copy-start.1 = (f32[256,1024]{1,0:T(8,128)}, f32[256,1024]{1,0:T(8,128)S(1)}, u32[]{:S(2)}) copy-start(f32[256,1024]{1,0:T(8,128)S(1)} %get-tuple-element.31.slope) | copy-start | bytes 3145732
  30.8 7.4 %copy-start.4 = (bf16[256,1024]{1,0:T(8,128)(2,1)}, bf16[256,1024]{1,0:T(8,128)(2,1)S(1)}, u32[]{:S(2)}) copy-start(bf16[256,1024]{1,0:T(8,128)(2,1)S(1)} %get-tuple-element.30.hidden) | copy-start | bytes 1572868
  30.8 11.3 %copy-start.6 = (bf16[512,256]{1,0:T(8,128)(2,1)}, bf16[512,256]{1,0:T(8,128)(2,1)S(1)}, u32[]{:S(2)}) copy-start(bf16[512,256]{1,0:T(8,128)(2,1)S(1)} %get-tuple-element.32.agg_t) | copy-start | bytes 786436
  30.8 5.4 %collective-permute-start.3 = (bf16[128,128]{1,0:T(8,128)(2,1)S(1)}, bf16[128,128]{1,0:T(8,128)(2,1)S(1)}, u32[]{:S(2)}, u32[]{:S(2)}) collective-permute-start(bf16[128,128]{1,0:T(8,128)(2,1)S(1)} %get-tuple-element.76), channel_id=1, source_target_pairs={{1,0},{2,1},{3,2},{4,3},{5,4},{6,5},{7,6},{8,7},{9,8},{10,9},{11,1... | collective-permute-start | bytes 98312 | tf_op jit(solution)/shard_map/ppermute | solution.py:31
  32.1 5.0 %collective-permute-start.2 = (bf16[128,128]{1,0:T(8,128)(2,1)S(1)}, bf16[128,128]{1,0:T(8,128)(2,1)S(1)}, u32[]{:S(2)}, u32[]{:S(2)}) collective-permute-start(bf16[128,128]{1,0:T(8,128)(2,1)S(1)} %get-tuple-element.77), channel_id=1, source_target_pairs={{0,1},{1,2},{2,3},{3,4},{4,5},{5,6},{6,7},{7,8},{8,9},{9,10},{10,1... | collective-permute-start | bytes 98312 | tf_op jit(solution)/shard_map/ppermute | solution.py:26
  38.1 5.3 %collective-permute-start.4 = (bf16[128,128]{1,0:T(8,128)(2,1)S(1)}, bf16[128,128]{1,0:T(8,128)(2,1)S(1)}, u32[]{:S(2)}, u32[]{:S(2)}) collective-permute-start(bf16[128,128]{1,0:T(8,128)(2,1)S(1)} %get-tuple-element.28), channel_id=1, source_target_pairs={{0,1},{1,2},{2,3},{3,4},{4,5},{5,6},{6,7},{7,8},{8,9},{9,10},{10,1... | collective-permute-start | bytes 98312 | tf_op jit(solution)/shard_map/ppermute | solution.py:26
  42.1 4.7 %collective-permute-start.5 = (bf16[128,128]{1,0:T(8,128)(2,1)S(1)}, bf16[128,128]{1,0:T(8,128)(2,1)S(1)}, u32[]{:S(2)}, u32[]{:S(2)}) collective-permute-start(bf16[128,128]{1,0:T(8,128)(2,1)S(1)} %get-tuple-element.29), channel_id=1, source_target_pairs={{1,0},{2,1},{3,2},{4,3},{5,4},{6,5},{7,6},{8,7},{9,8},{10,9},{11,1... | collective-permute-start | bytes 98312 | tf_op jit(solution)/shard_map/ppermute | solution.py:31
  46.7 1.2 copy-start.2
  47.9 1.0 copy-start.5
  49.0 0.9 copy-start.7
  50.8 8.6 %collective-permute-start.6 = (bf16[512,640]{1,0:T(8,128)(2,1)S(1)}, bf16[512,640]{1,0:T(8,128)(2,1)S(1)}, u32[]{:S(2)}, u32[]{:S(2)}) collective-permute-start(bf16[512,640]{1,0:T(8,128)(2,1)S(1)} %get-tuple-element.34), channel_id=1, source_target_pairs={{0,32},{32,0},{64,96},{96,64},{128,160},{160,128},{192,224},{224,1... | collective-permute-start | bytes 1966088 | tf_op jit(solution)/shard_map/ppermute | solution.py:21
  106.3 26.7 %all-to-all-start.2 = ((bf16[16,16,640]{2,1,0:T(8,128)(2,1)}), bf16[16,16,640]{2,1,0:T(8,128)(2,1)S(1)}, u32[]{:S(2)}, u32[]{:S(2)}) async-start(bf16[16,16,640]{2,1,0:T(8,128)(2,1)} %broadcast_in_dim.380), calls=%async_computation.2 | async-start | bytes 655360 | tf_op jit(solution)/shard_map/all_to_all | solution.py:198

commit v3 on v2

--- a/solution.py
+++ b/solution.py
@@ -31,27 +31,49 @@
     return lax.ppermute(x, axis, [(i + 1, i) for i in range(count - 1)])
 
 
-def adjacency(tile_vals, tile_src, tile_count, window_blocks):
-    block_rows, slots, blk, _ = tile_vals.shape
-    live = jnp.arange(slots, dtype=jnp.int32)[None, :] < tile_count[:, None]
-    columns = []
-    for t in range(window_blocks):
-        hit = (tile_src == t) & live
-        block = jnp.zeros((block_rows, blk, blk), BF)
-        for k in range(slots):
-            block = jnp.where(hit[:, k, None, None], tile_vals[:, k], block)
-        columns.append(block.reshape(block_rows * blk, blk))
-    return jnp.concatenate(columns, axis=1)
-
-
 def whole(kernel, outs, scratch=(), flops=0):
     return pl.pallas_call(
         kernel,
         out_shape=[jax.ShapeDtypeStruct(shape, dtype) for shape, dtype in outs],
         scratch_shapes=list(scratch),
-        compiler_params=pltpu.CompilerParams(vmem_limit_bytes=40 * 1024 * 1024),
+        compiler_params=pltpu.CompilerParams(vmem_limit_bytes=16 * 1024 * 1024),
         cost_estimate=pl.CostEstimate(flops=flops, bytes_accessed=4_000_000, transcendentals=0),
     )
+
+
+def widen_kernel(feats, wide):
+    parts, rows, reach = wide.shape
+    own = feats.shape[1] // parts
+    blk = (reach - own) // 2
+    none = jnp.zeros((rows, blk), wide.dtype)
+    for d in range(parts):
+        first, last = d * own - blk, (d + 1) * own + blk
+        wide[d, :, blk : blk + own] = feats[:, d * own : (d + 1) * own]
+        wide[d, :, :blk] = feats[:, first : first + blk] if d > 0 else none
+        wide[d, :, blk + own :] = feats[:, last - blk : last] if d < parts - 1 else none
+
+
+def adjacency_kernel(src, count, tiles, adj):
+    block_rows, slots, blk, _ = tiles.shape
+    for r in range(block_rows):
+        live = count[r]
+        for t in range(adj.shape[1] // blk):
+            block = jnp.zeros((blk, blk), BF)
+            for k in range(slots):
+                hit = jnp.logical_and(src[r, k] == t, k < live)
+                block = jnp.where(hit, tiles[r, k], block)
+            adj[r * blk : (r + 1) * blk, t * blk : (t + 1) * blk] = block
+
+
+def total_kernel(bands, first, second):
+    cores, half = 2, first.shape[1] // 2
+    rows = first.shape[0]
+    for c in range(cores):
+        total = bands[c].astype(F32)
+        for z in range(1, bands.shape[0] // cores):
+            total += bands[z * cores + c].astype(F32)
+        first[:, c * half : (c + 1) * half] = total[:, :half]
+        second[c * rows : (c + 1) * rows, :] = total[:, half:]
 
 
 def forward_kernel(adj, feats, w_first, stale, w_second, agg_t, hidden, slope, proj):
@@ -122,13 +144,13 @@
     out[...] = dot(back, adj[:, :width], 1, 0).astype(BF)
 
 
-def whole_core(kernel, outs, blocks, scratch, flops):
+def whole_core(kernel, outs, blocks, scratch=(), flops=0, scalars=1):
     return pl.pallas_call(
         kernel,
         out_shape=[jax.ShapeDtypeStruct(shape, dtype) for shape, dtype in outs],
-        in_specs=[pl.BlockSpec(memory_space=pltpu.SMEM)] + [pl.BlockSpec(memory_space=pltpu.VMEM)] * (blocks + 1),
+        in_specs=[pl.BlockSpec(memory_space=pltpu.SMEM)] * scalars + [pl.BlockSpec(memory_space=pltpu.VMEM)] * blocks,
         scratch_shapes=scratch,
-        compiler_params=pltpu.CompilerParams(vmem_limit_bytes=40 * 1024 * 1024),
+        compiler_params=pltpu.CompilerParams(vmem_limit_bytes=16 * 1024 * 1024),
         cost_estimate=pl.CostEstimate(flops=flops, bytes_accessed=4_000_000, transcendentals=0),
     )
 
@@ -146,15 +168,13 @@
     half = hid // 2
     core = lax.axis_index("grp") % 2
 
-    parts = feats_t.reshape(feat_rows, n_dom, own)
-    edge = jnp.zeros((feat_rows, 1, blk), BF)
-    left = jnp.concatenate([edge, parts[:, :-1, own - blk :]], axis=1)
-    right = jnp.concatenate([parts[:, 1:, :blk], edge], axis=1)
-    wide = jnp.concatenate([left, parts, right], axis=2)
+    (wide,) = whole(widen_kernel, [((n_dom, feat_rows, reach), BF)])(feats_t)
     wide, tile_vals, stale_rows = lax.optimization_barrier((wide, tile_vals, stale_rows))
-    feats = lax.all_to_all(wide, "dom", split_axis=1, concat_axis=0, tiled=True).reshape(feat_all, reach)
-
-    adj = adjacency(tile_vals, tile_src, tile_count, reach // blk + 2)
+    feats = lax.all_to_all(wide, "dom", split_axis=0, concat_axis=0, tiled=True).reshape(feat_all, reach)
+
+    (adj,) = whole_core(adjacency_kernel, [((own, reach + 2 * blk), BF)], 1, scalars=2)(
+        tile_src, tile_count, tile_vals
+    )
     stale_rows, adj = lax.optimization_barrier((stale_rows, adj))
     before = from_previous(stale_rows, "grp")
     after = from_next(stale_rows, "grp")
@@ -181,7 +201,7 @@
     send, keep, grad_agg = whole_core(
         functools.partial(backward_kernel, scale),
         [((feat_all, width), BF), ((feat_all, width), F32), ((own, hid), BF)],
-        6,
+        7,
         scratch=[pltpu.VMEM((n_dom, 2, feat_rows, classes), F32)],
         flops=2 * own * (hid * classes * 2 + feat_all * hid),
     )(core[None], inner, to_first, to_last, hidden, w_second, slope, agg_t)
@@ -196,9 +216,9 @@
     band = jnp.sum(got[:, :, :width].astype(F32), axis=0).astype(BF)
     copies = jnp.broadcast_to(band[None], (n_grp, feat_rows, width))
     bands = lax.all_to_all(copies, "grp", split_axis=0, concat_axis=0, tiled=True)
-    total = jnp.sum(bands.reshape(n_grp // 2, 2, feat_rows, width).astype(F32), axis=0)
-    grad_first = jnp.concatenate([total[0, :, :half], total[1, :, :half]], axis=1)
-    grad_second = total[:, :, half:].reshape(2 * feat_rows, classes)
+    grad_first, grad_second = whole(
+        total_kernel, [((feat_rows, hid), F32), ((2 * feat_rows, classes), F32)]
+    )(bands)
 
     wide_back = got[:, :, width:].astype(F32)
     none = jnp.zeros((1, feat_rows, blk), F32)

time: 135 us -> 133 us (0.985)
  waiting for transfers between devices: 21.9 us -> 25.5 us
  local copies, waits for them, and re-layouts: 9.17 us -> 5.74 us
  other arithmetic: 3.62 us -> 0.67 us
  Pallas kernels: 4.15 us -> 6.38 us
  starting transfers between devices: 48.4 us -> 46.5 us
    all_to_all x1, waiting for transfers between devices: 1.06 us -> 4.73 us  [local(): lax.all_to_all(wide, 'dom', split_axis=0, concat_axis=0, tiled=True)]
    pallas_call x0 -> x3, Pallas kernels: none -> 2.24 us  [the longest x1 0.87 us: local(): wide, = whole(widen_kernel, [((n_dom, feat_rows, reach), BF)])(feats_t)]
    broadcast_in_dim x24 -> x0, local copies, waits for them, and re-layouts: 1.74 us -> none  [adjacency(): block = jnp.where(hit[:, k, None, None], tile_vals[:, k], block)]
    all_to_all x1, starting transfers between devices: 13.6 us -> 11.9 us  [local(): lax.all_to_all(copies, 'grp', split_axis=0, concat_axis=0, tiled=True)]
    slice x6 -> x0, local copies, waits for them, and re-layouts: 1.56 us -> none  [the longest x4 0.91 us: adjacency(): block = jnp.where(hit[:, k, None, None], tile_vals[:, k], block)]
    concatenate x2 -> x0, other arithmetic: 1.5 us -> none  [the longest x1 0.87 us: local(): wide = jnp.concatenate([left, parts, right], axis=2)]
    unnamed x31 -> x28, local copies, waits for them, and re-layouts: 3.36 us -> 4.2 us
  transfers between devices with their start and end apart: 9 -> 9, of which waited for: 7 -> 7; matrix products, arithmetic and copies ran while one was open for 4% -> 1% of each run, Pallas kernels for 1% -> 1%
where the time goes in v3:
time: 133 us; the launch traced here: 132 us
  starting transfers between devices  46.5 us (35%)
  blocking collectives  45.8 us (34%)
  waiting for transfers between devices  25.5 us (19%)
  Pallas kernels  6.38 us (5%)
  local copies, waits for them, and re-layouts  5.74 us (4%)
    all_to_all x1, blocking collectives, local(): lax.all_to_all(sent, 'dom', split_axis=0, concat_axis=0, tiled=True)  45.8 us
    all_to_all x1, waiting for transfers between devices, local(): lax.all_to_all(copies, 'grp', split_axis=0, concat_axis=0, tiled=True)  12.1 us
    all_to_all x1, starting transfers between devices, local(): lax.all_to_all(copies, 'grp', split_axis=0, concat_axis=0, tiled=True)  11.9 us
    ppermute x3, starting transfers between devices, from_previous(): return lax.ppermute(x, axis, [(i, i + 1) for i in range(count - 1)])  11.8 us
    all_to_all x1, starting transfers between devices, local(): lax.all_to_all(wide, 'dom', split_axis=0, concat_axis=0, tiled=True)  10.5 us
    ppermute x1, starting transfers between devices, swapped(): return lax.ppermute(x, axis, [(i, i ^ 1) for i in range(count)])  6.87 us
    ppermute x3, waiting for transfers between devices, from_next(): return lax.ppermute(x, axis, [(i + 1, i) for i in range(count - 1)])  6.1 us
    ppermute x3, starting transfers between devices, from_next(): return lax.ppermute(x, axis, [(i + 1, i) for i in range(count - 1)])  5.45 us
  transfers between devices with their start and end apart: 9, of which 7 were waited for; matrix products, arithmetic and copies ran while one was open for 1% of the time, Pallas kernels for 1%

profile of v3, /device:TPU:1, one launch (start us, length us, event | category | flops | bytes accessed | tf_op | source)
XLA Modules:
  0.0 131.9 jit_solution(16932912653448808874)
XLA Ops:
  0.6 0.0 copy-start.6
  0.6 0.9 copy-done.6
  1.6 0.0 copy-start.9
  1.6 0.0 copy-start.10
  1.6 0.0 copy-start.11
  1.6 0.0 copy-start.13
  1.6 0.9 shard_map.111
  2.5 10.5 %all-to-all-start = ((bf16[32,16,512]{2,1,0:T(8,128)(2,1)}), bf16[32,16,512]{2,1,0:T(8,128)(2,1)S(1)}, u32[]{:S(2)}, u32[]{:S(2)}) async-start(bf16[32,16,512]{2,1,0:T(8,128)(2,1)} %shard_map.111), calls=%async_computation | async-start | bytes 1048576 | tf_op jit(solution)/shard_map/all_to_all | solution.py:173
  13.0 0.0 copy-done.9
  13.0 0.0 copy-done.10
  13.0 0.0 copy-done.11
  13.0 0.0 copy-start
  13.0 0.0 copy-start.3
  13.0 0.7 shard_map.112.adj
  13.7 0.0 copy-done.13
  13.7 2.9 %collective-permute-start.1 = (bf16[128,1152]{1,0:T(8,128)(2,1)S(1)}, bf16[128,1152]{1,0:T(8,128)(2,1)S(1)}, u32[]{:S(2)}, u32[]{:S(2)}) collective-permute-start(bf16[128,1152]{1,0:T(8,128)(2,1)S(1)} %copy-done.13), channel_id=1, source_target_pairs={{32,0},{64,32},{96,64},{128,96},{160,128},{192,160},{224,192},{256... | collective-permute-start | bytes 884744 | tf_op jit(solution)/shard_map/ppermute | solution.py:31
  16.6 3.9 %collective-permute-start = (bf16[128,1152]{1,0:T(8,128)(2,1)S(1)}, bf16[128,1152]{1,0:T(8,128)(2,1)S(1)}, u32[]{:S(2)}, u32[]{:S(2)}) collective-permute-start(bf16[128,1152]{1,0:T(8,128)(2,1)S(1)} %copy-done.13), channel_id=1, source_target_pairs={{0,32},{32,64},{64,96},{96,128},{128,160},{160,192},{192,224},{224... | collective-permute-start | bytes 884744 | tf_op jit(solution)/shard_map/ppermute | solution.py:26
  20.5 2.8 %collective-permute-done.1 = bf16[128,1152]{1,0:T(8,128)(2,1)S(1)} collective-permute-done((bf16[128,1152]{1,0:T(8,128)(2,1)S(1)}, bf16[128,1152]{1,0:T(8,128)(2,1)S(1)}, u32[]{:S(2)}, u32[]{:S(2)}) %collective-permute-start.1) | collective-permute-done | bytes 294944 | tf_op jit(solution)/shard_map/ppermute | solution.py:31
  23.3 0.9 collective-permute-done
  24.2 0.3 fusion.stale
  24.5 4.7 %all-to-all-done = bf16[32,16,512]{2,1,0:T(8,128)(2,1)S(1)} async-done(((bf16[32,16,512]{2,1,0:T(8,128)(2,1)}), bf16[32,16,512]{2,1,0:T(8,128)(2,1)S(1)}, u32[]{:S(2)}, u32[]{:S(2)}) %all-to-all-start) | async-done | bytes 524320 | tf_op jit(solution)/shard_map/all_to_all | solution.py:173
  29.2 0.0 copy-done
  29.3 0.0 copy-done.3
  29.3 0.0 copy-start.12
  29.3 1.4 %shard_map.113 = (bf16[512,256]{1,0:T(8,128)(2,1)S(1)}, bf16[256,1024]{1,0:T(8,128)(2,1)S(1)}, f32[256,1024]{1,0:T(8,128)S(1)}, bf16[256,128]{1,0:T(8,128)(2,1)S(1)}) custom-call(bf16[256,768]{1,0:T(8,128)(2,1)S(1)} %shard_map.112.adj, bf16[512,512]{1,0:T(8,128)(2,1)S(1)} %bitcast.7, bf16[512,1024]{1,0:T(8,128)(2,1)S(1)} %copy-done, ...), custom_call_target="tpu_custom_call" | custom-call | flops 603979776 | bytes 4000000 | tf_op jit(solution)/shard_map/pallas_call | solution.py:184
  30.6 0.0 copy-start.1
  30.7 0.0 copy-start.4
  30.7 0.0 copy-start.7
  30.7 1.3 collective-permute-start.3
  32.0 4.0 %collective-permute-start.2 = (bf16[128,128]{1,0:T(8,128)(2,1)S(1)}, bf16[128,128]{1,0:T(8,128)(2,1)S(1)}, u32[]{:S(2)}, u32[]{:S(2)}) collective-permute-start(bf16[128,128]{1,0:T(8,128)(2,1)S(1)} %get-tuple-element.43), channel_id=1, source_target_pairs={{0,1},{1,2},{2,3},{3,4},{4,5},{5,6},{6,7},{7,8},{8,9},{9,10},{10,1... | collective-permute-start | bytes 98312 | tf_op jit(solution)/shard_map/ppermute | solution.py:26
  36.0 0.0 copy-done.12
  36.0 0.1 fusion.7.mark
  36.1 0.0 collective-permute-done.3.down
  36.1 0.9 collective-permute-done.2.up
  37.0 1.0 shard_map.114
  38.0 0.0 copy-done.1
  38.0 0.0 copy-done.4
  38.0 3.9 %collective-permute-start.4 = (bf16[128,128]{1,0:T(8,128)(2,1)S(1)}, bf16[128,128]{1,0:T(8,128)(2,1)S(1)}, u32[]{:S(2)}, u32[]{:S(2)}) collective-permute-start(bf16[128,128]{1,0:T(8,128)(2,1)S(1)} %get-tuple-element.30), channel_id=1, source_target_pairs={{0,1},{1,2},{2,3},{3,4},{4,5},{5,6},{6,7},{7,8},{8,9},{9,10},{10,1... | collective-permute-start | bytes 98312 | tf_op jit(solution)/shard_map/ppermute | solution.py:26
  41.9 0.0 copy-done.7
  42.0 1.3 collective-permute-start.5
  43.3 0.0 collective-permute-done.4.up
  43.3 3.3 %collective-permute-done.5.down = bf16[128,128]{1,0:T(8,128)(2,1)S(1)} collective-permute-done((bf16[128,128]{1,0:T(8,128)(2,1)S(1)}, bf16[128,128]{1,0:T(8,128)(2,1)S(1)}, u32[]{:S(2)}, u32[]{:S(2)}) %collective-permute-start.5) | collective-permute-done | bytes 32800 | tf_op jit(solution)/shard_map/ppermute | solution.py:31
  46.6 0.0 copy-start.2
  46.6 1.2 copy-done.2
  47.8 0.0 copy-start.5
  47.8 1.0 copy-done.5
  48.9 0.0 copy-start.8
  48.9 0.9 copy-done.8
  49.8 0.9 shard_map.115
  50.7 6.9 %collective-permute-start.6 = (bf16[512,640]{1,0:T(8,128)(2,1)S(1)}, bf16[512,640]{1,0:T(8,128)(2,1)S(1)}, u32[]{:S(2)}, u32[]{:S(2)}) collective-permute-start(bf16[512,640]{1,0:T(8,128)(2,1)S(1)} %get-tuple-element.36), channel_id=1, source_target_pairs={{0,32},{32,0},{64,96},{96,64},{128,160},{160,128},{192,224},{224,1... | collective-permute-start | bytes 1966088 | tf_op jit(solution)/shard_map/ppermute | solution.py:21
  57.6 0.8 shard_map.116
  58.5 0.8 collective-permute-done.6
  59.3 0.2 add_convert_fusion
  59.5 0.1 pad_maximum_fusion
  59.6 45.8 %all_to_all.19 = bf16[32,16,1152]{2,1,0:T(8,128)(2,1)S(1)} all-to-all(bf16[32,16,1152]{2,1,0:T(8,128)(2,1)S(1)} %bitcast.8), channel_id=1, replica_groups=mesh['grp'=16,'dom'=32] {'dom'}, dimensions={0} | all-to-all | bytes 2359296 | tf_op jit(solution)/shard_map/all_to_all | solution.py:214
  105.4 0.1 slice_reduce_fusion
  105.5 0.8 broadcast_in_dim.5
  106.2 11.9 %all-to-all-start.2 = ((bf16[16,16,640]{2,1,0:T(8,128)(2,1)}), bf16[16,16,640]{2,1,0:T(8,128)(2,1)S(1)}, u32[]{:S(2)}, u32[]{:S(2)}) async-start(bf16[16,16,640]{2,1,0:T(8,128)(2,1)} %broadcast_in_dim.5), calls=%async_computation.2 | async-start | bytes 655360 | tf_op jit(solution)/shard_map/all_to_all | solution.py:218
  118.1 0.1 slice_convert_fusion
  118.3 0.1 fusion.5
  118.4 0.7 copy.13
  119.1 12.1 %all-to-all-done.2.bands = bf16[16,16,640]{2,1,0:T(8,128)(2,1)S(1)} async-done(((bf16[16,16,640]{2,1,0:T(8,128)(2,1)}), bf16[16,16,640]{2,1,0:T(8,128)(2,1)S(1)}, u32[]{:S(2)}, u32[]{:S(2)}) %all-to-all-start.2) | async-done | bytes 327712 | tf_op jit(solution)/shard_map/all_to_all | solution.py:218
  131.2 0.7 shard_map.117
  (2 shorter events, 0.1 us)
Async XLA Ops:
  0.6 1.0 copy-start.6
  1.6 11.4 %copy-start.9 = (bf16[2,4,128,128]{3,2,1,0:T(8,128)(2,1)S(1)}, bf16[2,4,128,128]{3,2,1,0:T(8,128)(2,1)}, u32[]{:S(2)}) copy-start(bf16[2,4,128,128]{3,2,1,0:T(8,128)(2,1)} %tiles) | copy-start | bytes 786436
  1.6 11.4 %copy-start.10 = (s32[2,4]{1,0:T(2,128)S(1)}, s32[2,4]{1,0:T(2,128)}, u32[]{:S(2)}) copy-start(s32[2,4]{1,0:T(2,128)} %src.1) | copy-start | bytes 100
  1.6 11.4 %copy-start.11 = (s32[2]{0:T(128)S(1)}, s32[2]{0:T(128)}, u32[]{:S(2)}) copy-start(s32[2]{0:T(128)} %count.1) | copy-start | bytes 28
  1.6 12.1 %copy-start.13 = (bf16[128,1152]{1,0:T(8,128)(2,1)S(1)}, bf16[128,1152]{1,0:T(8,128)(2,1)}, u32[]{:S(2)}) copy-start(bf16[128,1152]{1,0:T(8,128)(2,1)} %param.11) | copy-start | bytes 884740
  2.5 26.8 %all-to-all-start = ((bf16[32,16,512]{2,1,0:T(8,128)(2,1)}), bf16[32,16,512]{2,1,0:T(8,128)(2,1)S(1)}, u32[]{:S(2)}, u32[]{:S(2)}) async-start(bf16[32,16,512]{2,1,0:T(8,128)(2,1)} %shard_map.111), calls=%async_computation | async-start | bytes 1048576 | tf_op jit(solution)/shard_map/all_to_all | solution.py:173
  13.0 16.2 %copy-start = (bf16[512,1024]{1,0:T(8,128)(2,1)S(1)}, bf16[512,1024]{1,0:T(8,128)(2,1)}, u32[]{:S(2)}) copy-start(bf16[512,1024]{1,0:T(8,128)(2,1)} %w_first.3) | copy-start | bytes 3145732
  13.0 16.2 %copy-start.3 = (bf16[1024,128]{1,0:T(8,128)(2,1)S(1)}, bf16[1024,128]{1,0:T(8,128)(2,1)}, u32[]{:S(2)}) copy-start(bf16[1024,128]{1,0:T(8,128)(2,1)} %w_second.3) | copy-start | bytes 786436
  13.7 9.5 %collective-permute-start.1 = (bf16[128,1152]{1,0:T(8,128)(2,1)S(1)}, bf16[128,1152]{1,0:T(8,128)(2,1)S(1)}, u32[]{:S(2)}, u32[]{:S(2)}) collective-permute-start(bf16[128,1152]{1,0:T(8,128)(2,1)S(1)} %copy-done.13), channel_id=1, source_target_pairs={{32,0},{64,32},{96,64},{128,96},{160,128},{192,160},{224,192},{256... | collective-permute-start | bytes 884744 | tf_op jit(solution)/shard_map/ppermute | solution.py:31
  16.6 7.6 %collective-permute-start = (bf16[128,1152]{1,0:T(8,128)(2,1)S(1)}, bf16[128,1152]{1,0:T(8,128)(2,1)S(1)}, u32[]{:S(2)}, u32[]{:S(2)}) collective-permute-start(bf16[128,1152]{1,0:T(8,128)(2,1)S(1)} %copy-done.13), channel_id=1, source_target_pairs={{0,32},{32,64},{64,96},{96,128},{128,160},{160,192},{192,224},{224... | collective-permute-start | bytes 884744 | tf_op jit(solution)/shard_map/ppermute | solution.py:26
  29.3 6.7 %copy-start.12 = (s32[256]{0:T(256)S(1)}, s32[256]{0:T(256)}, u32[]{:S(2)}) copy-start(s32[256]{0:T(256)} %param.15) | copy-start | bytes 3076
  30.6 7.4 %copy-start.1 = (f32[256,1024]{1,0:T(8,128)}, f32[256,1024]{1,0:T(8,128)S(1)}, u32[]{:S(2)}) copy-start(f32[256,1024]{1,0:T(8,128)S(1)} %get-tuple-element.33.slope) | copy-start | bytes 3145732
  30.7 7.4 %copy-start.4 = (bf16[256,1024]{1,0:T(8,128)(2,1)}, bf16[256,1024]{1,0:T(8,128)(2,1)S(1)}, u32[]{:S(2)}) copy-start(bf16[256,1024]{1,0:T(8,128)(2,1)S(1)} %get-tuple-element.32.hidden) | copy-start | bytes 1572868
  30.7 11.3 %copy-start.7 = (bf16[512,256]{1,0:T(8,128)(2,1)}, bf16[512,256]{1,0:T(8,128)(2,1)S(1)}, u32[]{:S(2)}) copy-start(bf16[512,256]{1,0:T(8,128)(2,1)S(1)} %get-tuple-element.34.agg_t) | copy-start | bytes 786436
  30.7 5.4 %collective-permute-start.3 = (bf16[128,128]{1,0:T(8,128)(2,1)S(1)}, bf16[128,128]{1,0:T(8,128)(2,1)S(1)}, u32[]{:S(2)}, u32[]{:S(2)}) collective-permute-start(bf16[128,128]{1,0:T(8,128)(2,1)S(1)} %get-tuple-element.42), channel_id=1, source_target_pairs={{1,0},{2,1},{3,2},{4,3},{5,4},{6,5},{7,6},{8,7},{9,8},{10,9},{11,1... | collective-permute-start | bytes 98312 | tf_op jit(solution)/shard_map/ppermute | solution.py:31
  32.0 5.0 %collective-permute-start.2 = (bf16[128,128]{1,0:T(8,128)(2,1)S(1)}, bf16[128,128]{1,0:T(8,128)(2,1)S(1)}, u32[]{:S(2)}, u32[]{:S(2)}) collective-permute-start(bf16[128,128]{1,0:T(8,128)(2,1)S(1)} %get-tuple-element.43), channel_id=1, source_target_pairs={{0,1},{1,2},{2,3},{3,4},{4,5},{5,6},{6,7},{7,8},{8,9},{9,10},{10,1... | collective-permute-start | bytes 98312 | tf_op jit(solution)/shard_map/ppermute | solution.py:26
  38.0 5.3 %collective-permute-start.4 = (bf16[128,128]{1,0:T(8,128)(2,1)S(1)}, bf16[128,128]{1,0:T(8,128)(2,1)S(1)}, u32[]{:S(2)}, u32[]{:S(2)}) collective-permute-start(bf16[128,128]{1,0:T(8,128)(2,1)S(1)} %get-tuple-element.30), channel_id=1, source_target_pairs={{0,1},{1,2},{2,3},{3,4},{4,5},{5,6},{6,7},{7,8},{8,9},{9,10},{10,1... | collective-permute-start | bytes 98312 | tf_op jit(solution)/shard_map/ppermute | solution.py:26
  42.0 4.7 %collective-permute-start.5 = (bf16[128,128]{1,0:T(8,128)(2,1)S(1)}, bf16[128,128]{1,0:T(8,128)(2,1)S(1)}, u32[]{:S(2)}, u32[]{:S(2)}) collective-permute-start(bf16[128,128]{1,0:T(8,128)(2,1)S(1)} %get-tuple-element.31), channel_id=1, source_target_pairs={{1,0},{2,1},{3,2},{4,3},{5,4},{6,5},{7,6},{8,7},{9,8},{10,9},{11,1... | collective-permute-start | bytes 98312 | tf_op jit(solution)/shard_map/ppermute | solution.py:31
  46.6 1.2 copy-start.2
  47.8 1.0 copy-start.5
  48.9 0.9 copy-start.8
  50.7 8.6 %collective-permute-start.6 = (bf16[512,640]{1,0:T(8,128)(2,1)S(1)}, bf16[512,640]{1,0:T(8,128)(2,1)S(1)}, u32[]{:S(2)}, u32[]{:S(2)}) collective-permute-start(bf16[512,640]{1,0:T(8,128)(2,1)S(1)} %get-tuple-element.36), channel_id=1, source_target_pairs={{0,32},{32,0},{64,96},{96,64},{128,160},{160,128},{192,224},{224,1... | collective-permute-start | bytes 1966088 | tf_op jit(solution)/shard_map/ppermute | solution.py:21
  106.2 25.0 %all-to-all-start.2 = ((bf16[16,16,640]{2,1,0:T(8,128)(2,1)}), bf16[16,16,640]{2,1,0:T(8,128)(2,1)S(1)}, u32[]{:S(2)}, u32[]{:S(2)}) async-start(bf16[16,16,640]{2,1,0:T(8,128)(2,1)} %broadcast_in_dim.5), calls=%async_computation.2 | async-start | bytes 655360 | tf_op jit(solution)/shard_map/all_to_all | solution.py:218

commit v4 on v3

--- a/solution.py
+++ b/solution.py
@@ -29,6 +29,14 @@
 def from_next(x, axis):
     count = lax.axis_size(axis)
     return lax.ppermute(x, axis, [(i + 1, i) for i in range(count - 1)])
+
+
+def paired(x, axis, first):
+    count = lax.axis_size(axis)
+    pairs = []
+    for i in range(first, count - 1, 2):
+        pairs += [(i, i + 1), (i + 1, i)]
+    return lax.ppermute(x, axis, pairs)
 
 
 def whole(kernel, outs, scratch=(), flops=0):
@@ -41,16 +49,23 @@
     )
 
 
-def widen_kernel(feats, wide):
-    parts, rows, reach = wide.shape
+def widen_kernel(feats, wide, none, sems):
+    parts, _, reach = wide.shape
     own = feats.shape[1] // parts
     blk = (reach - own) // 2
-    none = jnp.zeros((rows, blk), wide.dtype)
+    none[...] = jnp.zeros_like(none)
+    copies = []
     for d in range(parts):
-        first, last = d * own - blk, (d + 1) * own + blk
-        wide[d, :, blk : blk + own] = feats[:, d * own : (d + 1) * own]
-        wide[d, :, :blk] = feats[:, first : first + blk] if d > 0 else none
-        wide[d, :, blk + own :] = feats[:, last - blk : last] if d < parts - 1 else none
+        low, high = max(d * own - blk, 0), min((d + 1) * own + blk, parts * own)
+        start = low - (d * own - blk)
+        copies.append((feats.at[:, low:high], wide.at[d, :, start : start + high - low]))
+    copies.append((none, wide.at[0, :, :blk]))
+    copies.append((none, wide.at[parts - 1, :, reach - blk :]))
+    copies = [pltpu.make_async_copy(src, dst, sems.at[i]) for i, (src, dst) in enumerate(copies)]
+    for copy in copies:
+        copy.start()
+    for copy in copies:
+        copy.wait()
 
 
 def adjacency_kernel(src, count, tiles, adj):
@@ -76,7 +91,7 @@
         second[c * rows : (c + 1) * rows, :] = total[:, half:]
 
 
-def forward_kernel(adj, feats, w_first, stale, w_second, agg_t, hidden, slope, proj):
+def forward_kernel(odd, adj, feats, w_first, stale, w_second, agg_t, hidden, slope, proj, within, across):
     width = feats.shape[1]
     hid = w_first.shape[1]
     step = min(256, hid)
@@ -93,34 +108,48 @@
         slope[:, cols] = s * (1.0 + a * (1.0 - s))
         total += dot(h, w_second[cols, :], 1, 0)
     proj[...] = total.astype(BF)
-
-
-def middle_kernel(hid, adj, up, own, down, stale, mark, logits, inner, rim_up, rim_down):
-    blk = up.shape[0]
+    blk = within.shape[0]
+    top, bottom = proj[:blk], proj[proj.shape[0] - blk :]
+    is_odd = odd[0] == 1
+    within[...] = jnp.where(is_odd, top, bottom)
+    across[...] = jnp.where(is_odd, bottom, top)
+
+
+def middle_kernel(
+    hid, odd, adj, own, paired_in, crossed_in, stale, mark, _hidden, _slope, _agg_t, logits, inner, within, across
+):
+    blk = within.shape[0]
+    is_odd = odd[0] == 1
+    up = jnp.where(is_odd, paired_in[...], crossed_in[...])
+    down = jnp.where(is_odd, crossed_in[...], paired_in[...])
     size = own.shape[0]
     reach = size + 2 * blk
-    agg = dot(adj[:, :blk], up[...], 1, 0)
+    agg = dot(adj[:, :blk], up, 1, 0)
     agg += dot(adj[:, blk : blk + size], own[...], 1, 0)
-    agg += dot(adj[:, blk + size : reach], down[...], 1, 0)
+    agg += dot(adj[:, blk + size : reach], down, 1, 0)
     agg += stale[:, hid:]
     logits[...] = agg.astype(BF)
     e = jnp.exp(agg - jnp.max(agg, axis=1, keepdims=True))
     grad = (e / jnp.sum(e, axis=1, keepdims=True) - mark[...]).astype(BF)
     spread = dot(adj[:, :reach], grad, 0, 0)
     inner[...] = spread[blk : blk + size]
-    rim_up[...] = spread[:blk].astype(BF)
-    rim_down[...] = spread[blk + size :].astype(BF)
-
-
-def backward_kernel(scale, core, inner, up, down, hidden, w_second, slope, agg_t, send, keep, grad_agg, second):
-    blk = up.shape[0]
+    rim_up, rim_down = spread[:blk], spread[blk + size :]
+    within[...] = jnp.where(is_odd, rim_up, rim_down).astype(BF)
+    across[...] = jnp.where(is_odd, rim_down, rim_up).astype(BF)
+
+
+def backward_kernel(
+    scale, odd, core, inner, paired_in, crossed_in, hidden, w_second, slope, agg_t, send, kept, grad_agg, second
+):
+    blk = paired_in.shape[0]
     size = inner.shape[0]
     hid = slope.shape[1]
     step = min(256, hid)
     half = hid // 2
-    other = 1 - core[0]
-    upper = inner[:blk] + up[...].astype(F32)
-    lower = inner[size - blk :] + down[...].astype(F32)
+    is_odd = odd[0] == 1
+    mine, other = core[0], 1 - core[0]
+    upper = inner[:blk] + jnp.where(is_odd, paired_in[...], crossed_in[...]).astype(F32)
+    lower = inner[size - blk :] + jnp.where(is_odd, crossed_in[...], paired_in[...]).astype(F32)
     if size > 2 * blk:
         parts = [upper, inner[blk : size - blk], lower]
     else:
@@ -132,14 +161,17 @@
     second[...] = (dot(hidden[...], grad_p2, 0, 0) * scale).reshape(second.shape)
     rows = second.shape[0] * second.shape[2]
     send[:, half:] = second[:, other].reshape(rows, second.shape[3]).astype(BF)
-    keep[:, half:] = second[:, core[0]].reshape(rows, second.shape[3])
-    for mine, out in ((other, send), (core[0], keep)):
-        g = grad_agg[:, pl.ds(pl.multiple_of(mine * half, half), half)]
-        out[:, :half] = (dot(agg_t[...], g, 1, 0) * scale).astype(out.dtype)
-
-
-def feature_kernel(grad_agg, w_first, adj, out):
+    kept[...] = second[:, mine].reshape(rows, second.shape[3])
+    g = grad_agg[:, pl.ds(pl.multiple_of(other * half, half), half)]
+    send[:, :half] = (dot(agg_t[...], g, 1, 0) * scale).astype(BF)
+
+
+def feature_kernel(scale, core, grad_agg, w_first, adj, agg_t, kept, keep, out):
     width = out.shape[1]
+    half = grad_agg.shape[1] // 2
+    g = grad_agg[:, pl.ds(pl.multiple_of(core[0] * half, half), half)]
+    keep[:, :half] = dot(agg_t[...], g, 1, 0) * scale
+    keep[:, half:] = kept[...]
     back = dot(w_first[...], grad_agg[...], 1, 1).astype(BF)
     out[...] = dot(back, adj[:, :width], 1, 0).astype(BF)
 
@@ -168,7 +200,14 @@
     half = hid // 2
     core = lax.axis_index("grp") % 2
 
-    (wide,) = whole(widen_kernel, [((n_dom, feat_rows, reach), BF)])(feats_t)
+    wide = pl.pallas_call(
+        widen_kernel,
+        out_shape=jax.ShapeDtypeStruct((n_dom, feat_rows, reach), BF),
+        in_specs=[pl.BlockSpec(memory_space=pl.ANY)],
+        out_specs=pl.BlockSpec(memory_space=pl.ANY),
+        scratch_shapes=[pltpu.VMEM((feat_rows, blk), BF), pltpu.SemaphoreType.DMA((n_dom + 2,))],
+        cost_estimate=pl.CostEstimate(flops=0, bytes_accessed=1_000_000, transcendentals=0),
+    )(feats_t)
     wide, tile_vals, stale_rows = lax.optimization_barrier((wide, tile_vals, stale_rows))
     feats = lax.all_to_all(wide, "dom", split_axis=0, concat_axis=0, tiled=True).reshape(feat_all, reach)
 
@@ -181,35 +220,57 @@
     stale_part = dot(adj[:, reach:], jnp.concatenate([before, after], axis=0), 1, 0)
     mark = (labels[:, None] == jnp.arange(classes, dtype=jnp.int32)[None, :]).astype(F32)
 
-    agg_t, hidden, slope, proj_second = whole(
+    odd = (lax.axis_index("dom") % 2)[None]
+    agg_t, hidden, slope, proj_second, within, across = whole_core(
         forward_kernel,
-        [((feat_all, own), BF), ((own, hid), BF), ((own, hid), F32), ((own, classes), BF)],
+        [
+            ((feat_all, own), BF),
+            ((own, hid), BF),
+            ((own, hid), F32),
+            ((own, classes), BF),
+            ((blk, classes), BF),
+            ((blk, classes), BF),
+        ],
+        5,
         flops=2 * own * (2 * feat_all * reach + feat_all * hid + hid * classes),
-    )(adj, feats, w_first, stale_part, w_second)
-
-    up = from_previous(proj_second[own - blk :], "dom")
-    down = from_next(proj_second[:blk], "dom")
-    logits, inner, rim_up, rim_down = whole(
+    )(odd, adj, feats, w_first, stale_part, w_second)
+
+    logits, inner, within, across = whole_core(
         functools.partial(middle_kernel, hid),
         [((own, classes), BF), ((own, classes), F32), ((blk, classes), BF), ((blk, classes), BF)],
+        9,
         flops=4 * own * reach * classes,
-    )(adj, up, proj_second, down, stale_part, mark)
-
-    to_first = from_previous(rim_down, "dom")
-    to_last = from_next(rim_up, "dom")
+    )(
+        odd,
+        adj,
+        proj_second,
+        paired(within, "dom", 0),
+        paired(across, "dom", 1),
+        stale_part,
+        mark,
+        hidden,
+        slope,
+        agg_t,
+    )
+
     width = half + classes
-    send, keep, grad_agg = whole_core(
+    send, kept, grad_agg = whole_core(
         functools.partial(backward_kernel, scale),
-        [((feat_all, width), BF), ((feat_all, width), F32), ((own, hid), BF)],
+        [((feat_all, width), BF), ((feat_all, classes), F32), ((own, hid), BF)],
         7,
         scratch=[pltpu.VMEM((n_dom, 2, feat_rows, classes), F32)],
-        flops=2 * own * (hid * classes * 2 + feat_all * hid),
-    )(core[None], inner, to_first, to_last, hidden, w_second, slope, agg_t)
-    summed = (keep + swapped(send, "grp").astype(F32)).astype(BF)
-
-    (grad_wide,) = whole(
-        feature_kernel, [((feat_all, reach), BF)], flops=2 * own * (hid * feat_all + reach * feat_all)
-    )(grad_agg, w_first, adj)
+        flops=2 * own * (hid * classes * 2 + feat_all * half),
+        scalars=2,
+    )(odd, core[None], inner, paired(within, "dom", 0), paired(across, "dom", 1), hidden, w_second, slope, agg_t)
+    received = swapped(send, "grp")
+
+    keep, grad_wide = whole_core(
+        functools.partial(feature_kernel, scale),
+        [((feat_all, width), F32), ((feat_all, reach), BF)],
+        5,
+        flops=2 * own * (hid * feat_all + reach * feat_all + feat_all * half),
+    )(core[None], grad_agg, w_first, adj, agg_t, kept)
+    summed = (keep + received.astype(F32)).astype(BF)
     sent = jnp.concatenate([summed, grad_wide], axis=1)
     got = lax.all_to_all(sent, "dom", split_axis=0, concat_axis=0, tiled=True).reshape(n_dom, feat_rows, -1)
 

time: 133 us -> 143 us (1.075)
  Pallas kernels: 6.38 us -> 22.6 us
  waiting for transfers between devices: 25.5 us -> 20.8 us
    pallas_call x4, Pallas kernels: 4.11 us -> 20.4 us  [the longest x1 17 us: local(): pl.pallas_call(widen_kernel, out_shape=jax.ShapeDtypeStruct((n_dom, feat_...]
    ppermute x0 -> x4, starting transfers between devices: none -> 9.92 us  [paired(): return lax.ppermute(x, axis, pairs)]
    ppermute x3 -> x1, starting transfers between devices: 11.8 us -> 4.84 us  [from_previous(): return lax.ppermute(x, axis, [(i, i + 1) for i in range(count - 1)])]
    all_to_all x1, waiting for transfers between devices: 4.73 us -> 0.93 us  [local(): lax.all_to_all(wide, 'dom', split_axis=0, concat_axis=0, tiled=True)]
    ppermute x3 -> x1, starting transfers between devices: 5.45 us -> 1.92 us  [from_next(): return lax.ppermute(x, axis, [(i + 1, i) for i in range(count - 1)])]
    ppermute x3 -> x1, waiting for transfers between devices: 6.1 us -> 3.96 us  [from_next(): return lax.ppermute(x, axis, [(i + 1, i) for i in range(count - 1)])]
    ppermute x0 -> x4, waiting for transfers between devices: none -> 1.45 us  [paired(): return lax.ppermute(x, axis, pairs)]
    unnamed x28 -> x26, local copies, waits for them, and re-layouts: 4.2 us -> 3.99 us
  transfers between devices with their start and end apart: 9 -> 9, of which waited for: 7 -> 7; matrix products, arithmetic and copies ran while one was open for 1% -> 2% of each run, Pallas kernels for 1% -> 1%
where the time goes in v4:
time: 143 us; the launch traced here: 142 us
  starting transfers between devices  45.4 us (32%)
  blocking collectives  44.9 us (31%)
  Pallas kernels  22.6 us (16%)
  waiting for transfers between devices  20.8 us (15%)
  local copies, waits for them, and re-layouts  5.51 us (4%)
    all_to_all x1, blocking collectives, local(): lax.all_to_all(sent, 'dom', split_axis=0, concat_axis=0, tiled=True)  44.9 us
    pallas_call x1, Pallas kernels, local(): pl.pallas_call(widen_kernel, out_shape=jax.ShapeDtypeStruct((n_dom, feat_...  17 us
    all_to_all x1, waiting for transfers between devices, local(): lax.all_to_all(copies, 'grp', split_axis=0, concat_axis=0, tiled=True)  12.1 us
    all_to_all x1, starting transfers between devices, local(): lax.all_to_all(copies, 'grp', split_axis=0, concat_axis=0, tiled=True)  11.9 us
    all_to_all x1, starting transfers between devices, local(): lax.all_to_all(wide, 'dom', split_axis=0, concat_axis=0, tiled=True)  10.5 us
    ppermute x4, starting transfers between devices, paired(): return lax.ppermute(x, axis, pairs)  9.92 us
    ppermute x1, starting transfers between devices, swapped(): return lax.ppermute(x, axis, [(i, i ^ 1) for i in range(count)])  6.3 us
    ppermute x1, starting transfers between devices, from_previous(): return lax.ppermute(x, axis, [(i, i + 1) for i in range(count - 1)])  4.84 us
  transfers between devices with their start and end apart: 9, of which 7 were waited for; matrix products, arithmetic and copies ran while one was open for 2% of the time, Pallas kernels for 1%

profile of v4, /device:TPU:1, one launch (start us, length us, event | category | flops | bytes accessed | tf_op | source)
XLA Modules:
  0.0 142.2 jit_solution(13571926896780265012)
XLA Ops:
  0.6 0.0 copy-start.12
  0.6 0.0 copy-start.7
  0.7 0.0 copy-start.8
  0.7 0.0 copy-start.9
  0.7 17.0 %shard_map.111 = bf16[32,16,512]{2,1,0:T(8,128)(2,1)} custom-call(bf16[16,8192]{1,0:T(8,128)(2,1)} %feats.1), custom_call_target="tpu_custom_call" | custom-call | bytes 1000000 | tf_op jit(solution)/shard_map/pallas_call | solution.py:203
  17.7 10.5 %all-to-all-start = ((bf16[32,16,512]{2,1,0:T(8,128)(2,1)}), bf16[32,16,512]{2,1,0:T(8,128)(2,1)S(1)}, u32[]{:S(2)}, u32[]{:S(2)}) async-start(bf16[32,16,512]{2,1,0:T(8,128)(2,1)} %shard_map.111), calls=%async_computation | async-start | bytes 1048576 | tf_op jit(solution)/shard_map/all_to_all | solution.py:212
  28.2 0.0 copy-done.7
  28.3 0.0 copy-done.8
  28.3 0.0 copy-done.9
  28.3 0.0 copy-start
  28.3 0.7 shard_map.112.adj
  29.0 0.0 copy-done.12
  29.0 4.8 %collective-permute-start = (bf16[128,1152]{1,0:T(8,128)(2,1)S(1)}, bf16[128,1152]{1,0:T(8,128)(2,1)S(1)}, u32[]{:S(2)}, u32[]{:S(2)}) collective-permute-start(bf16[128,1152]{1,0:T(8,128)(2,1)S(1)} %copy-done.12), channel_id=1, source_target_pairs={{0,32},{32,64},{64,96},{96,128},{128,160},{160,192},{192,224},{224... | collective-permute-start | bytes 884744 | tf_op jit(solution)/shard_map/ppermute | solution.py:26
  33.8 1.9 %collective-permute-start.1 = (bf16[128,1152]{1,0:T(8,128)(2,1)S(1)}, bf16[128,1152]{1,0:T(8,128)(2,1)}, u32[]{:S(2)}, u32[]{:S(2)}) collective-permute-start(bf16[128,1152]{1,0:T(8,128)(2,1)S(1)} %copy-done.12), channel_id=1, source_target_pairs={{32,0},{64,32},{96,64},{128,96},{160,128},{192,160},{224,192},{256... | collective-permute-start | bytes 884744 | tf_op jit(solution)/shard_map/ppermute | solution.py:31
  35.8 1.7 %collective-permute-done = bf16[128,1152]{1,0:T(8,128)(2,1)S(1)} collective-permute-done((bf16[128,1152]{1,0:T(8,128)(2,1)S(1)}, bf16[128,1152]{1,0:T(8,128)(2,1)S(1)}, u32[]{:S(2)}, u32[]{:S(2)}) %collective-permute-start) | collective-permute-done | bytes 294944 | tf_op jit(solution)/shard_map/ppermute | solution.py:26
  37.5 0.0 copy-start.10
  37.5 0.7 copy-done.10
  38.2 4.0 %collective-permute-done.1 = bf16[128,1152]{1,0:T(8,128)(2,1)} collective-permute-done((bf16[128,1152]{1,0:T(8,128)(2,1)S(1)}, bf16[128,1152]{1,0:T(8,128)(2,1)}, u32[]{:S(2)}, u32[]{:S(2)}) %collective-permute-start.1) | collective-permute-done | bytes 294944 | tf_op jit(solution)/shard_map/ppermute | solution.py:31
  42.2 1.4 fusion.stale
  43.6 0.9 all-to-all-done
  44.5 0.0 copy-done
  44.5 0.0 copy-start.5
  44.5 0.9 copy-done.5
  45.5 0.0 copy-start.11
  45.5 1.4 shard_map.113
  46.9 0.0 copy-start.1
  46.9 0.0 copy-start.3
  46.9 3.0 %collective-permute-start.2 = (bf16[128,128]{1,0:T(8,128)(2,1)S(1)}, bf16[128,128]{1,0:T(8,128)(2,1)S(1)}, u32[]{:S(2)}, u32[]{:S(2)}) collective-permute-start(bf16[128,128]{1,0:T(8,128)(2,1)S(1)} %get-tuple-element.32), channel_id=1, source_target_pairs={{0,1},{1,0},{2,3},{3,2},{4,5},{5,4},{6,7},{7,6},{8,9},{9,8},{10,11... | collective-permute-start | bytes 98312 | tf_op jit(solution)/shard_map/ppermute | solution.py:39
  49.9 0.7 collective-permute-start.3
  50.6 0.0 copy-done.11
  50.6 0.1 fusion.7.mark
  50.7 0.8 collective-permute-done.2.paired_in
  51.6 0.0 collective-permute-done.3.crossed_in
  51.6 0.0 copy-start.6
  51.6 1.0 shard_map.114
  52.6 0.0 copy-done.1
  52.6 0.0 copy-done.3
  52.6 5.6 %collective-permute-start.4 = (bf16[128,128]{1,0:T(8,128)(2,1)S(1)}, bf16[128,128]{1,0:T(8,128)(2,1)S(1)}, u32[]{:S(2)}, u32[]{:S(2)}) collective-permute-start(bf16[128,128]{1,0:T(8,128)(2,1)S(1)} %get-tuple-element.39), channel_id=1, source_target_pairs={{0,1},{1,0},{2,3},{3,2},{4,5},{5,4},{6,7},{7,6},{8,9},{9,8},{10,11... | collective-permute-start | bytes 98312 | tf_op jit(solution)/shard_map/ppermute | solution.py:39
  58.2 0.7 collective-permute-start.5
  58.8 0.6 collective-permute-done.4.paired_in
  59.5 0.0 collective-permute-done.5.crossed_in
  59.5 0.0 copy-done.6
  59.5 0.0 copy-start.2
  59.5 1.2 copy-done.2
  60.7 0.0 copy-start.4
  60.7 1.0 copy-done.4
  61.7 0.8 shard_map.115
  62.5 6.3 %collective-permute-start.6 = (bf16[512,640]{1,0:T(8,128)(2,1)S(1)}, bf16[512,640]{1,0:T(8,128)(2,1)S(1)}, u32[]{:S(2)}, u32[]{:S(2)}) collective-permute-start(bf16[512,640]{1,0:T(8,128)(2,1)S(1)} %get-tuple-element.44), channel_id=1, source_target_pairs={{0,32},{32,0},{64,96},{96,64},{128,160},{160,128},{192,224},{224,1... | collective-permute-start | bytes 1966088 | tf_op jit(solution)/shard_map/ppermute | solution.py:21
  68.8 1.0 shard_map.116
  69.8 0.7 collective-permute-done.6
  70.5 0.1 add_convert_fusion
  70.6 0.1 pad_maximum_fusion
  70.7 44.9 %all_to_all.19 = bf16[32,16,1152]{2,1,0:T(8,128)(2,1)S(1)} all-to-all(bf16[32,16,1152]{2,1,0:T(8,128)(2,1)S(1)} %bitcast.9), channel_id=1, replica_groups=mesh['grp'=16,'dom'=32] {'dom'}, dimensions={0} | all-to-all | bytes 2359296 | tf_op jit(solution)/shard_map/all_to_all | solution.py:275
  115.7 0.1 slice_reduce_fusion
  115.8 0.8 broadcast_in_dim.8
  116.5 11.9 %all-to-all-start.2 = ((bf16[16,16,640]{2,1,0:T(8,128)(2,1)}), bf16[16,16,640]{2,1,0:T(8,128)(2,1)S(1)}, u32[]{:S(2)}, u32[]{:S(2)}) async-start(bf16[16,16,640]{2,1,0:T(8,128)(2,1)} %broadcast_in_dim.8), calls=%async_computation.2 | async-start | bytes 655360 | tf_op jit(solution)/shard_map/all_to_all | solution.py:279
  128.4 0.1 slice_convert_fusion
  128.6 0.1 fusion.5
  128.7 0.7 copy.13
  129.4 12.1 %all-to-all-done.2.bands = bf16[16,16,640]{2,1,0:T(8,128)(2,1)S(1)} async-done(((bf16[16,16,640]{2,1,0:T(8,128)(2,1)}), bf16[16,16,640]{2,1,0:T(8,128)(2,1)S(1)}, u32[]{:S(2)}, u32[]{:S(2)}) %all-to-all-start.2) | async-done | bytes 327712 | tf_op jit(solution)/shard_map/all_to_all | solution.py:279
  141.5 0.7 shard_map.117
  (1 shorter events, 0.0 us)
Async XLA Ops:
  0.6 28.4 %copy-start.12 = (bf16[128,1152]{1,0:T(8,128)(2,1)S(1)}, bf16[128,1152]{1,0:T(8,128)(2,1)}, u32[]{:S(2)}) copy-start(bf16[128,1152]{1,0:T(8,128)(2,1)} %param.11) | copy-start | bytes 884740
  0.6 27.6 %copy-start.7 = (bf16[2,4,128,128]{3,2,1,0:T(8,128)(2,1)S(1)}, bf16[2,4,128,128]{3,2,1,0:T(8,128)(2,1)}, u32[]{:S(2)}) copy-start(bf16[2,4,128,128]{3,2,1,0:T(8,128)(2,1)} %tiles) | copy-start | bytes 786436
  0.7 27.6 %copy-start.8 = (s32[2,4]{1,0:T(2,128)S(1)}, s32[2,4]{1,0:T(2,128)}, u32[]{:S(2)}) copy-start(s32[2,4]{1,0:T(2,128)} %src.1) | copy-start | bytes 100
  0.7 27.6 %copy-start.9 = (s32[2]{0:T(128)S(1)}, s32[2]{0:T(128)}, u32[]{:S(2)}) copy-start(s32[2]{0:T(128)} %count.1) | copy-start | bytes 28
  17.7 26.8 %all-to-all-start = ((bf16[32,16,512]{2,1,0:T(8,128)(2,1)}), bf16[32,16,512]{2,1,0:T(8,128)(2,1)S(1)}, u32[]{:S(2)}, u32[]{:S(2)}) async-start(bf16[32,16,512]{2,1,0:T(8,128)(2,1)} %shard_map.111), calls=%async_computation | async-start | bytes 1048576 | tf_op jit(solution)/shard_map/all_to_all | solution.py:212
  28.3 16.2 %copy-start = (bf16[512,1024]{1,0:T(8,128)(2,1)S(1)}, bf16[512,1024]{1,0:T(8,128)(2,1)}, u32[]{:S(2)}) copy-start(bf16[512,1024]{1,0:T(8,128)(2,1)} %w_first.3) | copy-start | bytes 3145732
  29.0 8.5 %collective-permute-start = (bf16[128,1152]{1,0:T(8,128)(2,1)S(1)}, bf16[128,1152]{1,0:T(8,128)(2,1)S(1)}, u32[]{:S(2)}, u32[]{:S(2)}) collective-permute-start(bf16[128,1152]{1,0:T(8,128)(2,1)S(1)} %copy-done.12), channel_id=1, source_target_pairs={{0,32},{32,64},{64,96},{96,128},{128,160},{160,192},{192,224},{224... | collective-permute-start | bytes 884744 | tf_op jit(solution)/shard_map/ppermute | solution.py:26
  33.8 8.3 %collective-permute-start.1 = (bf16[128,1152]{1,0:T(8,128)(2,1)S(1)}, bf16[128,1152]{1,0:T(8,128)(2,1)}, u32[]{:S(2)}, u32[]{:S(2)}) collective-permute-start(bf16[128,1152]{1,0:T(8,128)(2,1)S(1)} %copy-done.12), channel_id=1, source_target_pairs={{32,0},{64,32},{96,64},{128,96},{160,128},{192,160},{224,192},{256... | collective-permute-start | bytes 884744 | tf_op jit(solution)/shard_map/ppermute | solution.py:31
  37.5 0.7 copy-start.10
  44.5 1.0 copy-start.5
  45.5 5.1 %copy-start.11 = (s32[256]{0:T(256)S(1)}, s32[256]{0:T(256)}, u32[]{:S(2)}) copy-start(s32[256]{0:T(256)} %param.15) | copy-start | bytes 3076
  46.9 5.7 %copy-start.1 = (f32[256,1024]{1,0:T(8,128)}, f32[256,1024]{1,0:T(8,128)S(1)}, u32[]{:S(2)}) copy-start(f32[256,1024]{1,0:T(8,128)S(1)} %get-tuple-element.35._slope.slope) | copy-start | bytes 3145732
  46.9 5.7 %copy-start.3 = (bf16[256,1024]{1,0:T(8,128)(2,1)}, bf16[256,1024]{1,0:T(8,128)(2,1)S(1)}, u32[]{:S(2)}) copy-start(bf16[256,1024]{1,0:T(8,128)(2,1)S(1)} %get-tuple-element.34._hidden.hidden) | copy-start | bytes 1572868
  46.9 4.7 %collective-permute-start.2 = (bf16[128,128]{1,0:T(8,128)(2,1)S(1)}, bf16[128,128]{1,0:T(8,128)(2,1)S(1)}, u32[]{:S(2)}, u32[]{:S(2)}) collective-permute-start(bf16[128,128]{1,0:T(8,128)(2,1)S(1)} %get-tuple-element.32), channel_id=1, source_target_pairs={{0,1},{1,0},{2,3},{3,2},{4,5},{5,4},{6,7},{7,6},{8,9},{9,8},{10,11... | collective-permute-start | bytes 98312 | tf_op jit(solution)/shard_map/ppermute | solution.py:39
  49.9 1.6 %collective-permute-start.3 = (bf16[128,128]{1,0:T(8,128)(2,1)S(1)}, bf16[128,128]{1,0:T(8,128)(2,1)S(1)}, u32[]{:S(2)}, u32[]{:S(2)}) collective-permute-start(bf16[128,128]{1,0:T(8,128)(2,1)S(1)} %get-tuple-element.33), channel_id=1, source_target_pairs={{1,2},{2,1},{3,4},{4,3},{5,6},{6,5},{7,8},{8,7},{9,10},{10,9},{11,... | collective-permute-start | bytes 98312 | tf_op jit(solution)/shard_map/ppermute | solution.py:39
  51.6 7.9 %copy-start.6 = (bf16[1024,128]{1,0:T(8,128)(2,1)S(1)}, bf16[1024,128]{1,0:T(8,128)(2,1)}, u32[]{:S(2)}) copy-start(bf16[1024,128]{1,0:T(8,128)(2,1)} %w_second.3) | copy-start | bytes 786436
  52.6 6.9 %collective-permute-start.4 = (bf16[128,128]{1,0:T(8,128)(2,1)S(1)}, bf16[128,128]{1,0:T(8,128)(2,1)S(1)}, u32[]{:S(2)}, u32[]{:S(2)}) collective-permute-start(bf16[128,128]{1,0:T(8,128)(2,1)S(1)} %get-tuple-element.39), channel_id=1, source_target_pairs={{0,1},{1,0},{2,3},{3,2},{4,5},{5,4},{6,7},{7,6},{8,9},{9,8},{10,11... | collective-permute-start | bytes 98312 | tf_op jit(solution)/shard_map/ppermute | solution.py:39
  58.2 1.3 collective-permute-start.5
  59.5 1.2 copy-start.2
  60.7 1.0 copy-start.4
  62.5 8.0 %collective-permute-start.6 = (bf16[512,640]{1,0:T(8,128)(2,1)S(1)}, bf16[512,640]{1,0:T(8,128)(2,1)S(1)}, u32[]{:S(2)}, u32[]{:S(2)}) collective-permute-start(bf16[512,640]{1,0:T(8,128)(2,1)S(1)} %get-tuple-element.44), channel_id=1, source_target_pairs={{0,32},{32,0},{64,96},{96,64},{128,160},{160,128},{192,224},{224,1... | collective-permute-start | bytes 1966088 | tf_op jit(solution)/shard_map/ppermute | solution.py:21
  116.5 25.0 %all-to-all-start.2 = ((bf16[16,16,640]{2,1,0:T(8,128)(2,1)}), bf16[16,16,640]{2,1,0:T(8,128)(2,1)S(1)}, u32[]{:S(2)}, u32[]{:S(2)}) async-start(bf16[16,16,640]{2,1,0:T(8,128)(2,1)} %broadcast_in_dim.8), calls=%async_computation.2 | async-start | bytes 655360 | tf_op jit(solution)/shard_map/all_to_all | solution.py:279

commit v5 on v4

--- a/solution.py
+++ b/solution.py
@@ -39,33 +39,34 @@
     return lax.ppermute(x, axis, pairs)
 
 
+def here(x):
+    return pltpu.with_memory_space_constraint(x, pltpu.VMEM)
+
+
+def result(shape, dtype, keep=False):
+    return pltpu.VMEM(shape, dtype) if keep else jax.ShapeDtypeStruct(shape, dtype)
+
+
 def whole(kernel, outs, scratch=(), flops=0):
     return pl.pallas_call(
         kernel,
-        out_shape=[jax.ShapeDtypeStruct(shape, dtype) for shape, dtype in outs],
+        out_shape=[result(*out) for out in outs],
         scratch_shapes=list(scratch),
         compiler_params=pltpu.CompilerParams(vmem_limit_bytes=16 * 1024 * 1024),
         cost_estimate=pl.CostEstimate(flops=flops, bytes_accessed=4_000_000, transcendentals=0),
     )
 
 
-def widen_kernel(feats, wide, none, sems):
-    parts, _, reach = wide.shape
+def widen_kernel(feats, wide):
+    parts, rows, reach = wide.shape
     own = feats.shape[1] // parts
     blk = (reach - own) // 2
-    none[...] = jnp.zeros_like(none)
-    copies = []
+    none = jnp.zeros((rows, blk), wide.dtype)
     for d in range(parts):
-        low, high = max(d * own - blk, 0), min((d + 1) * own + blk, parts * own)
-        start = low - (d * own - blk)
-        copies.append((feats.at[:, low:high], wide.at[d, :, start : start + high - low]))
-    copies.append((none, wide.at[0, :, :blk]))
-    copies.append((none, wide.at[parts - 1, :, reach - blk :]))
-    copies = [pltpu.make_async_copy(src, dst, sems.at[i]) for i, (src, dst) in enumerate(copies)]
-    for copy in copies:
-        copy.start()
-    for copy in copies:
-        copy.wait()
+        first, last = d * own - blk, (d + 1) * own + blk
+        wide[d, :, blk : blk + own] = feats[:, d * own : (d + 1) * own]
+        wide[d, :, :blk] = feats[:, first : first + blk] if d > 0 else none
+        wide[d, :, blk + own :] = feats[:, last - blk : last] if d < parts - 1 else none
 
 
 def adjacency_kernel(src, count, tiles, adj):
@@ -78,6 +79,12 @@
                 hit = jnp.logical_and(src[r, k] == t, k < live)
                 block = jnp.where(hit, tiles[r, k], block)
             adj[r * blk : (r + 1) * blk, t * blk : (t + 1) * blk] = block
+
+
+def stale_kernel(adj, before, after, out):
+    rows = before.shape[0]
+    at = adj.shape[1] - 2 * rows
+    out[...] = dot(adj[:, at : at + rows], before[...], 1, 0) + dot(adj[:, at + rows :], after[...], 1, 0)
 
 
 def total_kernel(bands, first, second):
@@ -116,7 +123,7 @@
 
 
 def middle_kernel(
-    hid, odd, adj, own, paired_in, crossed_in, stale, mark, _hidden, _slope, _agg_t, logits, inner, within, across
+    hid, odd, adj, own, paired_in, crossed_in, stale, mark, logits, inner, within, across
 ):
     blk = within.shape[0]
     is_odd = odd[0] == 1
@@ -179,7 +186,7 @@
 def whole_core(kernel, outs, blocks, scratch=(), flops=0, scalars=1):
     return pl.pallas_call(
         kernel,
-        out_shape=[jax.ShapeDtypeStruct(shape, dtype) for shape, dtype in outs],
+        out_shape=[result(*out) for out in outs],
         in_specs=[pl.BlockSpec(memory_space=pltpu.SMEM)] * scalars + [pl.BlockSpec(memory_space=pltpu.VMEM)] * blocks,
         scratch_shapes=scratch,
         compiler_params=pltpu.CompilerParams(vmem_limit_bytes=16 * 1024 * 1024),
@@ -200,14 +207,7 @@
     half = hid // 2
     core = lax.axis_index("grp") % 2
 
-    wide = pl.pallas_call(
-        widen_kernel,
-        out_shape=jax.ShapeDtypeStruct((n_dom, feat_rows, reach), BF),
-        in_specs=[pl.BlockSpec(memory_space=pl.ANY)],
-        out_specs=pl.BlockSpec(memory_space=pl.ANY),
-        scratch_shapes=[pltpu.VMEM((feat_rows, blk), BF), pltpu.SemaphoreType.DMA((n_dom + 2,))],
-        cost_estimate=pl.CostEstimate(flops=0, bytes_accessed=1_000_000, transcendentals=0),
-    )(feats_t)
+    (wide,) = whole(widen_kernel, [((n_dom, feat_rows, reach), BF)])(feats_t)
     wide, tile_vals, stale_rows = lax.optimization_barrier((wide, tile_vals, stale_rows))
     feats = lax.all_to_all(wide, "dom", split_axis=0, concat_axis=0, tiled=True).reshape(feat_all, reach)
 
@@ -217,28 +217,30 @@
     stale_rows, adj = lax.optimization_barrier((stale_rows, adj))
     before = from_previous(stale_rows, "grp")
     after = from_next(stale_rows, "grp")
-    stale_part = dot(adj[:, reach:], jnp.concatenate([before, after], axis=0), 1, 0)
+    (stale_part,) = whole(
+        stale_kernel, [((own, hid + classes), F32, True)], flops=2 * own * 2 * blk * (hid + classes)
+    )(adj, before, after)
     mark = (labels[:, None] == jnp.arange(classes, dtype=jnp.int32)[None, :]).astype(F32)
 
     odd = (lax.axis_index("dom") % 2)[None]
     agg_t, hidden, slope, proj_second, within, across = whole_core(
         forward_kernel,
         [
-            ((feat_all, own), BF),
-            ((own, hid), BF),
-            ((own, hid), F32),
+            ((feat_all, own), BF, True),
+            ((own, hid), BF, True),
+            ((own, hid), F32, True),
             ((own, classes), BF),
             ((blk, classes), BF),
             ((blk, classes), BF),
         ],
         5,
         flops=2 * own * (2 * feat_all * reach + feat_all * hid + hid * classes),
-    )(odd, adj, feats, w_first, stale_part, w_second)
+    )(odd, adj, feats, w_first, here(stale_part), w_second)
 
     logits, inner, within, across = whole_core(
         functools.partial(middle_kernel, hid),
         [((own, classes), BF), ((own, classes), F32), ((blk, classes), BF), ((blk, classes), BF)],
-        9,
+        6,
         flops=4 * own * reach * classes,
     )(
         odd,
@@ -246,11 +248,8 @@
         proj_second,
         paired(within, "dom", 0),
         paired(across, "dom", 1),
-        stale_part,
+        here(stale_part),
         mark,
-        hidden,
-        slope,
-        agg_t,
     )
 
     width = half + classes
@@ -261,7 +260,7 @@
         scratch=[pltpu.VMEM((n_dom, 2, feat_rows, classes), F32)],
         flops=2 * own * (hid * classes * 2 + feat_all * half),
         scalars=2,
-    )(odd, core[None], inner, paired(within, "dom", 0), paired(across, "dom", 1), hidden, w_second, slope, agg_t)
+    )(odd, core[None], inner, paired(within, "dom", 0), paired(across, "dom", 1), here(hidden), w_second, here(slope), here(agg_t))
     received = swapped(send, "grp")
 
     keep, grad_wide = whole_core(
@@ -269,7 +268,7 @@
         [((feat_all, width), F32), ((feat_all, reach), BF)],
         5,
         flops=2 * own * (hid * feat_all + reach * feat_all + feat_all * half),
-    )(core[None], grad_agg, w_first, adj, agg_t, kept)
+    )(core[None], grad_agg, w_first, adj, here(agg_t), kept)
     summed = (keep + received.astype(F32)).astype(BF)
     sent = jnp.concatenate([summed, grad_wide], axis=1)
     got = lax.all_to_all(sent, "dom", split_axis=0, concat_axis=0, tiled=True).reshape(n_dom, feat_rows, -1)

time: 143 us -> 129 us (0.902)
  Pallas kernels: 22.6 us -> 6.83 us
  local copies, waits for them, and re-layouts: 5.51 us -> 9.09 us
    pallas_call x2 -> x3, Pallas kernels: 18.4 us -> 2.73 us  [the longest x1 1.41 us: local(): whole_core(forward_kernel, [((feat_all, own), BF, True), ((own, hid), BF,...]
    unnamed x26 -> x36, local copies, waits for them, and re-layouts: 3.99 us -> 7.58 us
  transfers between devices with their start and end apart: 9 -> 9, of which waited for: 7 -> 6; matrix products, arithmetic and copies ran while one was open for 2% -> 1% of each run, Pallas kernels for 1% -> 2%
where the time goes in v5:
time: 129 us
  starting transfers between devices  46.1 us (36%)
  blocking collectives  45.4 us (35%)
  waiting for transfers between devices  19.6 us (15%)
  local copies, waits for them, and re-layouts  9.09 us (7%)
  Pallas kernels  6.83 us (5%)
    all_to_all x1, blocking collectives, local(): lax.all_to_all(sent, 'dom', split_axis=0, concat_axis=0, tiled=True)  45.4 us
    all_to_all x1, starting transfers between devices, local(): lax.all_to_all(copies, 'grp', split_axis=0, concat_axis=0, tiled=True)  13.1 us
    all_to_all x1, waiting for transfers between devices, local(): lax.all_to_all(copies, 'grp', split_axis=0, concat_axis=0, tiled=True)  12.1 us
    ppermute x4, starting transfers between devices, paired(): return lax.ppermute(x, axis, pairs)  10.6 us
    all_to_all x1, starting transfers between devices, local(): lax.all_to_all(wide, 'dom', split_axis=0, concat_axis=0, tiled=True)  10.5 us
    unnamed x36, local copies, waits for them, and re-layouts  7.58 us
    ppermute x1, starting transfers between devices, swapped(): return lax.ppermute(x, axis, [(i, i ^ 1) for i in range(count)])  4.98 us
    ppermute x1, starting transfers between devices, from_previous(): return lax.ppermute(x, axis, [(i, i + 1) for i in range(count - 1)])  4.97 us
  transfers between devices with their start and end apart: 9, of which 6 were waited for; matrix products, arithmetic and copies ran while one was open for 1% of the time, Pallas kernels for 2%

profile of v5, /device:TPU:1, one launch (start us, length us, event | category | flops | bytes accessed | tf_op | source)
XLA Modules:
  0.0 128.5 jit_solution(1709272947596273631)
XLA Ops:
  0.6 0.0 copy-start.12
  0.6 0.9 copy-done.12
  1.6 0.0 copy-start.13
  1.6 0.0 copy-start.14
  1.6 0.0 copy-start.15
  1.6 0.0 copy-start.17
  1.6 0.9 shard_map.111
  2.5 10.5 %all-to-all-start = ((bf16[32,16,512]{2,1,0:T(8,128)(2,1)}), bf16[32,16,512]{2,1,0:T(8,128)(2,1)S(1)}, u32[]{:S(2)}, u32[]{:S(2)}) async-start(bf16[32,16,512]{2,1,0:T(8,128)(2,1)} %shard_map.111), calls=%async_computation | async-start | bytes 1048576 | tf_op jit(solution)/shard_map/all_to_all | solution.py:212
  13.0 0.0 copy-done.13
  13.0 0.0 copy-done.14
  13.0 0.0 copy-done.15
  13.0 0.7 shard_map.112.adj
  13.7 0.0 copy-done.17
  13.7 0.0 copy-start
  13.7 0.0 copy-start.3
  13.7 5.0 %collective-permute-start = (bf16[128,1152]{1,0:T(8,128)(2,1)S(1)}, bf16[128,1152]{1,0:T(8,128)(2,1)S(1)}, u32[]{:S(2)}, u32[]{:S(2)}) collective-permute-start(bf16[128,1152]{1,0:T(8,128)(2,1)S(1)} %copy-done.17), channel_id=1, source_target_pairs={{0,32},{32,64},{64,96},{96,128},{128,160},{160,192},{192,224},{224... | collective-permute-start | bytes 884744 | tf_op jit(solution)/shard_map/ppermute | solution.py:26
  18.7 1.9 %collective-permute-start.1 = (bf16[128,1152]{1,0:T(8,128)(2,1)S(1)}, bf16[128,1152]{1,0:T(8,128)(2,1)S(1)}, u32[]{:S(2)}, u32[]{:S(2)}) collective-permute-start(bf16[128,1152]{1,0:T(8,128)(2,1)S(1)} %copy-done.17), channel_id=1, source_target_pairs={{32,0},{64,32},{96,64},{128,96},{160,128},{192,160},{224,192},{256... | collective-permute-start | bytes 884744 | tf_op jit(solution)/shard_map/ppermute | solution.py:31
  20.7 1.7 %collective-permute-done.before = bf16[128,1152]{1,0:T(8,128)(2,1)S(1)} collective-permute-done((bf16[128,1152]{1,0:T(8,128)(2,1)S(1)}, bf16[128,1152]{1,0:T(8,128)(2,1)S(1)}, u32[]{:S(2)}, u32[]{:S(2)}) %collective-permute-start) | collective-permute-done | bytes 294944 | tf_op jit(solution)/shard_map/ppermute | solution.py:26
  22.4 0.7 copy-done.8
  23.1 4.0 %collective-permute-done.1.after = bf16[128,1152]{1,0:T(8,128)(2,1)S(1)} collective-permute-done((bf16[128,1152]{1,0:T(8,128)(2,1)S(1)}, bf16[128,1152]{1,0:T(8,128)(2,1)S(1)}, u32[]{:S(2)}, u32[]{:S(2)}) %collective-permute-start.1) | collective-permute-done | bytes 294944 | tf_op jit(solution)/shard_map/ppermute | solution.py:31
  27.1 0.7 copy-done.10
  27.8 1.0 copy-done.9
  28.8 1.0 copy-done.11
  29.7 0.5 shard_map.113.stale
  30.2 0.0 all-to-all-done
  30.2 0.0 copy-done
  30.2 0.0 copy-done.3
  30.2 0.0 copy-start.16
  30.2 1.4 %shard_map.114 = (bf16[512,256]{1,0:T(8,128)(2,1)S(1)}, bf16[256,1024]{1,0:T(8,128)(2,1)S(1)}, f32[256,1024]{1,0:T(8,128)S(1)}, bf16[256,128]{1,0:T(8,128)(2,1)S...) custom-call(s32[1]{0:T(128)} %bitcast.odd, bf16[256,768]{1,0:T(8,128)(2,1)S(1)} %shard_map.112.adj, ...), custom_call_target="tpu_custom_call" | custom-call | flops 603979776 | bytes 4000000 | tf_op jit(solution)/shard_map/pallas_call | solution.py:226
  31.6 0.0 copy-start.1
  31.6 0.0 copy-start.4
  31.6 0.0 copy-start.6
  31.7 3.4 %collective-permute-start.2 = (bf16[128,128]{1,0:T(8,128)(2,1)S(1)}, bf16[128,128]{1,0:T(8,128)(2,1)S(1)}, u32[]{:S(2)}, u32[]{:S(2)}) collective-permute-start(bf16[128,128]{1,0:T(8,128)(2,1)S(1)} %get-tuple-element.32), channel_id=1, source_target_pairs={{0,1},{1,0},{2,3},{3,2},{4,5},{5,4},{6,7},{7,6},{8,9},{9,8},{10,11... | collective-permute-start | bytes 98312 | tf_op jit(solution)/shard_map/ppermute | solution.py:39
  35.1 0.7 collective-permute-start.3
  35.7 0.0 copy-done.16
  35.8 0.1 fusion.2.mark
  35.9 0.5 collective-permute-done.2.paired_in
  36.4 0.0 collective-permute-done.3.crossed_in
  36.4 1.0 shard_map.115
  37.4 0.0 copy-done.1
  37.4 0.0 copy-done.4
  37.4 5.9 %collective-permute-start.4 = (bf16[128,128]{1,0:T(8,128)(2,1)S(1)}, bf16[128,128]{1,0:T(8,128)(2,1)S(1)}, u32[]{:S(2)}, u32[]{:S(2)}) collective-permute-start(bf16[128,128]{1,0:T(8,128)(2,1)S(1)} %get-tuple-element.36), channel_id=1, source_target_pairs={{0,1},{1,0},{2,3},{3,2},{4,5},{5,4},{6,7},{7,6},{8,9},{9,8},{10,11... | collective-permute-start | bytes 98312 | tf_op jit(solution)/shard_map/ppermute | solution.py:39
  43.3 0.0 copy-done.6
  43.3 0.7 collective-permute-start.5
  44.0 0.6 collective-permute-done.4.paired_in
  44.6 0.0 collective-permute-done.5.crossed_in
  44.6 1.2 copy-done.2
  45.8 0.9 copy-done.5
  46.8 1.0 copy-done.7
  47.8 0.7 shard_map.116
  48.5 5.0 %collective-permute-start.6 = (bf16[512,640]{1,0:T(8,128)(2,1)S(1)}, bf16[512,640]{1,0:T(8,128)(2,1)S(1)}, u32[]{:S(2)}, u32[]{:S(2)}) collective-permute-start(bf16[512,640]{1,0:T(8,128)(2,1)S(1)} %get-tuple-element.44), channel_id=1, source_target_pairs={{0,32},{32,0},{64,96},{96,64},{128,160},{160,128},{192,224},{224,1... | collective-permute-start | bytes 1966088 | tf_op jit(solution)/shard_map/ppermute | solution.py:21
  53.5 1.0 shard_map.117
  54.5 0.7 collective-permute-done.6
  55.2 0.1 add_convert_fusion
  55.4 0.1 pad_maximum_fusion
  55.5 45.4 %all_to_all.19 = bf16[32,16,1152]{2,1,0:T(8,128)(2,1)S(1)} all-to-all(bf16[32,16,1152]{2,1,0:T(8,128)(2,1)S(1)} %bitcast.9), channel_id=1, replica_groups=mesh['grp'=16,'dom'=32] {'dom'}, dimensions={0} | all-to-all | bytes 2359296 | tf_op jit(solution)/shard_map/all_to_all | solution.py:274
  100.9 0.1 slice_reduce_fusion
  101.0 0.7 broadcast_in_dim.8
  101.7 13.1 %all-to-all-start.2 = ((bf16[16,16,640]{2,1,0:T(8,128)(2,1)}), bf16[16,16,640]{2,1,0:T(8,128)(2,1)S(1)}, u32[]{:S(2)}, u32[]{:S(2)}) async-start(bf16[16,16,640]{2,1,0:T(8,128)(2,1)} %broadcast_in_dim.8), calls=%async_computation.2 | async-start | bytes 655360 | tf_op jit(solution)/shard_map/all_to_all | solution.py:278
  114.8 0.1 slice_convert_fusion
  115.0 0.1 fusion.1
  115.0 0.7 copy.13
  115.8 12.1 %all-to-all-done.2.bands = bf16[16,16,640]{2,1,0:T(8,128)(2,1)S(1)} async-done(((bf16[16,16,640]{2,1,0:T(8,128)(2,1)}), bf16[16,16,640]{2,1,0:T(8,128)(2,1)S(1)}, u32[]{:S(2)}, u32[]{:S(2)}) %all-to-all-start.2) | async-done | bytes 327712 | tf_op jit(solution)/shard_map/all_to_all | solution.py:278
  127.9 0.7 shard_map.118
  (8 shorter events, 0.1 us)
Async XLA Ops:
  0.6 1.0 copy-start.12
  1.6 11.4 %copy-start.13 = (bf16[2,4,128,128]{3,2,1,0:T(8,128)(2,1)S(1)}, bf16[2,4,128,128]{3,2,1,0:T(8,128)(2,1)}, u32[]{:S(2)}) copy-start(bf16[2,4,128,128]{3,2,1,0:T(8,128)(2,1)} %tiles) | copy-start | bytes 786436
  1.6 11.4 %copy-start.14 = (s32[2,4]{1,0:T(2,128)S(1)}, s32[2,4]{1,0:T(2,128)}, u32[]{:S(2)}) copy-start(s32[2,4]{1,0:T(2,128)} %src.1) | copy-start | bytes 100
  1.6 11.4 %copy-start.15 = (s32[2]{0:T(128)S(1)}, s32[2]{0:T(128)}, u32[]{:S(2)}) copy-start(s32[2]{0:T(128)} %count.1) | copy-start | bytes 28
  1.6 12.1 %copy-start.17 = (bf16[128,1152]{1,0:T(8,128)(2,1)S(1)}, bf16[128,1152]{1,0:T(8,128)(2,1)}, u32[]{:S(2)}) copy-start(bf16[128,1152]{1,0:T(8,128)(2,1)} %param.11) | copy-start | bytes 884740
  2.5 27.7 %all-to-all-start = ((bf16[32,16,512]{2,1,0:T(8,128)(2,1)}), bf16[32,16,512]{2,1,0:T(8,128)(2,1)S(1)}, u32[]{:S(2)}, u32[]{:S(2)}) async-start(bf16[32,16,512]{2,1,0:T(8,128)(2,1)} %shard_map.111), calls=%async_computation | async-start | bytes 1048576 | tf_op jit(solution)/shard_map/all_to_all | solution.py:212
  13.7 16.5 %copy-start = (bf16[512,1024]{1,0:T(8,128)(2,1)S(1)}, bf16[512,1024]{1,0:T(8,128)(2,1)}, u32[]{:S(2)}) copy-start(bf16[512,1024]{1,0:T(8,128)(2,1)} %w_first.3) | copy-start | bytes 3145732
  13.7 16.5 %copy-start.3 = (bf16[1024,128]{1,0:T(8,128)(2,1)S(1)}, bf16[1024,128]{1,0:T(8,128)(2,1)}, u32[]{:S(2)}) copy-start(bf16[1024,128]{1,0:T(8,128)(2,1)} %w_second.3) | copy-start | bytes 786436
  13.7 8.6 %collective-permute-start = (bf16[128,1152]{1,0:T(8,128)(2,1)S(1)}, bf16[128,1152]{1,0:T(8,128)(2,1)S(1)}, u32[]{:S(2)}, u32[]{:S(2)}) collective-permute-start(bf16[128,1152]{1,0:T(8,128)(2,1)S(1)} %copy-done.17), channel_id=1, source_target_pairs={{0,32},{32,64},{64,96},{96,128},{128,160},{160,192},{192,224},{224... | collective-permute-start | bytes 884744 | tf_op jit(solution)/shard_map/ppermute | solution.py:26
  18.7 8.3 %collective-permute-start.1 = (bf16[128,1152]{1,0:T(8,128)(2,1)S(1)}, bf16[128,1152]{1,0:T(8,128)(2,1)S(1)}, u32[]{:S(2)}, u32[]{:S(2)}) collective-permute-start(bf16[128,1152]{1,0:T(8,128)(2,1)S(1)} %copy-done.17), channel_id=1, source_target_pairs={{32,0},{64,32},{96,64},{128,96},{160,128},{192,160},{224,192},{256... | collective-permute-start | bytes 884744 | tf_op jit(solution)/shard_map/ppermute | solution.py:31
  22.4 0.7 copy-start.8
  27.1 0.7 copy-start.10
  27.8 1.0 copy-start.9
  28.7 1.0 copy-start.11
  30.2 5.6 %copy-start.16 = (s32[256]{0:T(256)S(1)}, s32[256]{0:T(256)}, u32[]{:S(2)}) copy-start(s32[256]{0:T(256)} %param.15) | copy-start | bytes 3076
  31.6 5.8 %copy-start.1 = (f32[256,1024]{1,0:T(8,128)}, f32[256,1024]{1,0:T(8,128)S(1)}, u32[]{:S(2)}) copy-start(f32[256,1024]{1,0:T(8,128)S(1)} %get-tuple-element.39.slope) | copy-start | bytes 3145732
  31.6 5.8 %copy-start.4 = (bf16[512,256]{1,0:T(8,128)(2,1)}, bf16[512,256]{1,0:T(8,128)(2,1)S(1)}, u32[]{:S(2)}) copy-start(bf16[512,256]{1,0:T(8,128)(2,1)S(1)} %get-tuple-element.40.agg_t) | copy-start | bytes 786436
  31.6 11.6 %copy-start.6 = (bf16[256,1024]{1,0:T(8,128)(2,1)}, bf16[256,1024]{1,0:T(8,128)(2,1)S(1)}, u32[]{:S(2)}) copy-start(bf16[256,1024]{1,0:T(8,128)(2,1)S(1)} %get-tuple-element.38.hidden) | copy-start | bytes 1572868
  31.7 4.7 %collective-permute-start.2 = (bf16[128,128]{1,0:T(8,128)(2,1)S(1)}, bf16[128,128]{1,0:T(8,128)(2,1)S(1)}, u32[]{:S(2)}, u32[]{:S(2)}) collective-permute-start(bf16[128,128]{1,0:T(8,128)(2,1)S(1)} %get-tuple-element.32), channel_id=1, source_target_pairs={{0,1},{1,0},{2,3},{3,2},{4,5},{5,4},{6,7},{7,6},{8,9},{9,8},{10,11... | collective-permute-start | bytes 98312 | tf_op jit(solution)/shard_map/ppermute | solution.py:39
  35.1 1.3 %collective-permute-start.3 = (bf16[128,128]{1,0:T(8,128)(2,1)S(1)}, bf16[128,128]{1,0:T(8,128)(2,1)S(1)}, u32[]{:S(2)}, u32[]{:S(2)}) collective-permute-start(bf16[128,128]{1,0:T(8,128)(2,1)S(1)} %get-tuple-element.33), channel_id=1, source_target_pairs={{1,2},{2,1},{3,4},{4,3},{5,6},{6,5},{7,8},{8,7},{9,10},{10,9},{11,... | collective-permute-start | bytes 98312 | tf_op jit(solution)/shard_map/ppermute | solution.py:39
  37.4 7.2 %collective-permute-start.4 = (bf16[128,128]{1,0:T(8,128)(2,1)S(1)}, bf16[128,128]{1,0:T(8,128)(2,1)S(1)}, u32[]{:S(2)}, u32[]{:S(2)}) collective-permute-start(bf16[128,128]{1,0:T(8,128)(2,1)S(1)} %get-tuple-element.36), channel_id=1, source_target_pairs={{0,1},{1,0},{2,3},{3,2},{4,5},{5,4},{6,7},{7,6},{8,9},{9,8},{10,11... | collective-permute-start | bytes 98312 | tf_op jit(solution)/shard_map/ppermute | solution.py:39
  43.3 1.3 collective-permute-start.5
  44.6 1.2 copy-start.2
  45.8 0.9 copy-start.5
  46.8 1.0 copy-start.7
  48.5 6.7 %collective-permute-start.6 = (bf16[512,640]{1,0:T(8,128)(2,1)S(1)}, bf16[512,640]{1,0:T(8,128)(2,1)S(1)}, u32[]{:S(2)}, u32[]{:S(2)}) collective-permute-start(bf16[512,640]{1,0:T(8,128)(2,1)S(1)} %get-tuple-element.44), channel_id=1, source_target_pairs={{0,32},{32,0},{64,96},{96,64},{128,160},{160,128},{192,224},{224,1... | collective-permute-start | bytes 1966088 | tf_op jit(solution)/shard_map/ppermute | solution.py:21
  101.7 26.1 %all-to-all-start.2 = ((bf16[16,16,640]{2,1,0:T(8,128)(2,1)}), bf16[16,16,640]{2,1,0:T(8,128)(2,1)S(1)}, u32[]{:S(2)}, u32[]{:S(2)}) async-start(bf16[16,16,640]{2,1,0:T(8,128)(2,1)} %broadcast_in_dim.8), calls=%async_computation.2 | async-start | bytes 655360 | tf_op jit(solution)/shard_map/all_to_all | solution.py:278

commit v6 on v5

--- a/solution.py
+++ b/solution.py
@@ -39,18 +39,14 @@
     return lax.ppermute(x, axis, pairs)
 
 
-def here(x):
-    return pltpu.with_memory_space_constraint(x, pltpu.VMEM)
-
-
-def result(shape, dtype, keep=False):
-    return pltpu.VMEM(shape, dtype) if keep else jax.ShapeDtypeStruct(shape, dtype)
+def in_hbm(x):
+    return pltpu.with_memory_space_constraint(x, pltpu.HBM)
 
 
 def whole(kernel, outs, scratch=(), flops=0):
     return pl.pallas_call(
         kernel,
-        out_shape=[result(*out) for out in outs],
+        out_shape=[jax.ShapeDtypeStruct(*out) for out in outs],
         scratch_shapes=list(scratch),
         compiler_params=pltpu.CompilerParams(vmem_limit_bytes=16 * 1024 * 1024),
         cost_estimate=pl.CostEstimate(flops=flops, bytes_accessed=4_000_000, transcendentals=0),
@@ -69,22 +65,18 @@
         wide[d, :, blk + own :] = feats[:, last - blk : last] if d < parts - 1 else none
 
 
-def adjacency_kernel(src, count, tiles, adj):
+def adjacency_kernel(src, count, tiles, adj, adj_stale):
     block_rows, slots, blk, _ = tiles.shape
     for r in range(block_rows):
         live = count[r]
-        for t in range(adj.shape[1] // blk):
+        inside = adj.shape[1] // blk
+        for t in range(inside + adj_stale.shape[1] // blk):
             block = jnp.zeros((blk, blk), BF)
             for k in range(slots):
                 hit = jnp.logical_and(src[r, k] == t, k < live)
                 block = jnp.where(hit, tiles[r, k], block)
-            adj[r * blk : (r + 1) * blk, t * blk : (t + 1) * blk] = block
-
-
-def stale_kernel(adj, before, after, out):
-    rows = before.shape[0]
-    at = adj.shape[1] - 2 * rows
-    out[...] = dot(adj[:, at : at + rows], before[...], 1, 0) + dot(adj[:, at + rows :], after[...], 1, 0)
+            out, at = (adj, t) if t < inside else (adj_stale, t - inside)
+            out[r * blk : (r + 1) * blk, at * blk : (at + 1) * blk] = block
 
 
 def total_kernel(bands, first, second):
@@ -98,23 +90,52 @@
         second[c * rows : (c + 1) * rows, :] = total[:, half:]
 
 
-def forward_kernel(odd, adj, feats, w_first, stale, w_second, agg_t, hidden, slope, proj, within, across):
-    width = feats.shape[1]
+def forward_kernel(
+    odd,
+    adj,
+    adj_stale,
+    feats,
+    w_first,
+    before_far,
+    after_far,
+    w_second_far,
+    agg_t,
+    hidden,
+    slope,
+    proj,
+    within,
+    across,
+    stale_second,
+    before,
+    after,
+    w_second,
+    sems,
+):
+    pairs = [(before_far, before), (after_far, after), (w_second_far, w_second)]
+    fetches = [pltpu.make_async_copy(src, dst, sems.at[i]) for i, (src, dst) in enumerate(pairs)]
+    for fetch in fetches:
+        fetch.start()
     hid = w_first.shape[1]
     step = min(256, hid)
-    m = adj[:, :width]
+    m = adj[...]
     agg = dot(m, feats[...], 1, 1).astype(BF)
     agg_t[...] = dot(feats[...], m, 1, 1).astype(BF)
+    for fetch in fetches:
+        fetch.wait()
+    rows = before.shape[0]
+    m_before, m_after = adj_stale[:, :rows], adj_stale[:, rows:]
     total = jnp.zeros(proj.shape, F32)
     for at in range(0, hid, step):
         cols = slice(at, at + step)
-        a = dot(agg, w_first[:, cols], 1, 0) + stale[:, cols]
+        a = dot(agg, w_first[:, cols], 1, 0)
+        a += dot(m_before, before[:, cols], 1, 0) + dot(m_after, after[:, cols], 1, 0)
         s = jax.nn.sigmoid(a)
         h = (a * s).astype(BF)
         hidden[:, cols] = h
-        slope[:, cols] = s * (1.0 + a * (1.0 - s))
+        slope[:, cols] = (s * (1.0 + a * (1.0 - s))).astype(BF)
         total += dot(h, w_second[cols, :], 1, 0)
     proj[...] = total.astype(BF)
+    stale_second[...] = dot(m_before, before[:, hid:], 1, 0) + dot(m_after, after[:, hid:], 1, 0)
     blk = within.shape[0]
     top, bottom = proj[:blk], proj[proj.shape[0] - blk :]
     is_odd = odd[0] == 1
@@ -123,7 +144,7 @@
 
 
 def middle_kernel(
-    hid, odd, adj, own, paired_in, crossed_in, stale, mark, logits, inner, within, across
+    odd, adj, own, paired_in, crossed_in, stale, mark, logits, inner, within, across
 ):
     blk = within.shape[0]
     is_odd = odd[0] == 1
@@ -134,7 +155,7 @@
     agg = dot(adj[:, :blk], up, 1, 0)
     agg += dot(adj[:, blk : blk + size], own[...], 1, 0)
     agg += dot(adj[:, blk + size : reach], down, 1, 0)
-    agg += stale[:, hid:]
+    agg += stale[...]
     logits[...] = agg.astype(BF)
     e = jnp.exp(agg - jnp.max(agg, axis=1, keepdims=True))
     grad = (e / jnp.sum(e, axis=1, keepdims=True) - mark[...]).astype(BF)
@@ -164,7 +185,7 @@
     grad_p2 = jnp.concatenate(parts, axis=0).astype(BF)
     for at in range(0, hid, step):
         cols = slice(at, at + step)
-        grad_agg[:, cols] = (dot(grad_p2, w_second[cols, :], 1, 1) * slope[:, cols]).astype(BF)
+        grad_agg[:, cols] = (dot(grad_p2, w_second[cols, :], 1, 1) * slope[:, cols].astype(F32)).astype(BF)
     second[...] = (dot(hidden[...], grad_p2, 0, 0) * scale).reshape(second.shape)
     rows = second.shape[0] * second.shape[2]
     send[:, half:] = second[:, other].reshape(rows, second.shape[3]).astype(BF)
@@ -173,21 +194,25 @@
     send[:, :half] = (dot(agg_t[...], g, 1, 0) * scale).astype(BF)
 
 
-def feature_kernel(scale, core, grad_agg, w_first, adj, agg_t, kept, keep, out):
+def feature_kernel(scale, core, grad_agg, adj, agg_t, kept, w_first_far, keep, out, w_first, sem):
+    fetch = pltpu.make_async_copy(w_first_far, w_first, sem)
+    fetch.start()
     width = out.shape[1]
     half = grad_agg.shape[1] // 2
     g = grad_agg[:, pl.ds(pl.multiple_of(core[0] * half, half), half)]
     keep[:, :half] = dot(agg_t[...], g, 1, 0) * scale
     keep[:, half:] = kept[...]
+    fetch.wait()
     back = dot(w_first[...], grad_agg[...], 1, 1).astype(BF)
     out[...] = dot(back, adj[:, :width], 1, 0).astype(BF)
 
 
-def whole_core(kernel, outs, blocks, scratch=(), flops=0, scalars=1):
+def whole_core(kernel, outs, blocks, scratch=(), flops=0, scalars=1, fetched=0):
     return pl.pallas_call(
         kernel,
-        out_shape=[result(*out) for out in outs],
-        in_specs=[pl.BlockSpec(memory_space=pltpu.SMEM)] * scalars + [pl.BlockSpec(memory_space=pltpu.VMEM)] * blocks,
+        out_shape=[jax.ShapeDtypeStruct(*out) for out in outs],
+        in_specs=[pl.BlockSpec(memory_space=pltpu.SMEM)] * scalars + [pl.BlockSpec(memory_space=pltpu.VMEM)] * blocks
+        + [pl.BlockSpec(memory_space=pl.ANY)] * fetched,
         scratch_shapes=scratch,
         compiler_params=pltpu.CompilerParams(vmem_limit_bytes=16 * 1024 * 1024),
         cost_estimate=pl.CostEstimate(flops=flops, bytes_accessed=4_000_000, transcendentals=0),
@@ -211,34 +236,39 @@
     wide, tile_vals, stale_rows = lax.optimization_barrier((wide, tile_vals, stale_rows))
     feats = lax.all_to_all(wide, "dom", split_axis=0, concat_axis=0, tiled=True).reshape(feat_all, reach)
 
-    (adj,) = whole_core(adjacency_kernel, [((own, reach + 2 * blk), BF)], 1, scalars=2)(
+    adj, adj_stale = whole_core(adjacency_kernel, [((own, reach), BF), ((own, 2 * blk), BF)], 1, scalars=2)(
         tile_src, tile_count, tile_vals
     )
-    stale_rows, adj = lax.optimization_barrier((stale_rows, adj))
+    stale_rows, adj, adj_stale = lax.optimization_barrier((stale_rows, adj, adj_stale))
     before = from_previous(stale_rows, "grp")
     after = from_next(stale_rows, "grp")
-    (stale_part,) = whole(
-        stale_kernel, [((own, hid + classes), F32, True)], flops=2 * own * 2 * blk * (hid + classes)
-    )(adj, before, after)
     mark = (labels[:, None] == jnp.arange(classes, dtype=jnp.int32)[None, :]).astype(F32)
 
     odd = (lax.axis_index("dom") % 2)[None]
-    agg_t, hidden, slope, proj_second, within, across = whole_core(
+    agg_t, hidden, slope, proj_second, within, across, stale_second = whole_core(
         forward_kernel,
         [
-            ((feat_all, own), BF, True),
-            ((own, hid), BF, True),
-            ((own, hid), F32, True),
+            ((feat_all, own), BF),
+            ((own, hid), BF),
+            ((own, hid), BF),
             ((own, classes), BF),
             ((blk, classes), BF),
             ((blk, classes), BF),
+            ((own, classes), F32),
         ],
-        5,
+        4,
+        scratch=[
+            pltpu.VMEM(before.shape, BF),
+            pltpu.VMEM(after.shape, BF),
+            pltpu.VMEM(w_second.shape, BF),
+            pltpu.SemaphoreType.DMA((3,)),
+        ],
+        fetched=3,
         flops=2 * own * (2 * feat_all * reach + feat_all * hid + hid * classes),
-    )(odd, adj, feats, w_first, here(stale_part), w_second)
+    )(odd, adj, adj_stale, feats, w_first, in_hbm(before), in_hbm(after), in_hbm(w_second))
 
     logits, inner, within, across = whole_core(
-        functools.partial(middle_kernel, hid),
+        middle_kernel,
         [((own, classes), BF), ((own, classes), F32), ((blk, classes), BF), ((blk, classes), BF)],
         6,
         flops=4 * own * reach * classes,
@@ -248,7 +278,7 @@
         proj_second,
         paired(within, "dom", 0),
         paired(across, "dom", 1),
-        here(stale_part),
+        stale_second,
         mark,
     )
 
@@ -260,15 +290,17 @@
         scratch=[pltpu.VMEM((n_dom, 2, feat_rows, classes), F32)],
         flops=2 * own * (hid * classes * 2 + feat_all * half),
         scalars=2,
-    )(odd, core[None], inner, paired(within, "dom", 0), paired(across, "dom", 1), here(hidden), w_second, here(slope), here(agg_t))
+    )(odd, core[None], inner, paired(within, "dom", 0), paired(across, "dom", 1), hidden, w_second, slope, agg_t)
     received = swapped(send, "grp")
 
     keep, grad_wide = whole_core(
         functools.partial(feature_kernel, scale),
         [((feat_all, width), F32), ((feat_all, reach), BF)],
-        5,
+        4,
+        scratch=[pltpu.VMEM((feat_all, hid), BF), pltpu.SemaphoreType.DMA],
+        fetched=1,
         flops=2 * own * (hid * feat_all + reach * feat_all + feat_all * half),
-    )(core[None], grad_agg, w_first, adj, here(agg_t), kept)
+    )(core[None], grad_agg, adj, agg_t, kept, in_hbm(w_first))
     summed = (keep + received.astype(F32)).astype(BF)
     sent = jnp.concatenate([summed, grad_wide], axis=1)
     got = lax.all_to_all(sent, "dom", split_axis=0, concat_axis=0, tiled=True).reshape(n_dom, feat_rows, -1)

time: 129 us -> 126 us (0.977)
  local copies, waits for them, and re-layouts: 9.09 us -> 2.58 us
  waiting for transfers between devices: 19.6 us -> 22.3 us
  Pallas kernels: 6.83 us -> 9.11 us
    unnamed x36 -> x20, local copies, waits for them, and re-layouts: 7.58 us -> 1.07 us
    all_to_all x1, waiting for transfers between devices: 0.01 us -> 5.1 us  [local(): lax.all_to_all(wide, 'dom', split_axis=0, concat_axis=0, tiled=True)]
    all_to_all x1, starting transfers between devices: 13.1 us -> 11.5 us  [local(): lax.all_to_all(copies, 'grp', split_axis=0, concat_axis=0, tiled=True)]
    ppermute x1, starting transfers between devices: 4.98 us -> 6.3 us  [swapped(): return lax.ppermute(x, axis, [(i, i ^ 1) for i in range(count)])]
    pallas_call x4 -> x3, Pallas kernels: 3.58 us -> 4.74 us  [the longest x1 3.02 us: local(): whole_core(forward_kernel, [((feat_all, own), BF), ((own, hid), BF), ((ow...]
where the time goes in v6:
time: 126 us
  blocking collectives  45.1 us (36%)
  starting transfers between devices  45 us (36%)
  waiting for transfers between devices  22.3 us (18%)
  Pallas kernels  9.11 us (7%)
  local copies, waits for them, and re-layouts  2.58 us (2%)
    all_to_all x1, blocking collectives, local(): lax.all_to_all(sent, 'dom', split_axis=0, concat_axis=0, tiled=True)  45.1 us
    all_to_all x1, waiting for transfers between devices, local(): lax.all_to_all(copies, 'grp', split_axis=0, concat_axis=0, tiled=True)  12.1 us
    all_to_all x1, starting transfers between devices, local(): lax.all_to_all(copies, 'grp', split_axis=0, concat_axis=0, tiled=True)  11.5 us
    all_to_all x1, starting transfers between devices, local(): lax.all_to_all(wide, 'dom', split_axis=0, concat_axis=0, tiled=True)  10.5 us
    ppermute x4, starting transfers between devices, paired(): return lax.ppermute(x, axis, pairs)  9.91 us
    ppermute x1, starting transfers between devices, swapped(): return lax.ppermute(x, axis, [(i, i ^ 1) for i in range(count)])  6.3 us
    all_to_all x1, waiting for transfers between devices, local(): lax.all_to_all(wide, 'dom', split_axis=0, concat_axis=0, tiled=True)  5.1 us
    ppermute x1, starting transfers between devices, from_previous(): return lax.ppermute(x, axis, [(i, i + 1) for i in range(count - 1)])  3.9 us
  transfers between devices with their start and end apart: 9, of which 6 were waited for; matrix products, arithmetic and copies ran while one was open for 1% of the time, Pallas kernels for 2%

profile of v6, /device:TPU:1, one launch (start us, length us, event | category | flops | bytes accessed | tf_op | source)
XLA Modules:
  0.0 125.6 jit_solution(14645162090289435648)
XLA Ops:
  0.6 0.0 copy-start
  0.6 0.0 copy-start.2
  0.7 1.0 copy-done.2
  1.7 0.0 copy-start.3
  1.7 0.0 copy-start.4
  1.7 0.0 copy-start.5
  1.7 0.0 copy-start.9
  1.7 0.9 shard_map.111
  2.6 10.5 %all-to-all-start = ((bf16[32,16,512]{2,1,0:T(8,128)(2,1)}), bf16[32,16,512]{2,1,0:T(8,128)(2,1)S(1)}, u32[]{:S(2)}, u32[]{:S(2)}) async-start(bf16[32,16,512]{2,1,0:T(8,128)(2,1)} %shard_map.111), calls=%async_computation | async-start | bytes 1048576 | tf_op jit(solution)/shard_map/all_to_all | solution.py:237
  13.1 0.0 copy-done.3
  13.1 0.0 copy-done.4
  13.1 0.0 copy-done.5
  13.1 0.7 shard_map.112
  13.8 0.0 copy-done.9
  13.8 2.9 %collective-permute-start.1 = (bf16[128,1152]{1,0:T(8,128)(2,1)S(1)}, bf16[128,1152]{1,0:T(8,128)(2,1)S(1)}, u32[]{:S(2)}, u32[]{:S(2)}) collective-permute-start(bf16[128,1152]{1,0:T(8,128)(2,1)S(1)} %copy-done.9), channel_id=1, source_target_pairs={{32,0},{64,32},{96,64},{128,96},{160,128},{192,160},{224,192},{256... | collective-permute-start | bytes 884744 | tf_op jit(solution)/shard_map/ppermute | solution.py:31
  16.7 3.9 %collective-permute-start = (bf16[128,1152]{1,0:T(8,128)(2,1)S(1)}, bf16[128,1152]{1,0:T(8,128)(2,1)S(1)}, u32[]{:S(2)}, u32[]{:S(2)}) collective-permute-start(bf16[128,1152]{1,0:T(8,128)(2,1)S(1)} %copy-done.9), channel_id=1, source_target_pairs={{0,32},{32,64},{64,96},{96,128},{128,160},{160,192},{192,224},{224... | collective-permute-start | bytes 884744 | tf_op jit(solution)/shard_map/ppermute | solution.py:26
  20.6 2.7 %collective-permute-done.1.after_far = bf16[128,1152]{1,0:T(8,128)(2,1)S(1)} collective-permute-done((bf16[128,1152]{1,0:T(8,128)(2,1)S(1)}, bf16[128,1152]{1,0:T(8,128)(2,1)S(1)}, u32[]{:S(2)}, u32[]{:S(2)}) %collective-permute-start.1) | collective-permute-done | bytes 294944 | tf_op jit(solution)/shard_map/ppermute | solution.py:31
  23.3 0.0 copy-start.6
  23.3 0.9 collective-permute-done.before_far
  24.2 0.0 copy-start.7
  24.2 5.1 %all-to-all-done = bf16[32,16,512]{2,1,0:T(8,128)(2,1)S(1)} async-done(((bf16[32,16,512]{2,1,0:T(8,128)(2,1)}), bf16[32,16,512]{2,1,0:T(8,128)(2,1)S(1)}, u32[]{:S(2)}, u32[]{:S(2)}) %all-to-all-start) | async-done | bytes 524320 | tf_op jit(solution)/shard_map/all_to_all | solution.py:237
  29.3 0.0 copy-done.6
  29.3 0.0 copy-done.7
  29.3 0.0 copy-done
  29.4 0.0 copy-start.8
  29.4 0.0 copy-start.1
  29.4 3.0 %shard_map.113 = (bf16[512,256]{1,0:T(8,128)(2,1)S(1)}, bf16[256,1024]{1,0:T(8,128)(2,1)S(1)}, bf16[256,1024]{1,0:T(8,128)(2,1)S(1)}, bf16[256,128]{1,0:T(8,128)...) custom-call(s32[1]{0:T(128)} %bitcast.odd, ...), custom_call_target="tpu_custom_call" | custom-call | flops 603979776 | bytes 4000000 | tf_op jit(solution)/shard_map/pallas_call | solution.py:248
  32.4 3.0 %collective-permute-start.2 = (bf16[128,128]{1,0:T(8,128)(2,1)S(1)}, bf16[128,128]{1,0:T(8,128)(2,1)S(1)}, u32[]{:S(2)}, u32[]{:S(2)}) collective-permute-start(bf16[128,128]{1,0:T(8,128)(2,1)S(1)} %get-tuple-element.39), channel_id=1, source_target_pairs={{0,1},{1,0},{2,3},{3,2},{4,5},{5,4},{6,7},{7,6},{8,9},{9,8},{10,11... | collective-permute-start | bytes 98312 | tf_op jit(solution)/shard_map/ppermute | solution.py:39
  35.4 0.7 collective-permute-start.3
  36.1 0.0 copy-done.8
  36.1 0.1 fusion.2.mark
  36.2 0.8 collective-permute-done.2.paired_in
  37.1 0.0 collective-permute-done.3.crossed_in
  37.1 1.0 shard_map.114
  38.1 5.6 %collective-permute-start.4 = (bf16[128,128]{1,0:T(8,128)(2,1)S(1)}, bf16[128,128]{1,0:T(8,128)(2,1)S(1)}, u32[]{:S(2)}, u32[]{:S(2)}) collective-permute-start(bf16[128,128]{1,0:T(8,128)(2,1)S(1)} %get-tuple-element.44), channel_id=1, source_target_pairs={{0,1},{1,0},{2,3},{3,2},{4,5},{5,4},{6,7},{7,6},{8,9},{9,8},{10,11... | collective-permute-start | bytes 98312 | tf_op jit(solution)/shard_map/ppermute | solution.py:39
  43.7 0.7 collective-permute-start.5
  44.3 0.6 collective-permute-done.4.paired_in
  45.0 0.0 collective-permute-done.5.crossed_in
  45.0 0.0 copy-done.1
  45.0 0.7 shard_map.115
  45.7 6.3 %collective-permute-start.6 = (bf16[512,640]{1,0:T(8,128)(2,1)S(1)}, bf16[512,640]{1,0:T(8,128)(2,1)S(1)}, u32[]{:S(2)}, u32[]{:S(2)}) collective-permute-start(bf16[512,640]{1,0:T(8,128)(2,1)S(1)} %get-tuple-element.52), channel_id=1, source_target_pairs={{0,32},{32,0},{64,96},{96,64},{128,160},{160,128},{192,224},{224,1... | collective-permute-start | bytes 1966088 | tf_op jit(solution)/shard_map/ppermute | solution.py:21
  52.0 2.1 %shard_map.116 = (f32[512,640]{1,0:T(8,128)S(1)}, bf16[512,512]{1,0:T(8,128)(2,1)S(1)}) custom-call(s32[1]{0:T(128)} %bitcast.2.core, bf16[256,1024]{1,0:T(8,128)(2,1)S(1)} %get-tuple-element.49.grad_agg, bf16[256,512]{1,0:T(8,128)(2,1)S(1)} %get-tuple-element.34.adj, bf16[512,256]{1,0:T(8,128)(2,1)S(1)} %get-tuple-element.48.agg_t, ...), custom_call_target="tpu_custom_call" | custom-call | flops 536870912 | bytes 4000000 | tf_op jit(solution)/shard_map/pallas_call | solution.py:296
  54.1 0.0 collective-permute-done.6
  54.1 0.2 add_convert_fusion
  54.3 0.1 pad_maximum_fusion
  54.4 45.1 %all_to_all.19 = bf16[32,16,1152]{2,1,0:T(8,128)(2,1)S(1)} all-to-all(bf16[32,16,1152]{2,1,0:T(8,128)(2,1)S(1)} %bitcast.9), channel_id=1, replica_groups=mesh['grp'=16,'dom'=32] {'dom'}, dimensions={0} | all-to-all | bytes 2359296 | tf_op jit(solution)/shard_map/all_to_all | solution.py:306
  99.5 0.1 slice_reduce_fusion
  99.6 0.7 broadcast_in_dim.8
  100.4 11.5 %all-to-all-start.2 = ((bf16[16,16,640]{2,1,0:T(8,128)(2,1)}), bf16[16,16,640]{2,1,0:T(8,128)(2,1)S(1)}, u32[]{:S(2)}, u32[]{:S(2)}) async-start(bf16[16,16,640]{2,1,0:T(8,128)(2,1)} %broadcast_in_dim.8), calls=%async_computation.2 | async-start | bytes 655360 | tf_op jit(solution)/shard_map/all_to_all | solution.py:310
  111.9 0.1 slice_convert_fusion
  112.0 0.1 fusion.1
  112.1 0.7 copy.13
  112.9 12.1 %all-to-all-done.2.bands = bf16[16,16,640]{2,1,0:T(8,128)(2,1)S(1)} async-done(((bf16[16,16,640]{2,1,0:T(8,128)(2,1)}), bf16[16,16,640]{2,1,0:T(8,128)(2,1)S(1)}, u32[]{:S(2)}, u32[]{:S(2)}) %all-to-all-start.2) | async-done | bytes 327712 | tf_op jit(solution)/shard_map/all_to_all | solution.py:310
  124.9 0.7 shard_map.117
  (1 shorter events, 0.0 us)
Async XLA Ops:
  0.6 28.7 %copy-start = (bf16[512,1024]{1,0:T(8,128)(2,1)S(1)}, bf16[512,1024]{1,0:T(8,128)(2,1)}, u32[]{:S(2)}) copy-start(bf16[512,1024]{1,0:T(8,128)(2,1)} %w_first_far.1) | copy-start | bytes 3145732
  0.6 1.0 copy-start.2
  1.7 11.4 %copy-start.3 = (bf16[2,4,128,128]{3,2,1,0:T(8,128)(2,1)S(1)}, bf16[2,4,128,128]{3,2,1,0:T(8,128)(2,1)}, u32[]{:S(2)}) copy-start(bf16[2,4,128,128]{3,2,1,0:T(8,128)(2,1)} %tiles) | copy-start | bytes 786436
  1.7 11.4 %copy-start.4 = (s32[2,4]{1,0:T(2,128)S(1)}, s32[2,4]{1,0:T(2,128)}, u32[]{:S(2)}) copy-start(s32[2,4]{1,0:T(2,128)} %src.1) | copy-start | bytes 100
  1.7 11.4 %copy-start.5 = (s32[2]{0:T(128)S(1)}, s32[2]{0:T(128)}, u32[]{:S(2)}) copy-start(s32[2]{0:T(128)} %count.1) | copy-start | bytes 28
  1.7 12.1 %copy-start.9 = (bf16[128,1152]{1,0:T(8,128)(2,1)S(1)}, bf16[128,1152]{1,0:T(8,128)(2,1)}, u32[]{:S(2)}) copy-start(bf16[128,1152]{1,0:T(8,128)(2,1)} %param.11) | copy-start | bytes 884740
  2.6 26.8 %all-to-all-start = ((bf16[32,16,512]{2,1,0:T(8,128)(2,1)}), bf16[32,16,512]{2,1,0:T(8,128)(2,1)S(1)}, u32[]{:S(2)}, u32[]{:S(2)}) async-start(bf16[32,16,512]{2,1,0:T(8,128)(2,1)} %shard_map.111), calls=%async_computation | async-start | bytes 1048576 | tf_op jit(solution)/shard_map/all_to_all | solution.py:237
  13.8 9.5 %collective-permute-start.1 = (bf16[128,1152]{1,0:T(8,128)(2,1)S(1)}, bf16[128,1152]{1,0:T(8,128)(2,1)S(1)}, u32[]{:S(2)}, u32[]{:S(2)}) collective-permute-start(bf16[128,1152]{1,0:T(8,128)(2,1)S(1)} %copy-done.9), channel_id=1, source_target_pairs={{32,0},{64,32},{96,64},{128,96},{160,128},{192,160},{224,192},{256... | collective-permute-start | bytes 884744 | tf_op jit(solution)/shard_map/ppermute | solution.py:31
  16.7 7.6 %collective-permute-start = (bf16[128,1152]{1,0:T(8,128)(2,1)S(1)}, bf16[128,1152]{1,0:T(8,128)(2,1)S(1)}, u32[]{:S(2)}, u32[]{:S(2)}) collective-permute-start(bf16[128,1152]{1,0:T(8,128)(2,1)S(1)} %copy-done.9), channel_id=1, source_target_pairs={{0,32},{32,64},{64,96},{96,128},{128,160},{160,192},{192,224},{224... | collective-permute-start | bytes 884744 | tf_op jit(solution)/shard_map/ppermute | solution.py:26
  23.3 6.0 %copy-start.6 = (bf16[128,1152]{1,0:T(8,128)(2,1)}, bf16[128,1152]{1,0:T(8,128)(2,1)S(1)}, u32[]{:S(2)}) copy-start(bf16[128,1152]{1,0:T(8,128)(2,1)S(1)} %collective-permute-done.1.after_far) | copy-start | bytes 884740
  24.2 5.1 %copy-start.7 = (bf16[128,1152]{1,0:T(8,128)(2,1)}, bf16[128,1152]{1,0:T(8,128)(2,1)S(1)}, u32[]{:S(2)}) copy-start(bf16[128,1152]{1,0:T(8,128)(2,1)S(1)} %collective-permute-done.before_far) | copy-start | bytes 884740
  29.4 6.7 %copy-start.8 = (s32[256]{0:T(256)S(1)}, s32[256]{0:T(256)}, u32[]{:S(2)}) copy-start(s32[256]{0:T(256)} %param.15) | copy-start | bytes 3076
  29.4 15.6 %copy-start.1 = (bf16[1024,128]{1,0:T(8,128)(2,1)S(1)}, bf16[1024,128]{1,0:T(8,128)(2,1)}, u32[]{:S(2)}) copy-start(bf16[1024,128]{1,0:T(8,128)(2,1)} %w_second.1) | copy-start | bytes 786436
  32.4 4.7 %collective-permute-start.2 = (bf16[128,128]{1,0:T(8,128)(2,1)S(1)}, bf16[128,128]{1,0:T(8,128)(2,1)S(1)}, u32[]{:S(2)}, u32[]{:S(2)}) collective-permute-start(bf16[128,128]{1,0:T(8,128)(2,1)S(1)} %get-tuple-element.39), channel_id=1, source_target_pairs={{0,1},{1,0},{2,3},{3,2},{4,5},{5,4},{6,7},{7,6},{8,9},{9,8},{10,11... | collective-permute-start | bytes 98312 | tf_op jit(solution)/shard_map/ppermute | solution.py:39
  35.4 1.6 %collective-permute-start.3 = (bf16[128,128]{1,0:T(8,128)(2,1)S(1)}, bf16[128,128]{1,0:T(8,128)(2,1)S(1)}, u32[]{:S(2)}, u32[]{:S(2)}) collective-permute-start(bf16[128,128]{1,0:T(8,128)(2,1)S(1)} %get-tuple-element.40), channel_id=1, source_target_pairs={{1,2},{2,1},{3,4},{4,3},{5,6},{6,5},{7,8},{8,7},{9,10},{10,9},{11,... | collective-permute-start | bytes 98312 | tf_op jit(solution)/shard_map/ppermute | solution.py:39
  38.1 6.9 %collective-permute-start.4 = (bf16[128,128]{1,0:T(8,128)(2,1)S(1)}, bf16[128,128]{1,0:T(8,128)(2,1)S(1)}, u32[]{:S(2)}, u32[]{:S(2)}) collective-permute-start(bf16[128,128]{1,0:T(8,128)(2,1)S(1)} %get-tuple-element.44), channel_id=1, source_target_pairs={{0,1},{1,0},{2,3},{3,2},{4,5},{5,4},{6,7},{7,6},{8,9},{9,8},{10,11... | collective-permute-start | bytes 98312 | tf_op jit(solution)/shard_map/ppermute | solution.py:39
  43.7 1.3 %collective-permute-start.5 = (bf16[128,128]{1,0:T(8,128)(2,1)S(1)}, bf16[128,128]{1,0:T(8,128)(2,1)S(1)}, u32[]{:S(2)}, u32[]{:S(2)}) collective-permute-start(bf16[128,128]{1,0:T(8,128)(2,1)S(1)} %get-tuple-element.45), channel_id=1, source_target_pairs={{1,2},{2,1},{3,4},{4,3},{5,6},{6,5},{7,8},{8,7},{9,10},{10,9},{11,... | collective-permute-start | bytes 98312 | tf_op jit(solution)/shard_map/ppermute | solution.py:39
  45.7 8.4 %collective-permute-start.6 = (bf16[512,640]{1,0:T(8,128)(2,1)S(1)}, bf16[512,640]{1,0:T(8,128)(2,1)S(1)}, u32[]{:S(2)}, u32[]{:S(2)}) collective-permute-start(bf16[512,640]{1,0:T(8,128)(2,1)S(1)} %get-tuple-element.52), channel_id=1, source_target_pairs={{0,32},{32,0},{64,96},{96,64},{128,160},{160,128},{192,224},{224,1... | collective-permute-start | bytes 1966088 | tf_op jit(solution)/shard_map/ppermute | solution.py:21
  100.4 24.5 %all-to-all-start.2 = ((bf16[16,16,640]{2,1,0:T(8,128)(2,1)}), bf16[16,16,640]{2,1,0:T(8,128)(2,1)S(1)}, u32[]{:S(2)}, u32[]{:S(2)}) async-start(bf16[16,16,640]{2,1,0:T(8,128)(2,1)} %broadcast_in_dim.8), calls=%async_computation.2 | async-start | bytes 655360 | tf_op jit(solution)/shard_map/all_to_all | solution.py:310

commit v7 on v6

--- a/solution.py
+++ b/solution.py
@@ -90,52 +90,46 @@
         second[c * rows : (c + 1) * rows, :] = total[:, half:]
 
 
-def forward_kernel(
-    odd,
-    adj,
-    adj_stale,
-    feats,
-    w_first,
-    before_far,
-    after_far,
-    w_second_far,
-    agg_t,
-    hidden,
-    slope,
-    proj,
-    within,
-    across,
-    stale_second,
-    before,
-    after,
-    w_second,
-    sems,
-):
-    pairs = [(before_far, before), (after_far, after), (w_second_far, w_second)]
-    fetches = [pltpu.make_async_copy(src, dst, sems.at[i]) for i, (src, dst) in enumerate(pairs)]
+def stale_kernel(adj_stale, before, after, first, second, rows, sems):
+    count = before.shape[0]
+    fetches = [
+        pltpu.make_async_copy(before, rows.at[:count], sems.at[0]),
+        pltpu.make_async_copy(after, rows.at[count:], sems.at[1]),
+    ]
     for fetch in fetches:
         fetch.start()
+    for fetch in fetches:
+        fetch.wait()
+    hid = first.shape[1]
+    first[...] = dot(adj_stale[...], rows[:, :hid], 1, 0)
+    second[...] = dot(adj_stale[...], rows[:, hid:], 1, 0)
+
+
+def forward_kernel(
+    odd, adj, feats, stale, w_second, w_first_far, agg_t, hidden, slope, proj, within, across, w_first, sems
+):
     hid = w_first.shape[1]
-    step = min(256, hid)
+    step = hid // sems.shape[0]
+    fetches = []
+    for i in range(sems.shape[0]):
+        cols = slice(i * step, (i + 1) * step)
+        fetches.append(pltpu.make_async_copy(w_first_far.at[:, cols], w_first.at[:, cols], sems.at[i]))
+    for fetch in fetches:
+        fetch.start()
     m = adj[...]
     agg = dot(m, feats[...], 1, 1).astype(BF)
     agg_t[...] = dot(feats[...], m, 1, 1).astype(BF)
-    for fetch in fetches:
-        fetch.wait()
-    rows = before.shape[0]
-    m_before, m_after = adj_stale[:, :rows], adj_stale[:, rows:]
     total = jnp.zeros(proj.shape, F32)
     for at in range(0, hid, step):
         cols = slice(at, at + step)
-        a = dot(agg, w_first[:, cols], 1, 0)
-        a += dot(m_before, before[:, cols], 1, 0) + dot(m_after, after[:, cols], 1, 0)
+        fetches[at // step].wait()
+        a = dot(agg, w_first[:, cols], 1, 0) + stale[:, cols]
         s = jax.nn.sigmoid(a)
         h = (a * s).astype(BF)
         hidden[:, cols] = h
         slope[:, cols] = (s * (1.0 + a * (1.0 - s))).astype(BF)
         total += dot(h, w_second[cols, :], 1, 0)
     proj[...] = total.astype(BF)
-    stale_second[...] = dot(m_before, before[:, hid:], 1, 0) + dot(m_after, after[:, hid:], 1, 0)
     blk = within.shape[0]
     top, bottom = proj[:blk], proj[proj.shape[0] - blk :]
     is_odd = odd[0] == 1
@@ -242,10 +236,19 @@
     stale_rows, adj, adj_stale = lax.optimization_barrier((stale_rows, adj, adj_stale))
     before = from_previous(stale_rows, "grp")
     after = from_next(stale_rows, "grp")
+    stale_first, stale_second = whole_core(
+        stale_kernel,
+        [((own, hid), F32), ((own, classes), F32)],
+        1,
+        scratch=[pltpu.VMEM((2 * blk, hid + classes), BF), pltpu.SemaphoreType.DMA((2,))],
+        flops=2 * own * 2 * blk * (hid + classes),
+        scalars=0,
+        fetched=2,
+    )(adj_stale, in_hbm(before), in_hbm(after))
     mark = (labels[:, None] == jnp.arange(classes, dtype=jnp.int32)[None, :]).astype(F32)
 
-    odd = (lax.axis_index("dom") % 2)[None]
-    agg_t, hidden, slope, proj_second, within, across, stale_second = whole_core(
+    odd = ((lax.axis_index("dom") + 1) % 2)[None]
+    agg_t, hidden, slope, proj_second, within, across = whole_core(
         forward_kernel,
         [
             ((feat_all, own), BF),
@@ -254,18 +257,12 @@
             ((own, classes), BF),
             ((blk, classes), BF),
             ((blk, classes), BF),
-            ((own, classes), F32),
         ],
         4,
-        scratch=[
-            pltpu.VMEM(before.shape, BF),
-            pltpu.VMEM(after.shape, BF),
-            pltpu.VMEM(w_second.shape, BF),
-            pltpu.SemaphoreType.DMA((3,)),
-        ],
-        fetched=3,
+        scratch=[pltpu.VMEM((feat_all, hid), BF), pltpu.SemaphoreType.DMA((4,))],
+        fetched=1,
         flops=2 * own * (2 * feat_all * reach + feat_all * hid + hid * classes),
-    )(odd, adj, adj_stale, feats, w_first, in_hbm(before), in_hbm(after), in_hbm(w_second))
+    )(odd, adj, feats, stale_first, w_second, in_hbm(w_first))
 
     logits, inner, within, across = whole_core(
         middle_kernel,
@@ -276,8 +273,8 @@
         odd,
         adj,
         proj_second,
-        paired(within, "dom", 0),
-        paired(across, "dom", 1),
+        paired(within, "dom", 1),
+        paired(across, "dom", 0),
         stale_second,
         mark,
     )
@@ -290,7 +287,7 @@
         scratch=[pltpu.VMEM((n_dom, 2, feat_rows, classes), F32)],
         flops=2 * own * (hid * classes * 2 + feat_all * half),
         scalars=2,
-    )(odd, core[None], inner, paired(within, "dom", 0), paired(across, "dom", 1), hidden, w_second, slope, agg_t)
+    )(odd, core[None], inner, paired(within, "dom", 1), paired(across, "dom", 0), hidden, w_second, slope, agg_t)
     received = swapped(send, "grp")
 
     keep, grad_wide = whole_core(

time: 126 us -> 125 us (level)
  blocking collectives: 45.1 us -> 40 us
  starting transfers between devices: 45 us -> 47.9 us
    all_to_all x1, blocking collectives: 45.1 us -> 40 us  [local(): lax.all_to_all(sent, 'dom', split_axis=0, concat_axis=0, tiled=True)]
    all_to_all x1, waiting for transfers between devices: 5.1 us -> 2.97 us  [local(): lax.all_to_all(wide, 'dom', split_axis=0, concat_axis=0, tiled=True)]
    ppermute x4, starting transfers between devices: 9.91 us -> 12 us  [paired(): return lax.ppermute(x, axis, pairs)]
    pallas_call x0 -> x1, Pallas kernels: none -> 1.41 us  [local(): whole_core(stale_kernel, [((own, hid), F32), ((own, classes), F32)], 1, s...]
  transfers between devices with their start and end apart: 9 -> 9, of which waited for: 6 -> 6; matrix products, arithmetic and copies ran while one was open for 1% -> 1% of each run, Pallas kernels for 2% -> 3%
where the time goes in v7:
time: 125 us; the launch traced here: 124 us
  starting transfers between devices  47.9 us (38%)
  blocking collectives  40 us (32%)
  waiting for transfers between devices  21.1 us (17%)
  Pallas kernels  10.1 us (8%)
  local copies, waits for them, and re-layouts  3.23 us (3%)
    all_to_all x1, blocking collectives, local(): lax.all_to_all(sent, 'dom', split_axis=0, concat_axis=0, tiled=True)  40 us
    all_to_all x1, starting transfers between devices, local(): lax.all_to_all(copies, 'grp', split_axis=0, concat_axis=0, tiled=True)  12.1 us
    all_to_all x1, waiting for transfers between devices, local(): lax.all_to_all(copies, 'grp', split_axis=0, concat_axis=0, tiled=True)  12.1 us
    ppermute x4, starting transfers between devices, paired(): return lax.ppermute(x, axis, pairs)  12 us
    all_to_all x1, starting transfers between devices, local(): lax.all_to_all(wide, 'dom', split_axis=0, concat_axis=0, tiled=True)  10.5 us
    ppermute x1, starting transfers between devices, swapped(): return lax.ppermute(x, axis, [(i, i ^ 1) for i in range(count)])  6.52 us
    ppermute x1, starting transfers between devices, from_previous(): return lax.ppermute(x, axis, [(i, i + 1) for i in range(count - 1)])  3.9 us
    all_to_all x1, waiting for transfers between devices, local(): lax.all_to_all(wide, 'dom', split_axis=0, concat_axis=0, tiled=True)  2.97 us
  transfers between devices with their start and end apart: 9, of which 6 were waited for; matrix products, arithmetic and copies ran while one was open for 1% of the time, Pallas kernels for 3%

profile of v7, /device:TPU:1, one launch (start us, length us, event | category | flops | bytes accessed | tf_op | source)
XLA Modules:
  0.0 123.9 jit_solution(1587210265738917232)
XLA Ops:
  0.6 0.0 copy-start
  0.6 0.0 copy-start.1
  0.7 1.0 copy-done.1
  1.6 0.0 copy-start.2
  1.6 0.0 copy-start.3
  1.6 0.0 copy-start.4
  1.6 0.0 copy-start.8
  1.6 0.9 shard_map.111
  2.5 10.5 %all-to-all-start = ((bf16[32,16,512]{2,1,0:T(8,128)(2,1)}), bf16[32,16,512]{2,1,0:T(8,128)(2,1)S(1)}, u32[]{:S(2)}, u32[]{:S(2)}) async-start(bf16[32,16,512]{2,1,0:T(8,128)(2,1)} %shard_map.111), calls=%async_computation | async-start | bytes 1048576 | tf_op jit(solution)/shard_map/all_to_all | solution.py:231
  13.0 0.0 copy-done.2
  13.0 0.0 copy-done.3
  13.0 0.0 copy-done.4
  13.0 0.7 shard_map.112
  13.8 0.0 copy-done.8
  13.8 2.9 %collective-permute-start.1 = (bf16[128,1152]{1,0:T(8,128)(2,1)S(1)}, bf16[128,1152]{1,0:T(8,128)(2,1)S(1)}, u32[]{:S(2)}, u32[]{:S(2)}) collective-permute-start(bf16[128,1152]{1,0:T(8,128)(2,1)S(1)} %copy-done.8), channel_id=1, source_target_pairs={{32,0},{64,32},{96,64},{128,96},{160,128},{192,160},{224,192},{256... | collective-permute-start | bytes 884744 | tf_op jit(solution)/shard_map/ppermute | solution.py:31
  16.6 3.9 %collective-permute-start = (bf16[128,1152]{1,0:T(8,128)(2,1)S(1)}, bf16[128,1152]{1,0:T(8,128)(2,1)S(1)}, u32[]{:S(2)}, u32[]{:S(2)}) collective-permute-start(bf16[128,1152]{1,0:T(8,128)(2,1)S(1)} %copy-done.8), channel_id=1, source_target_pairs={{0,32},{32,64},{64,96},{96,128},{128,160},{160,192},{192,224},{224... | collective-permute-start | bytes 884744 | tf_op jit(solution)/shard_map/ppermute | solution.py:26
  20.6 2.7 %collective-permute-done.1.after = bf16[128,1152]{1,0:T(8,128)(2,1)S(1)} collective-permute-done((bf16[128,1152]{1,0:T(8,128)(2,1)S(1)}, bf16[128,1152]{1,0:T(8,128)(2,1)S(1)}, u32[]{:S(2)}, u32[]{:S(2)}) %collective-permute-start.1) | collective-permute-done | bytes 294944 | tf_op jit(solution)/shard_map/ppermute | solution.py:31
  23.3 0.0 copy-start.5
  23.3 0.9 collective-permute-done.before
  24.2 0.0 copy-done.5
  24.2 0.0 copy-start.6
  24.2 0.7 copy-done.6
  24.9 1.4 %shard_map.113 = (f32[256,1024]{1,0:T(8,128)S(1)}, f32[256,128]{1,0:T(8,128)S(1)}) custom-call(bf16[256,256]{1,0:T(8,128)(2,1)S(1)} %get-tuple-element.37.adj_stale, bf16[128,1152]{1,0:T(8,128)(2,1)} %copy-done.6, bf16[128,1152]{1,0:T(8,128)(2,1)} %copy-done.5), custom_call_target="tpu_custom_call" | custom-call | flops 150994944 | bytes 4000000 | tf_op jit(solution)/shard_map/pallas_call | solution.py:239
  26.3 3.0 %all-to-all-done = bf16[32,16,512]{2,1,0:T(8,128)(2,1)S(1)} async-done(((bf16[32,16,512]{2,1,0:T(8,128)(2,1)}), bf16[32,16,512]{2,1,0:T(8,128)(2,1)S(1)}, u32[]{:S(2)}, u32[]{:S(2)}) %all-to-all-start) | async-done | bytes 524320 | tf_op jit(solution)/shard_map/all_to_all | solution.py:231
  29.3 0.0 copy-done
  29.3 0.0 copy-start.7
  29.3 2.6 %shard_map.114 = (bf16[512,256]{1,0:T(8,128)(2,1)S(1)}, bf16[256,1024]{1,0:T(8,128)(2,1)S(1)}, bf16[256,1024]{1,0:T(8,128)(2,1)S(1)}, bf16[256,128]{1,0:T(8,128)...) custom-call(s32[1]{0:T(128)} %bitcast.odd, bf16[256,512]{1,0:T(8,128)(2,1)S(1)} %get-tuple-element.35.adj, ...), custom_call_target="tpu_custom_call" | custom-call | flops 603979776 | bytes 4000000 | tf_op jit(solution)/shard_map/pallas_call | solution.py:251
  31.9 0.7 collective-permute-start.2
  32.6 5.2 %collective-permute-start.3 = (bf16[128,128]{1,0:T(8,128)(2,1)S(1)}, bf16[128,128]{1,0:T(8,128)(2,1)S(1)}, u32[]{:S(2)}, u32[]{:S(2)}) collective-permute-start(bf16[128,128]{1,0:T(8,128)(2,1)S(1)} %get-tuple-element.42), channel_id=1, source_target_pairs={{0,1},{1,0},{2,3},{3,2},{4,5},{5,4},{6,7},{7,6},{8,9},{9,8},{10,11... | collective-permute-start | bytes 98312 | tf_op jit(solution)/shard_map/ppermute | solution.py:39
  37.8 0.0 copy-done.7
  37.8 0.1 fusion.2.mark
  37.9 0.0 collective-permute-done.2.paired_in
  38.0 1.2 collective-permute-done.3.crossed_in
  39.1 1.0 shard_map.115
  40.1 0.7 collective-permute-start.4
  40.8 5.4 %collective-permute-start.5 = (bf16[128,128]{1,0:T(8,128)(2,1)S(1)}, bf16[128,128]{1,0:T(8,128)(2,1)S(1)}, u32[]{:S(2)}, u32[]{:S(2)}) collective-permute-start(bf16[128,128]{1,0:T(8,128)(2,1)S(1)} %get-tuple-element.47), channel_id=1, source_target_pairs={{0,1},{1,0},{2,3},{3,2},{4,5},{5,4},{6,7},{7,6},{8,9},{9,8},{10,11... | collective-permute-start | bytes 98312 | tf_op jit(solution)/shard_map/ppermute | solution.py:39
  46.3 0.0 collective-permute-done.4.paired_in
  46.3 1.3 %collective-permute-done.5.crossed_in = bf16[128,128]{1,0:T(8,128)(2,1)S(1)} collective-permute-done((bf16[128,128]{1,0:T(8,128)(2,1)S(1)}, bf16[128,128]{1,0:T(8,128)(2,1)S(1)}, u32[]{:S(2)}, u32[]{:S(2)}) %collective-permute-start.5) | collective-permute-done | bytes 32800 | tf_op jit(solution)/shard_map/ppermute | solution.py:39
  47.5 0.7 shard_map.116
  48.3 6.5 %collective-permute-start.6 = (bf16[512,640]{1,0:T(8,128)(2,1)S(1)}, bf16[512,640]{1,0:T(8,128)(2,1)S(1)}, u32[]{:S(2)}, u32[]{:S(2)}) collective-permute-start(bf16[512,640]{1,0:T(8,128)(2,1)S(1)} %get-tuple-element.54), channel_id=1, source_target_pairs={{0,32},{32,0},{64,96},{96,64},{128,160},{160,128},{192,224},{224,1... | collective-permute-start | bytes 1966088 | tf_op jit(solution)/shard_map/ppermute | solution.py:21
  54.8 2.1 %shard_map.117 = (f32[512,640]{1,0:T(8,128)S(1)}, bf16[512,512]{1,0:T(8,128)(2,1)S(1)}) custom-call(s32[1]{0:T(128)} %bitcast.2.core, bf16[256,1024]{1,0:T(8,128)(2,1)S(1)} %get-tuple-element.51.grad_agg, bf16[256,512]{1,0:T(8,128)(2,1)S(1)} %get-tuple-element.35.adj, bf16[512,256]{1,0:T(8,128)(2,1)S(1)} %get-tuple-element.50.agg_t, ...), custom_call_target="tpu_custom_call" | custom-call | flops 536870912 | bytes 4000000 | tf_op jit(solution)/shard_map/pallas_call | solution.py:293
  56.9 0.0 collective-permute-done.6
  56.9 0.1 add_convert_fusion
  57.0 0.1 pad_maximum_fusion
  57.2 40.0 %all_to_all.19 = bf16[32,16,1152]{2,1,0:T(8,128)(2,1)S(1)} all-to-all(bf16[32,16,1152]{2,1,0:T(8,128)(2,1)S(1)} %bitcast.9), channel_id=1, replica_groups=mesh['grp'=16,'dom'=32] {'dom'}, dimensions={0} | all-to-all | bytes 2359296 | tf_op jit(solution)/shard_map/all_to_all | solution.py:303
  97.2 0.1 slice_reduce_fusion
  97.3 0.7 broadcast_in_dim.8
  98.0 12.1 %all-to-all-start.2 = ((bf16[16,16,640]{2,1,0:T(8,128)(2,1)}), bf16[16,16,640]{2,1,0:T(8,128)(2,1)S(1)}, u32[]{:S(2)}, u32[]{:S(2)}) async-start(bf16[16,16,640]{2,1,0:T(8,128)(2,1)} %broadcast_in_dim.8), calls=%async_computation.2 | async-start | bytes 655360 | tf_op jit(solution)/shard_map/all_to_all | solution.py:307
  110.2 0.1 slice_convert_fusion
  110.4 0.1 fusion.1
  110.4 0.7 copy.13
  111.2 12.1 %all-to-all-done.2.bands = bf16[16,16,640]{2,1,0:T(8,128)(2,1)S(1)} async-done(((bf16[16,16,640]{2,1,0:T(8,128)(2,1)}), bf16[16,16,640]{2,1,0:T(8,128)(2,1)S(1)}, u32[]{:S(2)}, u32[]{:S(2)}) %all-to-all-start.2) | async-done | bytes 327712 | tf_op jit(solution)/shard_map/all_to_all | solution.py:307
  123.3 0.7 shard_map.118
  (1 shorter events, 0.0 us)
Async XLA Ops:
  0.6 28.7 %copy-start = (bf16[1024,128]{1,0:T(8,128)(2,1)S(1)}, bf16[1024,128]{1,0:T(8,128)(2,1)}, u32[]{:S(2)}) copy-start(bf16[1024,128]{1,0:T(8,128)(2,1)} %w_second.3) | copy-start | bytes 786436
  0.6 1.0 copy-start.1
  1.6 11.4 %copy-start.2 = (bf16[2,4,128,128]{3,2,1,0:T(8,128)(2,1)S(1)}, bf16[2,4,128,128]{3,2,1,0:T(8,128)(2,1)}, u32[]{:S(2)}) copy-start(bf16[2,4,128,128]{3,2,1,0:T(8,128)(2,1)} %tiles) | copy-start | bytes 786436
  1.6 11.4 %copy-start.3 = (s32[2,4]{1,0:T(2,128)S(1)}, s32[2,4]{1,0:T(2,128)}, u32[]{:S(2)}) copy-start(s32[2,4]{1,0:T(2,128)} %src.1) | copy-start | bytes 100
  1.6 11.4 %copy-start.4 = (s32[2]{0:T(128)S(1)}, s32[2]{0:T(128)}, u32[]{:S(2)}) copy-start(s32[2]{0:T(128)} %count.1) | copy-start | bytes 28
  1.6 12.1 %copy-start.8 = (bf16[128,1152]{1,0:T(8,128)(2,1)S(1)}, bf16[128,1152]{1,0:T(8,128)(2,1)}, u32[]{:S(2)}) copy-start(bf16[128,1152]{1,0:T(8,128)(2,1)} %param.11) | copy-start | bytes 884740
  2.5 26.8 %all-to-all-start = ((bf16[32,16,512]{2,1,0:T(8,128)(2,1)}), bf16[32,16,512]{2,1,0:T(8,128)(2,1)S(1)}, u32[]{:S(2)}, u32[]{:S(2)}) async-start(bf16[32,16,512]{2,1,0:T(8,128)(2,1)} %shard_map.111), calls=%async_computation | async-start | bytes 1048576 | tf_op jit(solution)/shard_map/all_to_all | solution.py:231
  13.8 9.5 %collective-permute-start.1 = (bf16[128,1152]{1,0:T(8,128)(2,1)S(1)}, bf16[128,1152]{1,0:T(8,128)(2,1)S(1)}, u32[]{:S(2)}, u32[]{:S(2)}) collective-permute-start(bf16[128,1152]{1,0:T(8,128)(2,1)S(1)} %copy-done.8), channel_id=1, source_target_pairs={{32,0},{64,32},{96,64},{128,96},{160,128},{192,160},{224,192},{256... | collective-permute-start | bytes 884744 | tf_op jit(solution)/shard_map/ppermute | solution.py:31
  16.6 7.6 %collective-permute-start = (bf16[128,1152]{1,0:T(8,128)(2,1)S(1)}, bf16[128,1152]{1,0:T(8,128)(2,1)S(1)}, u32[]{:S(2)}, u32[]{:S(2)}) collective-permute-start(bf16[128,1152]{1,0:T(8,128)(2,1)S(1)} %copy-done.8), channel_id=1, source_target_pairs={{0,32},{32,64},{64,96},{96,128},{128,160},{160,192},{192,224},{224... | collective-permute-start | bytes 884744 | tf_op jit(solution)/shard_map/ppermute | solution.py:26
  23.3 0.9 copy-start.5
  24.2 0.7 copy-start.6
  29.3 8.5 %copy-start.7 = (s32[256]{0:T(256)S(1)}, s32[256]{0:T(256)}, u32[]{:S(2)}) copy-start(s32[256]{0:T(256)} %param.15) | copy-start | bytes 3076
  31.9 6.0 %collective-permute-start.2 = (bf16[128,128]{1,0:T(8,128)(2,1)S(1)}, bf16[128,128]{1,0:T(8,128)(2,1)S(1)}, u32[]{:S(2)}, u32[]{:S(2)}) collective-permute-start(bf16[128,128]{1,0:T(8,128)(2,1)S(1)} %get-tuple-element.41), channel_id=1, source_target_pairs={{1,2},{2,1},{3,4},{4,3},{5,6},{6,5},{7,8},{8,7},{9,10},{10,9},{11,... | collective-permute-start | bytes 98312 | tf_op jit(solution)/shard_map/ppermute | solution.py:39
  32.6 6.5 %collective-permute-start.3 = (bf16[128,128]{1,0:T(8,128)(2,1)S(1)}, bf16[128,128]{1,0:T(8,128)(2,1)S(1)}, u32[]{:S(2)}, u32[]{:S(2)}) collective-permute-start(bf16[128,128]{1,0:T(8,128)(2,1)S(1)} %get-tuple-element.42), channel_id=1, source_target_pairs={{0,1},{1,0},{2,3},{3,2},{4,5},{5,4},{6,7},{7,6},{8,9},{9,8},{10,11... | collective-permute-start | bytes 98312 | tf_op jit(solution)/shard_map/ppermute | solution.py:39
  40.1 6.1 %collective-permute-start.4 = (bf16[128,128]{1,0:T(8,128)(2,1)S(1)}, bf16[128,128]{1,0:T(8,128)(2,1)S(1)}, u32[]{:S(2)}, u32[]{:S(2)}) collective-permute-start(bf16[128,128]{1,0:T(8,128)(2,1)S(1)} %get-tuple-element.46), channel_id=1, source_target_pairs={{1,2},{2,1},{3,4},{4,3},{5,6},{6,5},{7,8},{8,7},{9,10},{10,9},{11,... | collective-permute-start | bytes 98312 | tf_op jit(solution)/shard_map/ppermute | solution.py:39
  40.8 6.7 %collective-permute-start.5 = (bf16[128,128]{1,0:T(8,128)(2,1)S(1)}, bf16[128,128]{1,0:T(8,128)(2,1)S(1)}, u32[]{:S(2)}, u32[]{:S(2)}) collective-permute-start(bf16[128,128]{1,0:T(8,128)(2,1)S(1)} %get-tuple-element.47), channel_id=1, source_target_pairs={{0,1},{1,0},{2,3},{3,2},{4,5},{5,4},{6,7},{7,6},{8,9},{9,8},{10,11... | collective-permute-start | bytes 98312 | tf_op jit(solution)/shard_map/ppermute | solution.py:39
  48.3 8.6 %collective-permute-start.6 = (bf16[512,640]{1,0:T(8,128)(2,1)S(1)}, bf16[512,640]{1,0:T(8,128)(2,1)S(1)}, u32[]{:S(2)}, u32[]{:S(2)}) collective-permute-start(bf16[512,640]{1,0:T(8,128)(2,1)S(1)} %get-tuple-element.54), channel_id=1, source_target_pairs={{0,32},{32,0},{64,96},{96,64},{128,160},{160,128},{192,224},{224,1... | collective-permute-start | bytes 1966088 | tf_op jit(solution)/shard_map/ppermute | solution.py:21
  98.0 25.2 %all-to-all-start.2 = ((bf16[16,16,640]{2,1,0:T(8,128)(2,1)}), bf16[16,16,640]{2,1,0:T(8,128)(2,1)S(1)}, u32[]{:S(2)}, u32[]{:S(2)}) async-start(bf16[16,16,640]{2,1,0:T(8,128)(2,1)} %broadcast_in_dim.8), calls=%async_computation.2 | async-start | bytes 655360 | tf_op jit(solution)/shard_map/all_to_all | solution.py:307

commit v8 on v7

--- a/solution.py
+++ b/solution.py
@@ -101,40 +101,35 @@
     for fetch in fetches:
         fetch.wait()
     hid = first.shape[1]
-    first[...] = dot(adj_stale[...], rows[:, :hid], 1, 0)
+    first[...] = dot(adj_stale[...], rows[:, :hid], 1, 0).astype(BF)
     second[...] = dot(adj_stale[...], rows[:, hid:], 1, 0)
 
 
 def forward_kernel(
-    odd, adj, feats, stale, w_second, w_first_far, agg_t, hidden, slope, proj, within, across, w_first, sems
+    odd, adj, feats, w_first, stale, w_second_far, hidden, slope, proj, within, across, w_second, sem
 ):
+    fetch = pltpu.make_async_copy(w_second_far, w_second, sem)
+    fetch.start()
     hid = w_first.shape[1]
-    step = hid // sems.shape[0]
-    fetches = []
-    for i in range(sems.shape[0]):
-        cols = slice(i * step, (i + 1) * step)
-        fetches.append(pltpu.make_async_copy(w_first_far.at[:, cols], w_first.at[:, cols], sems.at[i]))
-    for fetch in fetches:
-        fetch.start()
-    m = adj[...]
-    agg = dot(m, feats[...], 1, 1).astype(BF)
-    agg_t[...] = dot(feats[...], m, 1, 1).astype(BF)
-    total = jnp.zeros(proj.shape, F32)
+    step = min(256, hid)
+    agg = dot(adj[...], feats[...], 1, 1).astype(BF)
     for at in range(0, hid, step):
         cols = slice(at, at + step)
-        fetches[at // step].wait()
-        a = dot(agg, w_first[:, cols], 1, 0) + stale[:, cols]
+        a = dot(agg, w_first[:, cols], 1, 0) + stale[:, cols].astype(F32)
         s = jax.nn.sigmoid(a)
-        h = (a * s).astype(BF)
-        hidden[:, cols] = h
+        hidden[:, cols] = (a * s).astype(BF)
         slope[:, cols] = (s * (1.0 + a * (1.0 - s))).astype(BF)
-        total += dot(h, w_second[cols, :], 1, 0)
-    proj[...] = total.astype(BF)
+    fetch.wait()
+    proj[...] = dot(hidden[...], w_second[...], 1, 0).astype(BF)
     blk = within.shape[0]
     top, bottom = proj[:blk], proj[proj.shape[0] - blk :]
     is_odd = odd[0] == 1
     within[...] = jnp.where(is_odd, top, bottom)
     across[...] = jnp.where(is_odd, bottom, top)
+
+
+def aggregate_kernel(feats, adj, agg_t):
+    agg_t[...] = dot(feats[...], adj[...], 1, 1).astype(BF)
 
 
 def middle_kernel(
@@ -238,7 +233,7 @@
     after = from_next(stale_rows, "grp")
     stale_first, stale_second = whole_core(
         stale_kernel,
-        [((own, hid), F32), ((own, classes), F32)],
+        [((own, hid), BF), ((own, classes), F32)],
         1,
         scratch=[pltpu.VMEM((2 * blk, hid + classes), BF), pltpu.SemaphoreType.DMA((2,))],
         flops=2 * own * 2 * blk * (hid + classes),
@@ -248,10 +243,9 @@
     mark = (labels[:, None] == jnp.arange(classes, dtype=jnp.int32)[None, :]).astype(F32)
 
     odd = ((lax.axis_index("dom") + 1) % 2)[None]
-    agg_t, hidden, slope, proj_second, within, across = whole_core(
+    hidden, slope, proj_second, within, across = whole_core(
         forward_kernel,
         [
-            ((feat_all, own), BF),
             ((own, hid), BF),
             ((own, hid), BF),
             ((own, classes), BF),
@@ -259,10 +253,12 @@
             ((blk, classes), BF),
         ],
         4,
-        scratch=[pltpu.VMEM((feat_all, hid), BF), pltpu.SemaphoreType.DMA((4,))],
+        scratch=[pltpu.VMEM((hid, classes), BF), pltpu.SemaphoreType.DMA],
         fetched=1,
-        flops=2 * own * (2 * feat_all * reach + feat_all * hid + hid * classes),
-    )(odd, adj, feats, stale_first, w_second, in_hbm(w_first))
+        flops=2 * own * (feat_all * reach + feat_all * hid + hid * classes),
+    )(odd, adj, feats, w_first, stale_first, in_hbm(w_second))
+    feats, adj_beside, within = lax.optimization_barrier((feats, adj, within))
+    (agg_t,) = whole(aggregate_kernel, [((feat_all, own), BF)], flops=2 * own * feat_all * reach)(feats, adj_beside)
 
     logits, inner, within, across = whole_core(
         middle_kernel,

time: 125 us -> 124 us (level)
    pallas_call x2 -> x3, Pallas kernels: 4.05 us -> 3.46 us  [the longest x1 1.72 us: local(): whole_core(forward_kernel, [((own, hid), BF), ((own, hid), BF), ((own, cl...]
  transfers between devices with their start and end apart: 9 -> 9, of which waited for: 6 -> 6; matrix products, arithmetic and copies ran while one was open for 1% -> 1% of each run, Pallas kernels for 3% -> 4%
where the time goes in v8:
time: 124 us; the launch traced here: 123 us
  starting transfers between devices  48 us (39%)
  blocking collectives  40 us (32%)
  waiting for transfers between devices  20.8 us (17%)
  Pallas kernels  9.55 us (8%)
  local copies, waits for them, and re-layouts  3.31 us (3%)
    all_to_all x1, blocking collectives, local(): lax.all_to_all(sent, 'dom', split_axis=0, concat_axis=0, tiled=True)  40 us
    all_to_all x1, starting transfers between devices, local(): lax.all_to_all(copies, 'grp', split_axis=0, concat_axis=0, tiled=True)  12.1 us
    all_to_all x1, waiting for transfers between devices, local(): lax.all_to_all(copies, 'grp', split_axis=0, concat_axis=0, tiled=True)  12.1 us
    ppermute x4, starting transfers between devices, paired(): return lax.ppermute(x, axis, pairs)  12.1 us
    all_to_all x1, starting transfers between devices, local(): lax.all_to_all(wide, 'dom', split_axis=0, concat_axis=0, tiled=True)  10.5 us
    ppermute x1, starting transfers between devices, swapped(): return lax.ppermute(x, axis, [(i, i ^ 1) for i in range(count)])  6.52 us
    ppermute x1, starting transfers between devices, from_previous(): return lax.ppermute(x, axis, [(i, i + 1) for i in range(count - 1)])  3.9 us
    all_to_all x1, waiting for transfers between devices, local(): lax.all_to_all(wide, 'dom', split_axis=0, concat_axis=0, tiled=True)  2.96 us
  transfers between devices with their start and end apart: 9, of which 6 were waited for; matrix products, arithmetic and copies ran while one was open for 1% of the time, Pallas kernels for 4%

profile of v8, /device:TPU:1, one launch (start us, length us, event | category | flops | bytes accessed | tf_op | source)
XLA Modules:
  0.0 123.3 jit_solution(9900596156939557017)
XLA Ops:
  0.6 0.0 copy-start
  0.6 0.0 copy-start.2
  0.7 1.0 copy-done.2
  1.7 0.0 copy-start.3
  1.7 0.0 copy-start.4
  1.7 0.0 copy-start.5
  1.7 0.0 copy-start.9
  1.7 0.9 shard_map.111
  2.6 10.5 %all-to-all-start = ((bf16[32,16,512]{2,1,0:T(8,128)(2,1)}), bf16[32,16,512]{2,1,0:T(8,128)(2,1)S(1)}, u32[]{:S(2)}, u32[]{:S(2)}) async-start(bf16[32,16,512]{2,1,0:T(8,128)(2,1)} %shard_map.111), calls=%async_computation | async-start | bytes 1048576 | tf_op jit(solution)/shard_map/all_to_all | solution.py:226
  13.1 0.0 copy-done.3
  13.1 0.0 copy-done.4
  13.1 0.0 copy-done.5
  13.1 0.7 shard_map.112
  13.8 0.0 copy-done.9
  13.8 2.9 %collective-permute-start.1 = (bf16[128,1152]{1,0:T(8,128)(2,1)S(1)}, bf16[128,1152]{1,0:T(8,128)(2,1)S(1)}, u32[]{:S(2)}, u32[]{:S(2)}) collective-permute-start(bf16[128,1152]{1,0:T(8,128)(2,1)S(1)} %copy-done.9), channel_id=1, source_target_pairs={{32,0},{64,32},{96,64},{128,96},{160,128},{192,160},{224,192},{256... | collective-permute-start | bytes 884744 | tf_op jit(solution)/shard_map/ppermute | solution.py:31
  16.7 3.9 %collective-permute-start = (bf16[128,1152]{1,0:T(8,128)(2,1)S(1)}, bf16[128,1152]{1,0:T(8,128)(2,1)S(1)}, u32[]{:S(2)}, u32[]{:S(2)}) collective-permute-start(bf16[128,1152]{1,0:T(8,128)(2,1)S(1)} %copy-done.9), channel_id=1, source_target_pairs={{0,32},{32,64},{64,96},{96,128},{128,160},{160,192},{192,224},{224... | collective-permute-start | bytes 884744 | tf_op jit(solution)/shard_map/ppermute | solution.py:26
  20.6 2.7 %collective-permute-done.1.after = bf16[128,1152]{1,0:T(8,128)(2,1)S(1)} collective-permute-done((bf16[128,1152]{1,0:T(8,128)(2,1)S(1)}, bf16[128,1152]{1,0:T(8,128)(2,1)S(1)}, u32[]{:S(2)}, u32[]{:S(2)}) %collective-permute-start.1) | collective-permute-done | bytes 294944 | tf_op jit(solution)/shard_map/ppermute | solution.py:31
  23.3 0.0 copy-start.6
  23.3 0.9 collective-permute-done.before
  24.2 0.0 copy-done.6
  24.2 0.0 copy-start.7
  24.2 0.7 copy-done.7
  25.0 1.4 %shard_map.113 = (bf16[256,1024]{1,0:T(8,128)(2,1)S(1)}, f32[256,128]{1,0:T(8,128)S(1)}) custom-call(bf16[256,256]{1,0:T(8,128)(2,1)S(1)} %get-tuple-element.39.adj_stale, bf16[128,1152]{1,0:T(8,128)(2,1)} %copy-done.7, bf16[128,1152]{1,0:T(8,128)(2,1)} %copy-done.6), custom_call_target="tpu_custom_call" | custom-call | flops 150994944 | bytes 4000000 | tf_op jit(solution)/shard_map/pallas_call | solution.py:234
  26.4 3.0 %all-to-all-done = bf16[32,16,512]{2,1,0:T(8,128)(2,1)S(1)} async-done(((bf16[32,16,512]{2,1,0:T(8,128)(2,1)}), bf16[32,16,512]{2,1,0:T(8,128)(2,1)S(1)}, u32[]{:S(2)}, u32[]{:S(2)}) %all-to-all-start) | async-done | bytes 524320 | tf_op jit(solution)/shard_map/all_to_all | solution.py:226
  29.3 0.0 copy-done
  29.3 0.0 copy-start.8
  29.3 1.7 %shard_map.114 = (bf16[256,1024]{1,0:T(8,128)(2,1)S(1)}, bf16[256,1024]{1,0:T(8,128)(2,1)S(1)}, bf16[256,128]{1,0:T(8,128)(2,1)S(1)}, bf16[128,128]{1,0:T(8,128)(2,1)S(1)}, bf16[128,128]{1,0:T(8,128)(2,1)S(1)}) custom-call(s32[1]{0:T(128)} %bitcast.odd, bf16[256,512]{1,0:T(8,128)(2,1)S(1)} %get-tuple-element.54.adj, bf16[512,512]{1,0:T(8,128)(2,1)S(1)} %bitcast.8, ...), custom_call_target="tpu_custom_call" | custom-call | flops 469762048 | bytes 4000000 | tf_op jit(solution)/shard_map/pallas_call | solution.py:246
  31.1 0.0 copy-start.1
  31.1 0.8 collective-permute-start.2
  31.9 5.2 %collective-permute-start.3 = (bf16[128,128]{1,0:T(8,128)(2,1)S(1)}, bf16[128,128]{1,0:T(8,128)(2,1)S(1)}, u32[]{:S(2)}, u32[]{:S(2)}) collective-permute-start(bf16[128,128]{1,0:T(8,128)(2,1)S(1)} %get-tuple-element.45), channel_id=1, source_target_pairs={{0,1},{1,0},{2,3},{3,2},{4,5},{5,4},{6,7},{7,6},{8,9},{9,8},{10,11... | collective-permute-start | bytes 98312 | tf_op jit(solution)/shard_map/ppermute | solution.py:39
  37.1 0.0 copy-done.8
  37.1 0.1 fusion.2.mark
  37.2 0.0 collective-permute-done.2.paired_in
  37.2 1.2 collective-permute-done.3.crossed_in
  38.4 1.0 shard_map.115
  39.4 0.7 collective-permute-start.4
  40.1 5.4 %collective-permute-start.5 = (bf16[128,128]{1,0:T(8,128)(2,1)S(1)}, bf16[128,128]{1,0:T(8,128)(2,1)S(1)}, u32[]{:S(2)}, u32[]{:S(2)}) collective-permute-start(bf16[128,128]{1,0:T(8,128)(2,1)S(1)} %get-tuple-element.50), channel_id=1, source_target_pairs={{0,1},{1,0},{2,3},{3,2},{4,5},{5,4},{6,7},{7,6},{8,9},{9,8},{10,11... | collective-permute-start | bytes 98312 | tf_op jit(solution)/shard_map/ppermute | solution.py:39
  45.5 0.3 shard_map.116.agg_t
  45.9 0.0 collective-permute-done.4.paired_in
  45.9 0.9 collective-permute-done.5.crossed_in
  46.8 0.0 copy-done.1
  46.8 0.7 shard_map.117
  47.6 6.5 %collective-permute-start.6 = (bf16[512,640]{1,0:T(8,128)(2,1)S(1)}, bf16[512,640]{1,0:T(8,128)(2,1)S(1)}, u32[]{:S(2)}, u32[]{:S(2)}) collective-permute-start(bf16[512,640]{1,0:T(8,128)(2,1)S(1)} %get-tuple-element.58), channel_id=1, source_target_pairs={{0,32},{32,0},{64,96},{96,64},{128,160},{160,128},{192,224},{224,1... | collective-permute-start | bytes 1966088 | tf_op jit(solution)/shard_map/ppermute | solution.py:21
  54.1 2.1 %shard_map.118 = (f32[512,640]{1,0:T(8,128)S(1)}, bf16[512,512]{1,0:T(8,128)(2,1)S(1)}) custom-call(s32[1]{0:T(128)} %bitcast.2.core, bf16[256,1024]{1,0:T(8,128)(2,1)S(1)} %get-tuple-element.55.grad_agg, bf16[256,512]{1,0:T(8,128)(2,1)S(1)} %get-tuple-element.54.adj, bf16[512,256]{1,0:T(8,128)(2,1)S(1)} %shard_map.116.agg_t, ...), custom_call_target="tpu_custom_call" | custom-call | flops 536870912 | bytes 4000000 | tf_op jit(solution)/shard_map/pallas_call | solution.py:289
  56.2 0.0 collective-permute-done.6
  56.2 0.2 add_convert_fusion
  56.4 0.1 pad_maximum_fusion
  56.5 40.0 %all_to_all.19 = bf16[32,16,1152]{2,1,0:T(8,128)(2,1)S(1)} all-to-all(bf16[32,16,1152]{2,1,0:T(8,128)(2,1)S(1)} %bitcast.10), channel_id=1, replica_groups=mesh['grp'=16,'dom'=32] {'dom'}, dimensions={0} | all-to-all | bytes 2359296 | tf_op jit(solution)/shard_map/all_to_all | solution.py:299
  96.5 0.1 slice_reduce_fusion
  96.6 0.8 broadcast_in_dim.8
  97.4 12.1 %all-to-all-start.2 = ((bf16[16,16,640]{2,1,0:T(8,128)(2,1)}), bf16[16,16,640]{2,1,0:T(8,128)(2,1)S(1)}, u32[]{:S(2)}, u32[]{:S(2)}) async-start(bf16[16,16,640]{2,1,0:T(8,128)(2,1)} %broadcast_in_dim.8), calls=%async_computation.2 | async-start | bytes 655360 | tf_op jit(solution)/shard_map/all_to_all | solution.py:303
  109.5 0.1 slice_convert_fusion
  109.7 0.1 fusion.1
  109.8 0.7 copy.13
  110.5 12.1 %all-to-all-done.2.bands = bf16[16,16,640]{2,1,0:T(8,128)(2,1)S(1)} async-done(((bf16[16,16,640]{2,1,0:T(8,128)(2,1)}), bf16[16,16,640]{2,1,0:T(8,128)(2,1)S(1)}, u32[]{:S(2)}, u32[]{:S(2)}) %all-to-all-start.2) | async-done | bytes 327712 | tf_op jit(solution)/shard_map/all_to_all | solution.py:303
  122.6 0.7 shard_map.119
  (1 shorter events, 0.0 us)
Async XLA Ops:
  0.6 28.7 %copy-start = (bf16[512,1024]{1,0:T(8,128)(2,1)S(1)}, bf16[512,1024]{1,0:T(8,128)(2,1)}, u32[]{:S(2)}) copy-start(bf16[512,1024]{1,0:T(8,128)(2,1)} %w_first_far.1) | copy-start | bytes 3145732
  0.6 1.0 copy-start.2
  1.7 11.4 %copy-start.3 = (bf16[2,4,128,128]{3,2,1,0:T(8,128)(2,1)S(1)}, bf16[2,4,128,128]{3,2,1,0:T(8,128)(2,1)}, u32[]{:S(2)}) copy-start(bf16[2,4,128,128]{3,2,1,0:T(8,128)(2,1)} %tiles) | copy-start | bytes 786436
  1.7 11.4 %copy-start.4 = (s32[2,4]{1,0:T(2,128)S(1)}, s32[2,4]{1,0:T(2,128)}, u32[]{:S(2)}) copy-start(s32[2,4]{1,0:T(2,128)} %src.1) | copy-start | bytes 100
  1.7 11.4 %copy-start.5 = (s32[2]{0:T(128)S(1)}, s32[2]{0:T(128)}, u32[]{:S(2)}) copy-start(s32[2]{0:T(128)} %count.1) | copy-start | bytes 28
  1.7 12.1 %copy-start.9 = (bf16[128,1152]{1,0:T(8,128)(2,1)S(1)}, bf16[128,1152]{1,0:T(8,128)(2,1)}, u32[]{:S(2)}) copy-start(bf16[128,1152]{1,0:T(8,128)(2,1)} %param.11) | copy-start | bytes 884740
  2.6 26.8 %all-to-all-start = ((bf16[32,16,512]{2,1,0:T(8,128)(2,1)}), bf16[32,16,512]{2,1,0:T(8,128)(2,1)S(1)}, u32[]{:S(2)}, u32[]{:S(2)}) async-start(bf16[32,16,512]{2,1,0:T(8,128)(2,1)} %shard_map.111), calls=%async_computation | async-start | bytes 1048576 | tf_op jit(solution)/shard_map/all_to_all | solution.py:226
  13.8 9.5 %collective-permute-start.1 = (bf16[128,1152]{1,0:T(8,128)(2,1)S(1)}, bf16[128,1152]{1,0:T(8,128)(2,1)S(1)}, u32[]{:S(2)}, u32[]{:S(2)}) collective-permute-start(bf16[128,1152]{1,0:T(8,128)(2,1)S(1)} %copy-done.9), channel_id=1, source_target_pairs={{32,0},{64,32},{96,64},{128,96},{160,128},{192,160},{224,192},{256... | collective-permute-start | bytes 884744 | tf_op jit(solution)/shard_map/ppermute | solution.py:31
  16.7 7.6 %collective-permute-start = (bf16[128,1152]{1,0:T(8,128)(2,1)S(1)}, bf16[128,1152]{1,0:T(8,128)(2,1)S(1)}, u32[]{:S(2)}, u32[]{:S(2)}) collective-permute-start(bf16[128,1152]{1,0:T(8,128)(2,1)S(1)} %copy-done.9), channel_id=1, source_target_pairs={{0,32},{32,64},{64,96},{96,128},{128,160},{160,192},{192,224},{224... | collective-permute-start | bytes 884744 | tf_op jit(solution)/shard_map/ppermute | solution.py:26
  23.3 0.9 copy-start.6
  24.2 0.7 copy-start.7
  29.3 7.8 %copy-start.8 = (s32[256]{0:T(256)S(1)}, s32[256]{0:T(256)}, u32[]{:S(2)}) copy-start(s32[256]{0:T(256)} %param.15) | copy-start | bytes 3076
  31.1 15.7 %copy-start.1 = (bf16[1024,128]{1,0:T(8,128)(2,1)S(1)}, bf16[1024,128]{1,0:T(8,128)(2,1)}, u32[]{:S(2)}) copy-start(bf16[1024,128]{1,0:T(8,128)(2,1)} %w_second.1) | copy-start | bytes 786436
  31.1 6.1 %collective-permute-start.2 = (bf16[128,128]{1,0:T(8,128)(2,1)S(1)}, bf16[128,128]{1,0:T(8,128)(2,1)S(1)}, u32[]{:S(2)}, u32[]{:S(2)}) collective-permute-start(bf16[128,128]{1,0:T(8,128)(2,1)S(1)} %get-tuple-element.44), channel_id=1, source_target_pairs={{1,2},{2,1},{3,4},{4,3},{5,6},{6,5},{7,8},{8,7},{9,10},{10,9},{11,... | collective-permute-start | bytes 98312 | tf_op jit(solution)/shard_map/ppermute | solution.py:39
  31.9 6.5 %collective-permute-start.3 = (bf16[128,128]{1,0:T(8,128)(2,1)S(1)}, bf16[128,128]{1,0:T(8,128)(2,1)S(1)}, u32[]{:S(2)}, u32[]{:S(2)}) collective-permute-start(bf16[128,128]{1,0:T(8,128)(2,1)S(1)} %get-tuple-element.45), channel_id=1, source_target_pairs={{0,1},{1,0},{2,3},{3,2},{4,5},{5,4},{6,7},{7,6},{8,9},{9,8},{10,11... | collective-permute-start | bytes 98312 | tf_op jit(solution)/shard_map/ppermute | solution.py:39
  39.4 6.5 %collective-permute-start.4 = (bf16[128,128]{1,0:T(8,128)(2,1)S(1)}, bf16[128,128]{1,0:T(8,128)(2,1)S(1)}, u32[]{:S(2)}, u32[]{:S(2)}) collective-permute-start(bf16[128,128]{1,0:T(8,128)(2,1)S(1)} %get-tuple-element.49), channel_id=1, source_target_pairs={{1,2},{2,1},{3,4},{4,3},{5,6},{6,5},{7,8},{8,7},{9,10},{10,9},{11,... | collective-permute-start | bytes 98312 | tf_op jit(solution)/shard_map/ppermute | solution.py:39
  40.1 6.7 %collective-permute-start.5 = (bf16[128,128]{1,0:T(8,128)(2,1)S(1)}, bf16[128,128]{1,0:T(8,128)(2,1)S(1)}, u32[]{:S(2)}, u32[]{:S(2)}) collective-permute-start(bf16[128,128]{1,0:T(8,128)(2,1)S(1)} %get-tuple-element.50), channel_id=1, source_target_pairs={{0,1},{1,0},{2,3},{3,2},{4,5},{5,4},{6,7},{7,6},{8,9},{9,8},{10,11... | collective-permute-start | bytes 98312 | tf_op jit(solution)/shard_map/ppermute | solution.py:39
  47.6 8.6 %collective-permute-start.6 = (bf16[512,640]{1,0:T(8,128)(2,1)S(1)}, bf16[512,640]{1,0:T(8,128)(2,1)S(1)}, u32[]{:S(2)}, u32[]{:S(2)}) collective-permute-start(bf16[512,640]{1,0:T(8,128)(2,1)S(1)} %get-tuple-element.58), channel_id=1, source_target_pairs={{0,32},{32,0},{64,96},{96,64},{128,160},{160,128},{192,224},{224,1... | collective-permute-start | bytes 1966088 | tf_op jit(solution)/shard_map/ppermute | solution.py:21
  97.4 25.2 %all-to-all-start.2 = ((bf16[16,16,640]{2,1,0:T(8,128)(2,1)}), bf16[16,16,640]{2,1,0:T(8,128)(2,1)S(1)}, u32[]{:S(2)}, u32[]{:S(2)}) async-start(bf16[16,16,640]{2,1,0:T(8,128)(2,1)} %broadcast_in_dim.8), calls=%async_computation.2 | async-start | bytes 655360 | tf_op jit(solution)/shard_map/all_to_all | solution.py:303

commit v9 on v8

--- a/solution.py
+++ b/solution.py
@@ -90,16 +90,10 @@
         second[c * rows : (c + 1) * rows, :] = total[:, half:]
 
 
-def stale_kernel(adj_stale, before, after, first, second, rows, sems):
+def stale_kernel(adj_stale, before, after, first, second, rows):
     count = before.shape[0]
-    fetches = [
-        pltpu.make_async_copy(before, rows.at[:count], sems.at[0]),
-        pltpu.make_async_copy(after, rows.at[count:], sems.at[1]),
-    ]
-    for fetch in fetches:
-        fetch.start()
-    for fetch in fetches:
-        fetch.wait()
+    rows[:count] = before[...]
+    rows[count:] = after[...]
     hid = first.shape[1]
     first[...] = dot(adj_stale[...], rows[:, :hid], 1, 0).astype(BF)
     second[...] = dot(adj_stale[...], rows[:, hid:], 1, 0)
@@ -228,18 +222,14 @@
     adj, adj_stale = whole_core(adjacency_kernel, [((own, reach), BF), ((own, 2 * blk), BF)], 1, scalars=2)(
         tile_src, tile_count, tile_vals
     )
-    stale_rows, adj, adj_stale = lax.optimization_barrier((stale_rows, adj, adj_stale))
     before = from_previous(stale_rows, "grp")
     after = from_next(stale_rows, "grp")
-    stale_first, stale_second = whole_core(
+    stale_first, stale_second = whole(
         stale_kernel,
         [((own, hid), BF), ((own, classes), F32)],
-        1,
-        scratch=[pltpu.VMEM((2 * blk, hid + classes), BF), pltpu.SemaphoreType.DMA((2,))],
+        scratch=[pltpu.VMEM((2 * blk, hid + classes), BF)],
         flops=2 * own * 2 * blk * (hid + classes),
-        scalars=0,
-        fetched=2,
-    )(adj_stale, in_hbm(before), in_hbm(after))
+    )(adj_stale, before, after)
     mark = (labels[:, None] == jnp.arange(classes, dtype=jnp.int32)[None, :]).astype(F32)
 
     odd = ((lax.axis_index("dom") + 1) % 2)[None]

time: 124 us -> 123 us (level)
  waiting for transfers between devices: 20.8 us -> 22.6 us
    all_to_all x1, waiting for transfers between devices: 2.96 us -> 5.49 us  [local(): lax.all_to_all(wide, 'dom', split_axis=0, concat_axis=0, tiled=True)]
  transfers between devices with their start and end apart: 9 -> 9, of which waited for: 6 -> 6; matrix products, arithmetic and copies ran while one was open for 1% -> 1% of each run, Pallas kernels for 4% -> 3%
where the time goes in v9:
time: 123 us
  starting transfers between devices  47.3 us (38%)
  blocking collectives  40 us (33%)
  waiting for transfers between devices  22.6 us (18%)
  Pallas kernels  8.48 us (7%)
  local copies, waits for them, and re-layouts  2.59 us (2%)
    all_to_all x1, blocking collectives, local(): lax.all_to_all(sent, 'dom', split_axis=0, concat_axis=0, tiled=True)  40 us
    all_to_all x1, waiting for transfers between devices, local(): lax.all_to_all(copies, 'grp', split_axis=0, concat_axis=0, tiled=True)  12.1 us
    ppermute x4, starting transfers between devices, paired(): return lax.ppermute(x, axis, pairs)  12.1 us
    all_to_all x1, starting transfers between devices, local(): lax.all_to_all(copies, 'grp', split_axis=0, concat_axis=0, tiled=True)  11.5 us
    all_to_all x1, starting transfers between devices, local(): lax.all_to_all(wide, 'dom', split_axis=0, concat_axis=0, tiled=True)  10.5 us
    ppermute x1, starting transfers between devices, swapped(): return lax.ppermute(x, axis, [(i, i ^ 1) for i in range(count)])  6.52 us
    all_to_all x1, waiting for transfers between devices, local(): lax.all_to_all(wide, 'dom', split_axis=0, concat_axis=0, tiled=True)  5.49 us
    ppermute x1, starting transfers between devices, from_previous(): return lax.ppermute(x, axis, [(i, i + 1) for i in range(count - 1)])  3.9 us
  transfers between devices with their start and end apart: 9, of which 6 were waited for; matrix products, arithmetic and copies ran while one was open for 1% of the time, Pallas kernels for 3%

profile of v9, /device:TPU:1, one launch (start us, length us, event | category | flops | bytes accessed | tf_op | source)
XLA Modules:
  0.0 122.6 jit_solution(10749575742989272055)
XLA Ops:
  0.6 0.0 copy-start
  0.6 0.0 copy-start.2
  0.7 1.0 copy-done.2
  1.7 0.0 copy-start.7
  1.7 0.0 copy-start.3
  1.7 0.0 copy-start.4
  1.7 0.0 copy-start.5
  1.7 0.9 shard_map.111
  2.6 10.5 %all-to-all-start = ((bf16[32,16,512]{2,1,0:T(8,128)(2,1)}), bf16[32,16,512]{2,1,0:T(8,128)(2,1)S(1)}, u32[]{:S(2)}, u32[]{:S(2)}) async-start(bf16[32,16,512]{2,1,0:T(8,128)(2,1)} %shard_map.111), calls=%async_computation | async-start | bytes 1048576 | tf_op jit(solution)/shard_map/all_to_all | solution.py:220
  13.1 0.0 copy-done.7
  13.1 2.9 %collective-permute-start.1 = (bf16[128,1152]{1,0:T(8,128)(2,1)S(1)}, bf16[128,1152]{1,0:T(8,128)(2,1)S(1)}, u32[]{:S(2)}, u32[]{:S(2)}) collective-permute-start(bf16[128,1152]{1,0:T(8,128)(2,1)S(1)} %copy-done.7), channel_id=1, source_target_pairs={{32,0},{64,32},{96,64},{128,96},{160,128},{192,160},{224,192},{256... | collective-permute-start | bytes 884744 | tf_op jit(solution)/shard_map/ppermute | solution.py:31
  16.0 3.9 %collective-permute-start = (bf16[128,1152]{1,0:T(8,128)(2,1)S(1)}, bf16[128,1152]{1,0:T(8,128)(2,1)S(1)}, u32[]{:S(2)}, u32[]{:S(2)}) collective-permute-start(bf16[128,1152]{1,0:T(8,128)(2,1)S(1)} %copy-done.7), channel_id=1, source_target_pairs={{0,32},{32,64},{64,96},{96,128},{128,160},{160,192},{192,224},{224... | collective-permute-start | bytes 884744 | tf_op jit(solution)/shard_map/ppermute | solution.py:26
  19.9 0.0 copy-done.3
  19.9 0.0 copy-done.4
  19.9 0.0 copy-done.5
  19.9 0.7 shard_map.112
  20.6 2.0 %collective-permute-done.1.after = bf16[128,1152]{1,0:T(8,128)(2,1)S(1)} collective-permute-done((bf16[128,1152]{1,0:T(8,128)(2,1)S(1)}, bf16[128,1152]{1,0:T(8,128)(2,1)S(1)}, u32[]{:S(2)}, u32[]{:S(2)}) %collective-permute-start.1) | collective-permute-done | bytes 294944 | tf_op jit(solution)/shard_map/ppermute | solution.py:31
  22.6 0.9 collective-permute-done.before
  23.5 0.3 shard_map.113
  23.8 5.5 %all-to-all-done = bf16[32,16,512]{2,1,0:T(8,128)(2,1)S(1)} async-done(((bf16[32,16,512]{2,1,0:T(8,128)(2,1)}), bf16[32,16,512]{2,1,0:T(8,128)(2,1)S(1)}, u32[]{:S(2)}, u32[]{:S(2)}) %all-to-all-start) | async-done | bytes 524320 | tf_op jit(solution)/shard_map/all_to_all | solution.py:220
  29.3 0.0 copy-done
  29.3 0.0 copy-start.6
  29.3 1.7 %shard_map.114 = (bf16[256,1024]{1,0:T(8,128)(2,1)S(1)}, bf16[256,1024]{1,0:T(8,128)(2,1)S(1)}, bf16[256,128]{1,0:T(8,128)(2,1)S(1)}, bf16[128,128]{1,0:T(8,128)(2,1)S(1)}, bf16[128,128]{1,0:T(8,128)(2,1)S(1)}) custom-call(s32[1]{0:T(128)} %bitcast.odd, bf16[256,512]{1,0:T(8,128)(2,1)S(1)} %get-tuple-element.48.adj, bf16[512,512]{1,0:T(8,128)(2,1)S(1)} %bitcast.8, ...), custom_call_target="tpu_custom_call" | custom-call | flops 469762048 | bytes 4000000 | tf_op jit(solution)/shard_map/pallas_call | solution.py:236
  31.1 0.0 copy-start.1
  31.1 0.8 collective-permute-start.2
  31.9 5.2 %collective-permute-start.3 = (bf16[128,128]{1,0:T(8,128)(2,1)S(1)}, bf16[128,128]{1,0:T(8,128)(2,1)S(1)}, u32[]{:S(2)}, u32[]{:S(2)}) collective-permute-start(bf16[128,128]{1,0:T(8,128)(2,1)S(1)} %get-tuple-element.39), channel_id=1, source_target_pairs={{0,1},{1,0},{2,3},{3,2},{4,5},{5,4},{6,7},{7,6},{8,9},{9,8},{10,11... | collective-permute-start | bytes 98312 | tf_op jit(solution)/shard_map/ppermute | solution.py:39
  37.1 0.0 copy-done.6
  37.1 0.1 fusion.2.mark
  37.2 0.0 collective-permute-done.2.paired_in
  37.2 1.2 collective-permute-done.3.crossed_in
  38.4 1.0 shard_map.115
  39.4 0.7 collective-permute-start.4
  40.1 5.4 %collective-permute-start.5 = (bf16[128,128]{1,0:T(8,128)(2,1)S(1)}, bf16[128,128]{1,0:T(8,128)(2,1)S(1)}, u32[]{:S(2)}, u32[]{:S(2)}) collective-permute-start(bf16[128,128]{1,0:T(8,128)(2,1)S(1)} %get-tuple-element.44), channel_id=1, source_target_pairs={{0,1},{1,0},{2,3},{3,2},{4,5},{5,4},{6,7},{7,6},{8,9},{9,8},{10,11... | collective-permute-start | bytes 98312 | tf_op jit(solution)/shard_map/ppermute | solution.py:39
  45.5 0.3 shard_map.116.agg_t
  45.9 0.0 collective-permute-done.4.paired_in
  45.9 0.9 collective-permute-done.5.crossed_in
  46.8 0.0 copy-done.1
  46.8 0.7 shard_map.117
  47.6 6.5 %collective-permute-start.6 = (bf16[512,640]{1,0:T(8,128)(2,1)S(1)}, bf16[512,640]{1,0:T(8,128)(2,1)S(1)}, u32[]{:S(2)}, u32[]{:S(2)}) collective-permute-start(bf16[512,640]{1,0:T(8,128)(2,1)S(1)} %get-tuple-element.52), channel_id=1, source_target_pairs={{0,32},{32,0},{64,96},{96,64},{128,160},{160,128},{192,224},{224,1... | collective-permute-start | bytes 1966088 | tf_op jit(solution)/shard_map/ppermute | solution.py:21
  54.1 2.1 %shard_map.118 = (f32[512,640]{1,0:T(8,128)S(1)}, bf16[512,512]{1,0:T(8,128)(2,1)S(1)}) custom-call(s32[1]{0:T(128)} %bitcast.2.core, bf16[256,1024]{1,0:T(8,128)(2,1)S(1)} %get-tuple-element.49.grad_agg, bf16[256,512]{1,0:T(8,128)(2,1)S(1)} %get-tuple-element.48.adj, bf16[512,256]{1,0:T(8,128)(2,1)S(1)} %shard_map.116.agg_t, ...), custom_call_target="tpu_custom_call" | custom-call | flops 536870912 | bytes 4000000 | tf_op jit(solution)/shard_map/pallas_call | solution.py:279
  56.2 0.0 collective-permute-done.6
  56.2 0.2 add_convert_fusion
  56.4 0.1 pad_maximum_fusion
  56.5 40.0 %all_to_all.19 = bf16[32,16,1152]{2,1,0:T(8,128)(2,1)S(1)} all-to-all(bf16[32,16,1152]{2,1,0:T(8,128)(2,1)S(1)} %bitcast.10), channel_id=1, replica_groups=mesh['grp'=16,'dom'=32] {'dom'}, dimensions={0} | all-to-all | bytes 2359296 | tf_op jit(solution)/shard_map/all_to_all | solution.py:289
  96.5 0.1 slice_reduce_fusion
  96.6 0.8 broadcast_in_dim.8
  97.4 11.5 %all-to-all-start.2 = ((bf16[16,16,640]{2,1,0:T(8,128)(2,1)}), bf16[16,16,640]{2,1,0:T(8,128)(2,1)S(1)}, u32[]{:S(2)}, u32[]{:S(2)}) async-start(bf16[16,16,640]{2,1,0:T(8,128)(2,1)} %broadcast_in_dim.8), calls=%async_computation.2 | async-start | bytes 655360 | tf_op jit(solution)/shard_map/all_to_all | solution.py:293
  108.8 0.1 slice_convert_fusion
  109.0 0.1 fusion.1
  109.1 0.7 copy.13
  109.8 12.1 %all-to-all-done.2.bands = bf16[16,16,640]{2,1,0:T(8,128)(2,1)S(1)} async-done(((bf16[16,16,640]{2,1,0:T(8,128)(2,1)}), bf16[16,16,640]{2,1,0:T(8,128)(2,1)S(1)}, u32[]{:S(2)}, u32[]{:S(2)}) %all-to-all-start.2) | async-done | bytes 327712 | tf_op jit(solution)/shard_map/all_to_all | solution.py:293
  121.9 0.7 shard_map.119
  (1 shorter events, 0.0 us)
Async XLA Ops:
  0.6 28.7 %copy-start = (bf16[512,1024]{1,0:T(8,128)(2,1)S(1)}, bf16[512,1024]{1,0:T(8,128)(2,1)}, u32[]{:S(2)}) copy-start(bf16[512,1024]{1,0:T(8,128)(2,1)} %w_first_far.1) | copy-start | bytes 3145732
  0.6 1.0 copy-start.2
  1.7 11.4 %copy-start.7 = (bf16[128,1152]{1,0:T(8,128)(2,1)S(1)}, bf16[128,1152]{1,0:T(8,128)(2,1)}, u32[]{:S(2)}) copy-start(bf16[128,1152]{1,0:T(8,128)(2,1)} %param.11) | copy-start | bytes 884740
  1.7 18.2 %copy-start.3 = (bf16[2,4,128,128]{3,2,1,0:T(8,128)(2,1)S(1)}, bf16[2,4,128,128]{3,2,1,0:T(8,128)(2,1)}, u32[]{:S(2)}) copy-start(bf16[2,4,128,128]{3,2,1,0:T(8,128)(2,1)} %tiles) | copy-start | bytes 786436
  1.7 18.2 %copy-start.4 = (s32[2,4]{1,0:T(2,128)S(1)}, s32[2,4]{1,0:T(2,128)}, u32[]{:S(2)}) copy-start(s32[2,4]{1,0:T(2,128)} %src.1) | copy-start | bytes 100
  1.7 18.2 %copy-start.5 = (s32[2]{0:T(128)S(1)}, s32[2]{0:T(128)}, u32[]{:S(2)}) copy-start(s32[2]{0:T(128)} %count.1) | copy-start | bytes 28
  2.6 26.8 %all-to-all-start = ((bf16[32,16,512]{2,1,0:T(8,128)(2,1)}), bf16[32,16,512]{2,1,0:T(8,128)(2,1)S(1)}, u32[]{:S(2)}, u32[]{:S(2)}) async-start(bf16[32,16,512]{2,1,0:T(8,128)(2,1)} %shard_map.111), calls=%async_computation | async-start | bytes 1048576 | tf_op jit(solution)/shard_map/all_to_all | solution.py:220
  13.1 9.5 %collective-permute-start.1 = (bf16[128,1152]{1,0:T(8,128)(2,1)S(1)}, bf16[128,1152]{1,0:T(8,128)(2,1)S(1)}, u32[]{:S(2)}, u32[]{:S(2)}) collective-permute-start(bf16[128,1152]{1,0:T(8,128)(2,1)S(1)} %copy-done.7), channel_id=1, source_target_pairs={{32,0},{64,32},{96,64},{128,96},{160,128},{192,160},{224,192},{256... | collective-permute-start | bytes 884744 | tf_op jit(solution)/shard_map/ppermute | solution.py:31
  16.0 7.6 %collective-permute-start = (bf16[128,1152]{1,0:T(8,128)(2,1)S(1)}, bf16[128,1152]{1,0:T(8,128)(2,1)S(1)}, u32[]{:S(2)}, u32[]{:S(2)}) collective-permute-start(bf16[128,1152]{1,0:T(8,128)(2,1)S(1)} %copy-done.7), channel_id=1, source_target_pairs={{0,32},{32,64},{64,96},{96,128},{128,160},{160,192},{192,224},{224... | collective-permute-start | bytes 884744 | tf_op jit(solution)/shard_map/ppermute | solution.py:26
  29.3 7.8 %copy-start.6 = (s32[256]{0:T(256)S(1)}, s32[256]{0:T(256)}, u32[]{:S(2)}) copy-start(s32[256]{0:T(256)} %param.15) | copy-start | bytes 3076
  31.1 15.7 %copy-start.1 = (bf16[1024,128]{1,0:T(8,128)(2,1)S(1)}, bf16[1024,128]{1,0:T(8,128)(2,1)}, u32[]{:S(2)}) copy-start(bf16[1024,128]{1,0:T(8,128)(2,1)} %w_second.1) | copy-start | bytes 786436
  31.1 6.1 %collective-permute-start.2 = (bf16[128,128]{1,0:T(8,128)(2,1)S(1)}, bf16[128,128]{1,0:T(8,128)(2,1)S(1)}, u32[]{:S(2)}, u32[]{:S(2)}) collective-permute-start(bf16[128,128]{1,0:T(8,128)(2,1)S(1)} %get-tuple-element.38), channel_id=1, source_target_pairs={{1,2},{2,1},{3,4},{4,3},{5,6},{6,5},{7,8},{8,7},{9,10},{10,9},{11,... | collective-permute-start | bytes 98312 | tf_op jit(solution)/shard_map/ppermute | solution.py:39
  31.9 6.5 %collective-permute-start.3 = (bf16[128,128]{1,0:T(8,128)(2,1)S(1)}, bf16[128,128]{1,0:T(8,128)(2,1)S(1)}, u32[]{:S(2)}, u32[]{:S(2)}) collective-permute-start(bf16[128,128]{1,0:T(8,128)(2,1)S(1)} %get-tuple-element.39), channel_id=1, source_target_pairs={{0,1},{1,0},{2,3},{3,2},{4,5},{5,4},{6,7},{7,6},{8,9},{9,8},{10,11... | collective-permute-start | bytes 98312 | tf_op jit(solution)/shard_map/ppermute | solution.py:39
  39.4 6.4 %collective-permute-start.4 = (bf16[128,128]{1,0:T(8,128)(2,1)S(1)}, bf16[128,128]{1,0:T(8,128)(2,1)S(1)}, u32[]{:S(2)}, u32[]{:S(2)}) collective-permute-start(bf16[128,128]{1,0:T(8,128)(2,1)S(1)} %get-tuple-element.43), channel_id=1, source_target_pairs={{1,2},{2,1},{3,4},{4,3},{5,6},{6,5},{7,8},{8,7},{9,10},{10,9},{11,... | collective-permute-start | bytes 98312 | tf_op jit(solution)/shard_map/ppermute | solution.py:39
  40.1 6.7 %collective-permute-start.5 = (bf16[128,128]{1,0:T(8,128)(2,1)S(1)}, bf16[128,128]{1,0:T(8,128)(2,1)S(1)}, u32[]{:S(2)}, u32[]{:S(2)}) collective-permute-start(bf16[128,128]{1,0:T(8,128)(2,1)S(1)} %get-tuple-element.44), channel_id=1, source_target_pairs={{0,1},{1,0},{2,3},{3,2},{4,5},{5,4},{6,7},{7,6},{8,9},{9,8},{10,11... | collective-permute-start | bytes 98312 | tf_op jit(solution)/shard_map/ppermute | solution.py:39
  47.6 8.6 %collective-permute-start.6 = (bf16[512,640]{1,0:T(8,128)(2,1)S(1)}, bf16[512,640]{1,0:T(8,128)(2,1)S(1)}, u32[]{:S(2)}, u32[]{:S(2)}) collective-permute-start(bf16[512,640]{1,0:T(8,128)(2,1)S(1)} %get-tuple-element.52), channel_id=1, source_target_pairs={{0,32},{32,0},{64,96},{96,64},{128,160},{160,128},{192,224},{224,1... | collective-permute-start | bytes 1966088 | tf_op jit(solution)/shard_map/ppermute | solution.py:21
  97.4 24.5 %all-to-all-start.2 = ((bf16[16,16,640]{2,1,0:T(8,128)(2,1)}), bf16[16,16,640]{2,1,0:T(8,128)(2,1)S(1)}, u32[]{:S(2)}, u32[]{:S(2)}) async-start(bf16[16,16,640]{2,1,0:T(8,128)(2,1)} %broadcast_in_dim.8), calls=%async_computation.2 | async-start | bytes 655360 | tf_op jit(solution)/shard_map/all_to_all | solution.py:293

commit v10 on v9

--- a/solution.py
+++ b/solution.py
@@ -122,12 +122,16 @@
     across[...] = jnp.where(is_odd, bottom, top)
 
 
+def turn_kernel(adj, adj_t):
+    adj_t[...] = adj[...].T
+
+
 def aggregate_kernel(feats, adj, agg_t):
     agg_t[...] = dot(feats[...], adj[...], 1, 1).astype(BF)
 
 
 def middle_kernel(
-    odd, adj, own, paired_in, crossed_in, stale, mark, logits, inner, within, across
+    odd, adj, adj_t, own, paired_in, crossed_in, stale, mark, logits, inner, within, across
 ):
     blk = within.shape[0]
     is_odd = odd[0] == 1
@@ -142,7 +146,7 @@
     logits[...] = agg.astype(BF)
     e = jnp.exp(agg - jnp.max(agg, axis=1, keepdims=True))
     grad = (e / jnp.sum(e, axis=1, keepdims=True) - mark[...]).astype(BF)
-    spread = dot(adj[:, :reach], grad, 0, 0)
+    spread = dot(adj_t[...], grad, 1, 0)
     inner[...] = spread[blk : blk + size]
     rim_up, rim_down = spread[:blk], spread[blk + size :]
     within[...] = jnp.where(is_odd, rim_up, rim_down).astype(BF)
@@ -250,14 +254,16 @@
     feats, adj_beside, within = lax.optimization_barrier((feats, adj, within))
     (agg_t,) = whole(aggregate_kernel, [((feat_all, own), BF)], flops=2 * own * feat_all * reach)(feats, adj_beside)
 
+    (adj_t,) = whole(turn_kernel, [((reach, own), BF)])(adj_beside)
     logits, inner, within, across = whole_core(
         middle_kernel,
         [((own, classes), BF), ((own, classes), F32), ((blk, classes), BF), ((blk, classes), BF)],
-        6,
+        7,
         flops=4 * own * reach * classes,
     )(
         odd,
         adj,
+        adj_t,
         proj_second,
         paired(within, "dom", 1),
         paired(across, "dom", 0),

time: 123 us -> 123 us (level)
  no operation moved by 1% of the time
where the time goes in v10:
time: 123 us; the launch traced here: 122 us
  starting transfers between devices  47.3 us (38%)
  blocking collectives  40 us (33%)
  waiting for transfers between devices  22.5 us (18%)
  Pallas kernels  8.42 us (7%)
  local copies, waits for them, and re-layouts  2.59 us (2%)
    all_to_all x1, blocking collectives, local(): lax.all_to_all(sent, 'dom', split_axis=0, concat_axis=0, tiled=True)  40 us
    all_to_all x1, waiting for transfers between devices, local(): lax.all_to_all(copies, 'grp', split_axis=0, concat_axis=0, tiled=True)  12.1 us
    ppermute x4, starting transfers between devices, paired(): return lax.ppermute(x, axis, pairs)  12.1 us
    all_to_all x1, starting transfers between devices, local(): lax.all_to_all(copies, 'grp', split_axis=0, concat_axis=0, tiled=True)  11.5 us
    all_to_all x1, starting transfers between devices, local(): lax.all_to_all(wide, 'dom', split_axis=0, concat_axis=0, tiled=True)  10.5 us
    ppermute x1, starting transfers between devices, swapped(): return lax.ppermute(x, axis, [(i, i ^ 1) for i in range(count)])  6.53 us
    all_to_all x1, waiting for transfers between devices, local(): lax.all_to_all(wide, 'dom', split_axis=0, concat_axis=0, tiled=True)  5.49 us
    ppermute x1, starting transfers between devices, from_previous(): return lax.ppermute(x, axis, [(i, i + 1) for i in range(count - 1)])  3.9 us
  transfers between devices with their start and end apart: 9, of which 6 were waited for; matrix products, arithmetic and copies ran while one was open for 1% of the time, Pallas kernels for 3%

profile of v10, /device:TPU:1, one launch (start us, length us, event | category | flops | bytes accessed | tf_op | source)
XLA Modules:
  0.0 122.4 jit_solution(18259016103025016786)
XLA Ops:
  0.6 0.0 copy-start
  0.6 0.0 copy-start.2
  0.7 1.0 copy-done.2
  1.7 0.0 copy-start.7
  1.7 0.0 copy-start.3
  1.7 0.0 copy-start.4
  1.7 0.0 copy-start.5
  1.7 0.9 shard_map.111
  2.6 10.5 %all-to-all-start = ((bf16[32,16,512]{2,1,0:T(8,128)(2,1)}), bf16[32,16,512]{2,1,0:T(8,128)(2,1)S(1)}, u32[]{:S(2)}, u32[]{:S(2)}) async-start(bf16[32,16,512]{2,1,0:T(8,128)(2,1)} %shard_map.111), calls=%async_computation | async-start | bytes 1048576 | tf_op jit(solution)/shard_map/all_to_all | solution.py:224
  13.1 0.0 copy-done.7
  13.1 2.9 %collective-permute-start.1 = (bf16[128,1152]{1,0:T(8,128)(2,1)S(1)}, bf16[128,1152]{1,0:T(8,128)(2,1)S(1)}, u32[]{:S(2)}, u32[]{:S(2)}) collective-permute-start(bf16[128,1152]{1,0:T(8,128)(2,1)S(1)} %copy-done.7), channel_id=1, source_target_pairs={{32,0},{64,32},{96,64},{128,96},{160,128},{192,160},{224,192},{256... | collective-permute-start | bytes 884744 | tf_op jit(solution)/shard_map/ppermute | solution.py:31
  16.0 3.9 %collective-permute-start = (bf16[128,1152]{1,0:T(8,128)(2,1)S(1)}, bf16[128,1152]{1,0:T(8,128)(2,1)S(1)}, u32[]{:S(2)}, u32[]{:S(2)}) collective-permute-start(bf16[128,1152]{1,0:T(8,128)(2,1)S(1)} %copy-done.7), channel_id=1, source_target_pairs={{0,32},{32,64},{64,96},{96,128},{128,160},{160,192},{192,224},{224... | collective-permute-start | bytes 884744 | tf_op jit(solution)/shard_map/ppermute | solution.py:26
  19.9 0.0 copy-done.3
  19.9 0.0 copy-done.4
  19.9 0.0 copy-done.5
  19.9 0.7 shard_map.112
  20.6 2.0 %collective-permute-done.1.after = bf16[128,1152]{1,0:T(8,128)(2,1)S(1)} collective-permute-done((bf16[128,1152]{1,0:T(8,128)(2,1)S(1)}, bf16[128,1152]{1,0:T(8,128)(2,1)S(1)}, u32[]{:S(2)}, u32[]{:S(2)}) %collective-permute-start.1) | collective-permute-done | bytes 294944 | tf_op jit(solution)/shard_map/ppermute | solution.py:31
  22.6 0.9 collective-permute-done.before
  23.5 0.3 shard_map.113
  23.8 5.5 %all-to-all-done = bf16[32,16,512]{2,1,0:T(8,128)(2,1)S(1)} async-done(((bf16[32,16,512]{2,1,0:T(8,128)(2,1)}), bf16[32,16,512]{2,1,0:T(8,128)(2,1)S(1)}, u32[]{:S(2)}, u32[]{:S(2)}) %all-to-all-start) | async-done | bytes 524320 | tf_op jit(solution)/shard_map/all_to_all | solution.py:224
  29.3 0.0 copy-done
  29.3 0.0 copy-start.6
  29.3 1.7 %shard_map.114 = (bf16[256,1024]{1,0:T(8,128)(2,1)S(1)}, bf16[256,1024]{1,0:T(8,128)(2,1)S(1)}, bf16[256,128]{1,0:T(8,128)(2,1)S(1)}, bf16[128,128]{1,0:T(8,128)(2,1)S(1)}, bf16[128,128]{1,0:T(8,128)(2,1)S(1)}) custom-call(s32[1]{0:T(128)} %bitcast.odd, bf16[256,512]{1,0:T(8,128)(2,1)S(1)} %get-tuple-element.37.adj, bf16[512,512]{1,0:T(8,128)(2,1)S(1)} %bitcast.8, ...), custom_call_target="tpu_custom_call" | custom-call | flops 469762048 | bytes 4000000 | tf_op jit(solution)/shard_map/pallas_call | solution.py:240
  31.1 0.7 collective-permute-start.2
  31.7 0.0 copy-start.1
  31.8 5.3 %collective-permute-start.3 = (bf16[128,128]{1,0:T(8,128)(2,1)S(1)}, bf16[128,128]{1,0:T(8,128)(2,1)S(1)}, u32[]{:S(2)}, u32[]{:S(2)}) collective-permute-start(bf16[128,128]{1,0:T(8,128)(2,1)S(1)} %get-tuple-element.40), channel_id=1, source_target_pairs={{0,1},{1,0},{2,3},{3,2},{4,5},{5,4},{6,7},{7,6},{8,9},{9,8},{10,11... | collective-permute-start | bytes 98312 | tf_op jit(solution)/shard_map/ppermute | solution.py:39
  37.1 0.0 copy-done.6
  37.1 0.1 fusion.2.mark
  37.2 0.1 shard_map.115.adj_t
  37.3 0.0 collective-permute-done.2.paired_in
  37.4 1.0 collective-permute-done.3.crossed_in
  38.4 0.9 shard_map.116
  39.3 0.7 collective-permute-start.4
  39.9 5.4 %collective-permute-start.5 = (bf16[128,128]{1,0:T(8,128)(2,1)S(1)}, bf16[128,128]{1,0:T(8,128)(2,1)S(1)}, u32[]{:S(2)}, u32[]{:S(2)}) collective-permute-start(bf16[128,128]{1,0:T(8,128)(2,1)S(1)} %get-tuple-element.45), channel_id=1, source_target_pairs={{0,1},{1,0},{2,3},{3,2},{4,5},{5,4},{6,7},{7,6},{8,9},{9,8},{10,11... | collective-permute-start | bytes 98312 | tf_op jit(solution)/shard_map/ppermute | solution.py:39
  45.4 0.3 shard_map.117.agg_t
  45.7 0.0 collective-permute-done.4.paired_in
  45.7 0.9 collective-permute-done.5.crossed_in
  46.6 0.0 copy-done.1
  46.6 0.7 shard_map.118
  47.4 6.5 %collective-permute-start.6 = (bf16[512,640]{1,0:T(8,128)(2,1)S(1)}, bf16[512,640]{1,0:T(8,128)(2,1)S(1)}, u32[]{:S(2)}, u32[]{:S(2)}) collective-permute-start(bf16[512,640]{1,0:T(8,128)(2,1)S(1)} %get-tuple-element.52), channel_id=1, source_target_pairs={{0,32},{32,0},{64,96},{96,64},{128,160},{160,128},{192,224},{224,1... | collective-permute-start | bytes 1966088 | tf_op jit(solution)/shard_map/ppermute | solution.py:21
  53.9 2.1 %shard_map.119 = (f32[512,640]{1,0:T(8,128)S(1)}, bf16[512,512]{1,0:T(8,128)(2,1)S(1)}) custom-call(s32[1]{0:T(128)} %bitcast.2.core, bf16[256,1024]{1,0:T(8,128)(2,1)S(1)} %get-tuple-element.49.grad_agg, bf16[256,512]{1,0:T(8,128)(2,1)S(1)} %get-tuple-element.37.adj, bf16[512,256]{1,0:T(8,128)(2,1)S(1)} %shard_map.117.agg_t, ...), custom_call_target="tpu_custom_call" | custom-call | flops 536870912 | bytes 4000000 | tf_op jit(solution)/shard_map/pallas_call | solution.py:285
  56.0 0.0 collective-permute-done.6
  56.0 0.1 add_convert_fusion
  56.2 0.1 pad_maximum_fusion
  56.3 40.0 %all_to_all.19 = bf16[32,16,1152]{2,1,0:T(8,128)(2,1)S(1)} all-to-all(bf16[32,16,1152]{2,1,0:T(8,128)(2,1)S(1)} %bitcast.10), channel_id=1, replica_groups=mesh['grp'=16,'dom'=32] {'dom'}, dimensions={0} | all-to-all | bytes 2359296 | tf_op jit(solution)/shard_map/all_to_all | solution.py:295
  96.3 0.1 slice_reduce_fusion
  96.4 0.8 broadcast_in_dim.8
  97.2 11.5 %all-to-all-start.2 = ((bf16[16,16,640]{2,1,0:T(8,128)(2,1)}), bf16[16,16,640]{2,1,0:T(8,128)(2,1)S(1)}, u32[]{:S(2)}, u32[]{:S(2)}) async-start(bf16[16,16,640]{2,1,0:T(8,128)(2,1)} %broadcast_in_dim.8), calls=%async_computation.2 | async-start | bytes 655360 | tf_op jit(solution)/shard_map/all_to_all | solution.py:299
  108.6 0.1 slice_convert_fusion
  108.8 0.1 fusion.1
  108.9 0.7 copy.13
  109.6 12.1 %all-to-all-done.2.bands = bf16[16,16,640]{2,1,0:T(8,128)(2,1)S(1)} async-done(((bf16[16,16,640]{2,1,0:T(8,128)(2,1)}), bf16[16,16,640]{2,1,0:T(8,128)(2,1)S(1)}, u32[]{:S(2)}, u32[]{:S(2)}) %all-to-all-start.2) | async-done | bytes 327712 | tf_op jit(solution)/shard_map/all_to_all | solution.py:299
  121.7 0.7 shard_map.120
  (1 shorter events, 0.0 us)
Async XLA Ops:
  0.6 28.7 %copy-start = (bf16[512,1024]{1,0:T(8,128)(2,1)S(1)}, bf16[512,1024]{1,0:T(8,128)(2,1)}, u32[]{:S(2)}) copy-start(bf16[512,1024]{1,0:T(8,128)(2,1)} %w_first_far.1) | copy-start | bytes 3145732
  0.6 1.0 copy-start.2
  1.7 11.4 %copy-start.7 = (bf16[128,1152]{1,0:T(8,128)(2,1)S(1)}, bf16[128,1152]{1,0:T(8,128)(2,1)}, u32[]{:S(2)}) copy-start(bf16[128,1152]{1,0:T(8,128)(2,1)} %param.11) | copy-start | bytes 884740
  1.7 18.2 %copy-start.3 = (bf16[2,4,128,128]{3,2,1,0:T(8,128)(2,1)S(1)}, bf16[2,4,128,128]{3,2,1,0:T(8,128)(2,1)}, u32[]{:S(2)}) copy-start(bf16[2,4,128,128]{3,2,1,0:T(8,128)(2,1)} %tiles) | copy-start | bytes 786436
  1.7 18.2 %copy-start.4 = (s32[2,4]{1,0:T(2,128)S(1)}, s32[2,4]{1,0:T(2,128)}, u32[]{:S(2)}) copy-start(s32[2,4]{1,0:T(2,128)} %src.1) | copy-start | bytes 100
  1.7 18.2 %copy-start.5 = (s32[2]{0:T(128)S(1)}, s32[2]{0:T(128)}, u32[]{:S(2)}) copy-start(s32[2]{0:T(128)} %count.1) | copy-start | bytes 28
  2.6 26.8 %all-to-all-start = ((bf16[32,16,512]{2,1,0:T(8,128)(2,1)}), bf16[32,16,512]{2,1,0:T(8,128)(2,1)S(1)}, u32[]{:S(2)}, u32[]{:S(2)}) async-start(bf16[32,16,512]{2,1,0:T(8,128)(2,1)} %shard_map.111), calls=%async_computation | async-start | bytes 1048576 | tf_op jit(solution)/shard_map/all_to_all | solution.py:224
  13.1 9.5 %collective-permute-start.1 = (bf16[128,1152]{1,0:T(8,128)(2,1)S(1)}, bf16[128,1152]{1,0:T(8,128)(2,1)S(1)}, u32[]{:S(2)}, u32[]{:S(2)}) collective-permute-start(bf16[128,1152]{1,0:T(8,128)(2,1)S(1)} %copy-done.7), channel_id=1, source_target_pairs={{32,0},{64,32},{96,64},{128,96},{160,128},{192,160},{224,192},{256... | collective-permute-start | bytes 884744 | tf_op jit(solution)/shard_map/ppermute | solution.py:31
  16.0 7.6 %collective-permute-start = (bf16[128,1152]{1,0:T(8,128)(2,1)S(1)}, bf16[128,1152]{1,0:T(8,128)(2,1)S(1)}, u32[]{:S(2)}, u32[]{:S(2)}) collective-permute-start(bf16[128,1152]{1,0:T(8,128)(2,1)S(1)} %copy-done.7), channel_id=1, source_target_pairs={{0,32},{32,64},{64,96},{96,128},{128,160},{160,192},{192,224},{224... | collective-permute-start | bytes 884744 | tf_op jit(solution)/shard_map/ppermute | solution.py:26
  29.3 7.8 %copy-start.6 = (s32[256]{0:T(256)S(1)}, s32[256]{0:T(256)}, u32[]{:S(2)}) copy-start(s32[256]{0:T(256)} %param.15) | copy-start | bytes 3076
  31.1 6.3 %collective-permute-start.2 = (bf16[128,128]{1,0:T(8,128)(2,1)S(1)}, bf16[128,128]{1,0:T(8,128)(2,1)S(1)}, u32[]{:S(2)}, u32[]{:S(2)}) collective-permute-start(bf16[128,128]{1,0:T(8,128)(2,1)S(1)} %get-tuple-element.39), channel_id=1, source_target_pairs={{1,2},{2,1},{3,4},{4,3},{5,6},{6,5},{7,8},{8,7},{9,10},{10,9},{11,... | collective-permute-start | bytes 98312 | tf_op jit(solution)/shard_map/ppermute | solution.py:39
  31.7 14.9 %copy-start.1 = (bf16[1024,128]{1,0:T(8,128)(2,1)S(1)}, bf16[1024,128]{1,0:T(8,128)(2,1)}, u32[]{:S(2)}) copy-start(bf16[1024,128]{1,0:T(8,128)(2,1)} %w_second.1) | copy-start | bytes 786436
  31.8 6.6 %collective-permute-start.3 = (bf16[128,128]{1,0:T(8,128)(2,1)S(1)}, bf16[128,128]{1,0:T(8,128)(2,1)S(1)}, u32[]{:S(2)}, u32[]{:S(2)}) collective-permute-start(bf16[128,128]{1,0:T(8,128)(2,1)S(1)} %get-tuple-element.40), channel_id=1, source_target_pairs={{0,1},{1,0},{2,3},{3,2},{4,5},{5,4},{6,7},{7,6},{8,9},{9,8},{10,11... | collective-permute-start | bytes 98312 | tf_op jit(solution)/shard_map/ppermute | solution.py:39
  39.3 6.4 %collective-permute-start.4 = (bf16[128,128]{1,0:T(8,128)(2,1)S(1)}, bf16[128,128]{1,0:T(8,128)(2,1)S(1)}, u32[]{:S(2)}, u32[]{:S(2)}) collective-permute-start(bf16[128,128]{1,0:T(8,128)(2,1)S(1)} %get-tuple-element.44), channel_id=1, source_target_pairs={{1,2},{2,1},{3,4},{4,3},{5,6},{6,5},{7,8},{8,7},{9,10},{10,9},{11,... | collective-permute-start | bytes 98312 | tf_op jit(solution)/shard_map/ppermute | solution.py:39
  39.9 6.7 %collective-permute-start.5 = (bf16[128,128]{1,0:T(8,128)(2,1)S(1)}, bf16[128,128]{1,0:T(8,128)(2,1)S(1)}, u32[]{:S(2)}, u32[]{:S(2)}) collective-permute-start(bf16[128,128]{1,0:T(8,128)(2,1)S(1)} %get-tuple-element.45), channel_id=1, source_target_pairs={{0,1},{1,0},{2,3},{3,2},{4,5},{5,4},{6,7},{7,6},{8,9},{9,8},{10,11... | collective-permute-start | bytes 98312 | tf_op jit(solution)/shard_map/ppermute | solution.py:39
  47.4 8.6 %collective-permute-start.6 = (bf16[512,640]{1,0:T(8,128)(2,1)S(1)}, bf16[512,640]{1,0:T(8,128)(2,1)S(1)}, u32[]{:S(2)}, u32[]{:S(2)}) collective-permute-start(bf16[512,640]{1,0:T(8,128)(2,1)S(1)} %get-tuple-element.52), channel_id=1, source_target_pairs={{0,32},{32,0},{64,96},{96,64},{128,160},{160,128},{192,224},{224,1... | collective-permute-start | bytes 1966088 | tf_op jit(solution)/shard_map/ppermute | solution.py:21
  97.2 24.5 %all-to-all-start.2 = ((bf16[16,16,640]{2,1,0:T(8,128)(2,1)}), bf16[16,16,640]{2,1,0:T(8,128)(2,1)S(1)}, u32[]{:S(2)}, u32[]{:S(2)}) async-start(bf16[16,16,640]{2,1,0:T(8,128)(2,1)} %broadcast_in_dim.8), calls=%async_computation.2 | async-start | bytes 655360 | tf_op jit(solution)/shard_map/all_to_all | solution.py:299
